TPU v7x, 512 devices: a whole 4x4x16 slice. The times are simulated.
512 devices in a mesh: lat: 4 (over x_lo, core), lon: 128 (over z, x_hi, y).
Axes of the slice: x: 4 (x_hi: 2, x_lo: 2; x = x_hi * 2 + x_lo), y: 4, z: 16, core: 2. Of those that a mesh axis runs over, the one named last changes fastest.
Arguments:
- coarse: bfloat16 [16, 4096, 256], P('lat', 'lon'), may hold values from -6 to 6
- w_first: bfloat16 [9, 256, 128], P(None, 'lon'), may hold values from -0.125 to 0.125
- w_second: bfloat16 [9, 128, 128], P(None, 'lon'), may hold values from -0.1875 to 0.1875
- w_skip: bfloat16 [256, 128], P('lon'), may hold values from -0.375 to 0.375
- cotangent: bfloat16 [32, 8192, 128], P('lat', 'lon'), may hold values from -6 to 6
Outputs:
- result: bfloat16 [32, 8192, 128], P('lat', 'lon')
- coarse_gradient: bfloat16 [16, 4096, 256], P('lat', 'lon')
- grad_first: float32 [9, 256, 128], P(None, 'lon')
- grad_second: float32 [9, 128, 128], P(None, 'lon')
- grad_skip: float32 [256, 128], P('lon')
All inputs are finite; a program needn't handle non-finite values.
Results may differ from a plain program's by a relative error of at most 0.014.
Values may be sent and summed in bfloat16 or wider, within the bound.
No kernel may reach another device: no remote copies, remote signals or barrier semaphores. Data moves between devices by JAX's collectives and lax.ppermute only.
A program may use at most 64 MiB of HBM per device.

v0:
```python
import math

import jax
import jax.numpy as jnp
from jax import lax
from jax.sharding import PartitionSpec as P


def extended(block, sides, width, periodic):
    for axis, dim in sides:
        count = lax.axis_size(axis)
        forward = [(i, i + 1) for i in range(count - 1)]
        if periodic:
            forward.append((count - 1, 0))
        backward = [(target, source) for source, target in forward]
        low = lax.ppermute(
            lax.slice_in_dim(block, block.shape[dim] - width, None, axis=dim), axis, forward
        )
        high = lax.ppermute(lax.slice_in_dim(block, 0, width, axis=dim), axis, backward)
        block = jnp.concatenate([low, block, high], axis=dim)
    return block


def displace(input_field, offset, along_axis):
    length = input_field.shape[along_axis]
    widths = [(0, 0)] * input_field.ndim
    widths[along_axis] = (max(-offset, 0), max(offset, 0))
    padded = jnp.pad(input_field, widths)
    return lax.slice_in_dim(padded, max(offset, 0), max(offset, 0) + length, 1, along_axis)


def upsample_axis(input_field, along_axis):
    before = displace(input_field, -1, along_axis)
    following = displace(input_field, 1, along_axis)
    even_part = 0.75 * input_field + 0.25 * before
    odd_part = 0.75 * input_field + 0.25 * following
    stacked = jnp.stack([even_part, odd_part], along_axis + 1)
    new_shape = list(input_field.shape)
    new_shape[along_axis] = new_shape[along_axis] * 2
    return stacked.reshape(new_shape)


def decimate_with_border(input_field, along_axis):
    length = (input_field.shape[along_axis] - 2) // 2
    inner = lax.slice_in_dim(input_field, 1, 1 + 2 * length, 1, along_axis)
    split = inner.reshape(
        input_field.shape[:along_axis] + (length, 2) + input_field.shape[along_axis + 1 :]
    )
    even_part = lax.index_in_dim(split, 0, along_axis + 1, keepdims=False)
    odd_part = lax.index_in_dim(split, 1, along_axis + 1, keepdims=False)
    odd_before = lax.slice_in_dim(input_field, 0, 2 * length, 2, along_axis)
    even_after = lax.slice_in_dim(input_field, 3, 2 * length + 2, 2, along_axis)
    return 0.75 * (even_part + odd_part) + 0.25 * (odd_before + even_after)


def bordered(input_field, width):
    lat_ext = extended(input_field, (("lat", 0),), width, False)
    return extended(lat_ext, (("lon", 1),), width, True)


def conv_valid(padded, kernels):
    row_count = padded.shape[0] - 2
    col_count = padded.shape[1] - 2
    summed = None
    for i in range(3):
        for j in range(3):
            window = padded[i : i + row_count, j : j + col_count].reshape(row_count * col_count, -1)
            partial_value = jnp.dot(window, kernels[3 * i + j], preferred_element_type=jnp.float32)
            summed = partial_value if summed is None else summed + partial_value
    return summed.reshape(row_count, col_count, -1)


def tap_grads(padded, cot):
    row_count, col_count = (cot.shape[0], cot.shape[1])
    flat_cot = cot.reshape(row_count * col_count, -1)
    pieces = []
    for i in range(3):
        for j in range(3):
            window = padded[i : i + row_count, j : j + col_count].reshape(row_count * col_count, -1)
            pieces.append(
                lax.dot_general(
                    window, flat_cot, (((0,), (0,)), ((), ())), preferred_element_type=jnp.float32
                )
            )
    return jnp.stack(pieces, 0)


def flipped(kernels):
    return jnp.swapaxes(kernels[::-1], 1, 2)


def row_keep(count, margin, row_dev):
    positions = lax.axis_index("lat") * row_dev - margin + jnp.arange(count, dtype=jnp.int32)
    inside = (positions >= 0) & (positions < row_dev * lax.axis_size("lat"))
    return inside.astype(jnp.float32)[:, None, None]


def fine_from(coarse_ext, reach, margin, row_dev):
    wide = upsample_axis(coarse_ext.astype(jnp.float32), 0)
    wide = upsample_axis(wide, 1)
    begin = 2 * reach - margin
    row_total = wide.shape[0] - 2 * begin
    col_total = wide.shape[1] - 2 * begin
    sliced = wide[begin : begin + row_total, begin : begin + col_total]
    return (sliced * row_keep(row_total, margin, row_dev)).astype(jnp.bfloat16)


def on_device(coarse, w_first, w_second, w_skip, cotangent):
    first_full, second_full, skip_full = (
        lax.all_gather(w_first, "lon", axis=1, tiled=True),
        lax.all_gather(w_second, "lon", axis=1, tiled=True),
        lax.all_gather(w_skip, "lon", axis=0, tiled=True),
    )
    row_dev = 2 * coarse.shape[0]
    col_dev = 2 * coarse.shape[1]
    scale = 1.0 / math.sqrt(row_dev * lax.axis_size("lat") * col_dev * lax.axis_size("lon"))
    coarse_ext = bordered(coarse, 1)
    fine_ext = fine_from(coarse_ext, 1, 1, row_dev)
    act = conv_valid(fine_ext, first_full)
    hidden_ext = bordered(jax.nn.silu(act).astype(jnp.bfloat16), 1)
    fine_in = fine_ext[1:-1, 1:-1]
    flat_in = fine_in.reshape(row_dev * col_dev, -1)
    flat_cot = cotangent.reshape(row_dev * col_dev, -1)
    skip_term = jnp.dot(flat_in, skip_full, preferred_element_type=jnp.float32).reshape(
        row_dev, col_dev, -1
    )
    result = (conv_valid(hidden_ext, second_full) + skip_term).astype(jnp.bfloat16)
    cot_ext = bordered(cotangent, 1)
    grad_hidden = conv_valid(cot_ext, flipped(second_full))
    sigma = jax.nn.sigmoid(act)
    grad_act = (grad_hidden * sigma * (1.0 + act * (1.0 - sigma))).astype(jnp.bfloat16)
    grad_act_ext = bordered(grad_act, 1)
    back_skip = jnp.dot(flat_cot, skip_full.T, preferred_element_type=jnp.float32).reshape(
        row_dev, col_dev, -1
    )
    fine_gradient = (conv_valid(grad_act_ext, flipped(first_full)) + back_skip).astype(jnp.bfloat16)
    fine_gradient_padded = bordered(fine_gradient, 1)
    reduced_field = decimate_with_border(fine_gradient_padded.astype(jnp.float32), 1)
    coarse_gradient = decimate_with_border(reduced_field, 0).astype(jnp.bfloat16)
    local_first = tap_grads(fine_ext, grad_act) * scale
    local_second = tap_grads(hidden_ext, cotangent) * scale
    local_skip = (
        lax.dot_general(
            flat_in, flat_cot, (((0,), (0,)), ((), ())), preferred_element_type=jnp.float32
        )
        * scale
    )
    replicas = (
        lax.psum(local_first.astype(jnp.bfloat16), "lat").astype(jnp.float32),
        lax.psum(local_second.astype(jnp.bfloat16), "lat").astype(jnp.float32),
        lax.psum(local_skip.astype(jnp.bfloat16), "lat").astype(jnp.float32),
    )
    grad_first, grad_second, grad_skip = (
        lax.psum_scatter(replicas[0], "lon", scatter_dimension=1, tiled=True),
        lax.psum_scatter(replicas[1], "lon", scatter_dimension=1, tiled=True),
        lax.psum_scatter(replicas[2], "lon", scatter_dimension=0, tiled=True),
    )
    return (result, coarse_gradient, grad_first, grad_second, grad_skip)


def solution(mesh):
    placed = (
        P("lat", "lon", None),
        P(None, "lon", None),
        P(None, "lon", None),
        P("lon", None),
        P("lat", "lon", None),
    )
    return jax.shard_map(
        on_device,
        mesh=mesh,
        in_specs=placed,
        out_specs=(
            P("lat", "lon", None),
            P("lat", "lon", None),
            P(None, "lon", None),
            P(None, "lon", None),
            P("lon", None),
        ),
        check_vma=False,
    )
```

profile of v0, /device:TPU:2, one launch (start us, length us, event | category | flops | bytes accessed | tf_op | source)
XLA Modules:
  0.0 1955.0 jit_solution(2377457684650827696)
XLA Ops:
  8.0 1.9 collective-permute-start
  9.9 3.6 collective-permute-start.1
  14.3 1.9 collective-permute-start.8
  16.2 5.6 collective-permute-start.9
  21.8 361.7 %all_gather.10 = bf16[9,128,128]{2,0,1:T(8,128)(2,1)S(1)} all-gather(bf16[9,1,128]{2,0,1:T(8,128)(2,1)} %param.7), channel_id=1, replica_groups=mesh['lat'=4,'lon'=128] {'lon'}, dimensions={1}, use_global_device_ids=true | all-gather | bytes 297216 | tf_op jit(solution)/shard_map/all_gather | solution.py:111
  383.8 1.2 fusion.84
  385.0 352.7 %all_gather.9 = bf16[9,256,128]{2,0,1:T(8,128)(2,1)S(1)} all-gather(bf16[9,2,128]{2,0,1:T(8,128)(2,1)S(1)} %copy.46), channel_id=1, replica_groups=mesh['lat'=4,'lon'=128] {'lon'}, dimensions={1}, use_global_device_ids=true | all-gather | bytes 594432 | tf_op jit(solution)/shard_map/all_gather | solution.py:110
  737.7 1.7 fusion.82
  740.8 1.3 dynamic-slice
  742.7 347.6 %all-gather = bf16[128,2,128]{2,1,0:T(2,128)(2,1)S(1)} all-gather(bf16[1,2,128]{2,1,0:T(2,128)(2,1)S(1)} %bitcast.392), channel_id=1, replica_groups=mesh['lat'=4,'lon'=128] {'lon'}, dimensions={0}, use_global_device_ids=true | all-gather | bytes 66048 | tf_op jit(solution)/shard_map/all_gather | solution.py:112
  1090.4 1.9 collective-permute-start.3
  1092.3 3.9 collective-permute-start.2
  1096.4 1.9 collective-permute-start.10
  1098.3 9.6 collective-permute-start.11
  1108.3 1.0 collective-permute-done.11
  1117.0 1.9 collective-permute-start.5
  1118.9 2.4 collective-permute-start.4
  1121.4 3.2 collective-permute-start.13
  1124.5 1.9 collective-permute-start.12
  1128.7 1.0 multiply_convert_fusion
  1129.7 1.9 collective-permute-start.6
  1131.6 9.9 collective-permute-start.7
  1141.6 1.9 collective-permute-start.14
  1143.5 9.8 collective-permute-start.15
  1157.9 3.4 collective-permute-start.17
  1161.3 1.9 collective-permute-start.16
  1168.2 7.8 collective-permute-start.19
  1176.0 1.9 collective-permute-start.18
  1178.8 8.6 collective-permute-done.18
  1190.2 28.9 %all-reduce.12.cloned.1.call-done = (bf16[9,256,128]{2,1,0:T(8,128)(2,1)}, bf16[9,128,128]{2,1,0:T(8,128)(2,1)}, bf16[256,128]{1,0:T(8,128)(2,1)}) async-done(((bf16[9,256,128]{2,1,0:T(8,128)(2,1)}, bf16[9,128,128]{2,1,0:T(8,128)(2,1)}, bf16[256,128]{1,0:T(8,128)(2,1)}), (bf16[9,256,128]{2,1,0:T(8,128)(2,1)}, bf16[9,128,128]{2,1,0:T(8,128)(2,1)}, bf16[256,128]{1,0:T(8,128)(2,1)})) %all-reduce.12.cloned.1.call-update) | async-done | bytes 950288 | tf_op jit(solution)/shard_map/psum | solution.py:149
  1219.1 726.6 %all-reduce.13 = (f32[9,256,128]{2,1,0:T(8,128)S(1)}, f32[9,128,128]{2,1,0:T(8,128)S(1)}, f32[256,128]{1,0:T(8,128)S(1)}) all-reduce(bf16[9,256,128]{2,1,0:T(8,128)(2,1)} %get-tuple-element.8, bf16[9,128,128]{2,1,0:T(8,128)(2,1)} %get-tuple-element.9, ...), channel_id=2, replica_groups=mesh['lat'=4,'lon'=128] {'lon'}, use_global_device_ids=true, to_apply=%region_1.2.clone | all-reduce | flops 475136 | bytes 2850816
  1945.7 1.2 constant_dynamic-slice_fusion.1
  (172 shorter events, 27.3 us)
Async XLA Ops:
  7.2 1211.9 %all-reduce.12.cloned.1.call-start = ((), (), s32[]{:S(2)}) async-start(), calls=%async_computation | async-start | bytes 1900544 | tf_op jit(solution)/shard_map/psum | solution.py:149
  8.0 1082.3 %collective-permute-start = (bf16[1,32,256]{2,1,0:T(8,128)(2,1)S(1)}, bf16[1,32,256]{2,1,0:T(8,128)(2,1)S(1)}, u32[]{:S(2)}, u32[]{:S(2)}) collective-permute-start(bf16[1,32,256]{2,1,0:T(8,128)(2,1)S(1)} %get-tuple-element.97), channel_id=1, source_target_pairs={{0,128},{128,256},{256,384},{1,129},{129,257},{257,385},{2,130},{1... | collective-permute-start | bytes 49160 | tf_op jit(solution)/shard_map/ppermute | solution.py:16
  9.9 1080.4 %collective-permute-start.1 = (bf16[1,32,256]{2,1,0:T(8,128)(2,1)S(1)}, bf16[1,32,256]{2,1,0:T(8,128)(2,1)S(1)}, u32[]{:S(2)}, u32[]{:S(2)}) collective-permute-start(bf16[1,32,256]{2,1,0:T(8,128)(2,1)S(1)} %get-tuple-element.96), channel_id=1, source_target_pairs={{128,0},{256,128},{384,256},{129,1},{257,129},{385,257},{130,2},{2... | collective-permute-start | bytes 49160 | tf_op jit(solution)/shard_map/ppermute | solution.py:19
  14.3 1082.0 %collective-permute-start.8 = (bf16[1,64,128]{2,1,0:T(8,128)(2,1)S(1)}, bf16[1,64,128]{2,1,0:T(8,128)(2,1)S(1)}, u32[]{:S(2)}, u32[]{:S(2)}) collective-permute-start(bf16[1,64,128]{2,1,0:T(8,128)(2,1)S(1)} %get-tuple-element.89), channel_id=1, source_target_pairs={{0,128},{128,256},{256,384},{1,129},{129,257},{257,385},{2,130},{1... | collective-permute-start | bytes 49160 | tf_op jit(solution)/shard_map/ppermute | solution.py:16
  16.2 1080.1 %collective-permute-start.9 = (bf16[1,64,128]{2,1,0:T(8,128)(2,1)S(1)}, bf16[1,64,128]{2,1,0:T(8,128)(2,1)S(1)}, u32[]{:S(2)}, u32[]{:S(2)}) collective-permute-start(bf16[1,64,128]{2,1,0:T(8,128)(2,1)S(1)} %get-tuple-element.88), channel_id=1, source_target_pairs={{128,0},{256,128},{384,256},{129,1},{257,129},{385,257},{130,2},{2... | collective-permute-start | bytes 49160 | tf_op jit(solution)/shard_map/ppermute | solution.py:19
  21.8 363.3 %copy-start.19 = (bf16[9,2,128]{2,1,0:T(2,128)(2,1)S(1)}, bf16[9,2,128]{2,1,0:T(2,128)(2,1)}, u32[]{:S(2)}) copy-start(bf16[9,2,128]{2,1,0:T(2,128)(2,1)} %param.6) | copy-start | bytes 13828
  740.1 2.6 copy-start.20
  740.1 350.2 %copy-start.9 = (bf16[4,32,256]{2,1,0:T(8,128)(2,1)S(1)}, bf16[4,32,256]{2,1,0:T(8,128)(2,1)}, u32[]{:S(2)}) copy-start(bf16[4,32,256]{2,1,0:T(8,128)(2,1)} %param.5) | copy-start | bytes 196612
  740.1 356.1 %copy-start = (bf16[8,64,128]{2,1,0:T(8,128)(2,1)S(1)}, bf16[8,64,128]{2,1,0:T(8,128)(2,1)}, u32[]{:S(2)}) copy-start(bf16[8,64,128]{2,1,0:T(8,128)(2,1)} %param.9) | copy-start | bytes 393220
  1090.4 20.4 %collective-permute-start.3 = (bf16[6,1,256]{2,1,0:T(2,128)(2,1)S(1)}, bf16[6,1,256]{2,1,0:T(2,128)(2,1)S(1)}, u32[]{:S(2)}, u32[]{:S(2)}) collective-permute-start(bf16[6,1,256]{2,1,0:T(2,128)(2,1)S(1)} %get-tuple-element.95), channel_id=1, source_target_pairs={{1,0},{2,1},{3,2},{4,3},{5,4},{6,5},{7,6},{8,7},{9,8},{10,9},{11,1... | collective-permute-start | bytes 9224 | tf_op jit(solution)/shard_map/ppermute | solution.py:19
  1092.3 18.5 collective-permute-start.2
  1096.4 11.9 collective-permute-start.10
  1098.3 11.0 collective-permute-start.11
  1117.0 12.7 collective-permute-start.5
  1118.9 10.7 collective-permute-start.4
  1121.4 20.2 %collective-permute-start.13 = (bf16[1,64,128]{2,1,0:T(8,128)(2,1)S(1)}, bf16[1,64,128]{2,1,0:T(8,128)(2,1)S(1)}, u32[]{:S(2)}, u32[]{:S(2)}) collective-permute-start(bf16[1,64,128]{2,1,0:T(8,128)(2,1)S(1)} %get-tuple-element.84), channel_id=1, source_target_pairs={{128,0},{256,128},{384,256},{129,1},{257,129},{385,257},{130,2},{2... | collective-permute-start | bytes 49160 | tf_op jit(solution)/shard_map/ppermute | solution.py:19
  1124.5 17.1 collective-permute-start.12
  1129.7 24.6 %copy-start.11 = (bf16[1,128,128]{2,0,1:T(2,128)(2,1)S(1)}, bf16[1,128,128]{2,0,1:T(2,128)(2,1)}, u32[]{:S(2)}) copy-start(bf16[1,128,128]{2,0,1:T(2,128)(2,1)} %get-tuple-element.28) | copy-start | bytes 98308
  1129.7 24.7 %collective-permute-start.6 = (bf16[10,1,128]{2,1,0:T(2,128)(2,1)S(1)}, bf16[10,1,128]{2,1,0:T(2,128)(2,1)S(1)}, u32[]{:S(2)}, u32[]{:S(2)}) collective-permute-start(bf16[10,1,128]{2,1,0:T(2,128)(2,1)S(1)} %get-tuple-element.79), channel_id=1, source_target_pairs={{0,1},{1,2},{2,3},{3,4},{4,5},{5,6},{6,7},{7,8},{8,9},{9,10},{10,1... | collective-permute-start | bytes 7688 | tf_op jit(solution)/shard_map/ppermute | solution.py:16
  1131.6 22.8 %collective-permute-start.7 = (bf16[10,1,128]{2,1,0:T(2,128)(2,1)S(1)}, bf16[10,1,128]{2,1,0:T(2,128)(2,1)S(1)}, u32[]{:S(2)}, u32[]{:S(2)}) collective-permute-start(bf16[10,1,128]{2,1,0:T(2,128)(2,1)S(1)} %get-tuple-element.80), channel_id=1, source_target_pairs={{1,0},{2,1},{3,2},{4,3},{5,4},{6,5},{7,6},{8,7},{9,8},{10,9},{11,1... | collective-permute-start | bytes 7688 | tf_op jit(solution)/shard_map/ppermute | solution.py:19
  1141.6 14.0 collective-permute-start.14
  1143.5 12.1 collective-permute-start.15
  1157.9 10.2 collective-permute-start.17
  1161.3 6.8 collective-permute-start.16
  1164.2 1.8 copy-start.10
  1164.4 1.7 copy-start.2
  1164.4 1.7 copy-start.16
  1164.9 1.4 copy-start.1
  1164.9 1.4 copy-start.15
  1165.2 1.4 copy-start.14
  1168.2 10.6 collective-permute-start.19
  1176.0 11.4 collective-permute-start.18
  (11 other events, 9.9 us)
Sparse Core Ops, SparseCore 0:
  1167.7 51.2 all-reduce.11
where the time goes:
time: 1960 us; the launch traced here: 1950 us
  blocking collectives  1790 us (91%)
  starting transfers between devices  78.5 us (4%)
  waiting for transfers between devices  38.5 us (2%)
    unnamed x1, blocking collectives  727 us
    all_gather x1, blocking collectives, on_device(): lax.all_gather(w_second, 'lon', axis=1, tiled=True)  362 us
    all_gather x1, blocking collectives, on_device(): lax.all_gather(w_first, 'lon', axis=1, tiled=True)  353 us
    all_gather x1, blocking collectives, on_device(): lax.all_gather(w_skip, 'lon', axis=0, tiled=True)  348 us
    ppermute x10, starting transfers between devices, extended(): lax.ppermute(lax.slice_in_dim(block, 0, width, axis=dim), axis, backward)  56.8 us
  transfers between devices with their start and end apart: 21, of which 3 were waited for; matrix products, arithmetic and copies ran while one was open for 1% of the time, Pallas kernels for 0%

commit v1 on v0

v1 whole, which is shorter than its diff:
```python
import functools

import jax
import jax.numpy as jnp
import numpy as np
from jax import lax
from jax.experimental import pallas as pl
from jax.experimental.pallas import tpu as pltpu
from jax.sharding import Mesh, PartitionSpec as P

PITCH = 80
LENGTH = 14 * PITCH + 16
WIDE = (PITCH, 12 * PITCH + 96)
MIDDLE = (2 * PITCH, 12 * PITCH + 16)
HIDDEN = (2 * PITCH + 16, 12 * PITCH)
INNER = (256, 880)
F32 = jnp.float32
BF16 = jnp.bfloat16
SCALE = 1.0 / 512.0
LAT = ("xl", "core")
LON = ("z", "xh", "y")
PLANE = ("xl", "core", "xh", "y")


def upsampling_matrices():
    taps = {}
    for parity in range(2):
        for dc in (-1, 0, 1):
            for u in range(PITCH):
                row, col = (parity - 1, 64 + u + dc) if u < 8 else (parity, u - 16 + dc)
                if not -3 <= col <= 66:
                    continue
                for wr, m in ((0.75, row // 2), (0.25, row // 2 + (1 if row % 2 else -1))):
                    for wc, n in ((0.75, col // 2), (0.25, col // 2 + (1 if col % 2 else -1))):
                        taps[parity, (dc + 1) * PITCH + u, (m + 1) * 48 + n % 48] = wr * wc
    out = np.zeros((2, 3 * PITCH, 144), np.float32)
    for place, weight in taps.items():
        out[place] = weight
    return out


def decimation_matrix():
    out = np.zeros((32, 4 * PITCH + 16), np.float32)
    weights = (0.25, 0.75, 0.75, 0.25)
    for j in range(32):
        for a in range(4):
            for b in range(4):
                out[j, a * PITCH + 16 + 2 * j - 1 + b] = weights[a] * weights[b]
    return out


def channel_orders():
    spread = np.zeros((256, 256), np.float32)
    pairs = np.zeros((256, 256), np.float32)
    for p in range(8):
        for z in range(16):
            for k in range(2):
                spread[z * 16 + p * 2 + k, p * 32 + z * 2 + k] = 1.0
                pairs[k * 128 + z * 8 + p, p * 32 + z * 2 + k] = 1.0
    return spread, pairs


def dot(a, b):
    return lax.dot_general(a, b, (((1,), (0,)), ((), ())), preferred_element_type=F32)


def dot_nt(a, b):
    return lax.dot_general(a, b, (((1,), (1,)), ((), ())), preferred_element_type=F32)


def inside(bounds_ref, begin, shape):
    place = lax.broadcasted_iota(jnp.int32, shape, 0) + begin
    return (place >= bounds_ref[0]) & (place < bounds_ref[1])


def shifted(field):
    count = field.shape[0]
    return jnp.concatenate(
        [
            pltpu.roll(field, 1, 0).astype(BF16),
            field.astype(BF16),
            pltpu.roll(field, count - 1, 0).astype(BF16),
        ],
        axis=1,
    )


def cells(ref, begin, lanes=slice(None)):
    return jnp.concatenate(
        [ref[begin + PITCH * r : begin + PITCH * r + 64, lanes] for r in range(8)], axis=0
    )


def transposed(field):
    return field.astype(F32).T.astype(BF16)


def identity():
    shape = (256, 256)
    same = lax.broadcasted_iota(jnp.int32, shape, 0) == lax.broadcasted_iota(jnp.int32, shape, 1)
    return jnp.where(same, 1.0, 0.0).astype(BF16)


def prepare_kernel(bounds, coarse, cot, up, spread, fine3, cot3, skip_share):
    ordered = dot(coarse[...], spread[...]).astype(BF16)
    for r in range(-3, 12):
        j, parity = divmod(r, 2)
        block = dot(up[parity], ordered[(j + 2) * 48 : (j + 2) * 48 + 144])
        begin = (r + 3) * PITCH
        rows = min(PITCH, LENGTH - begin)
        keep = inside(bounds, begin, (rows, 256))
        for k in range(3):
            part = block[k * PITCH : k * PITCH + rows]
            fine3[begin : begin + rows, k * 256 : k * 256 + 256] = jnp.where(keep, part, 0.0).astype(BF16)
    cot3[...] = shifted(cot[...].astype(F32))
    share = dot(transposed(cells(cot, INNER[0])), cells(fine3, INNER[0], slice(256, 512)))
    share = (share * SCALE).astype(BF16)
    skip_share[...] = dot_nt(identity(), share).astype(BF16).reshape(8, 32, 128)


def first_block(weights, k):
    return weights[k // 4, :, k % 4].reshape(256, 128)


def gradient_kernel(
    bounds, weights, fine3, cot3, skip_share, pairs, pairs_t, shares, hidden3, grad_act, second
):
    for k in range(5):
        block = dot(pairs[...], first_block(weights, 10 + k)).astype(BF16)
        second[2 * k] = block[:128]
        second[2 * k + 1] = block[128:]
    begin, end = WIDE
    count = end - begin
    act = jnp.zeros((count, 128), F32)
    for i in range(3):
        kernels = jnp.concatenate([first_block(weights, 3 * i + j) for j in range(3)], axis=0)
        at = begin + PITCH * (i - 1)
        act = act + dot(fine3[at : at + count, :], kernels)
    keep = inside(bounds, begin, (count, 128))
    sigma = jax.nn.sigmoid(act)
    hidden = jnp.where(keep, act * sigma, 0.0)
    hidden3[...] = shifted(hidden)[HIDDEN[0] - begin : HIDDEN[1] - begin]
    grad_hidden = jnp.zeros((count, 128), F32)
    for i in range(3):
        kernels = jnp.concatenate([second[3 * i + 2 - j] for j in range(3)], axis=1)
        at = begin - PITCH * (i - 1)
        grad_hidden = grad_hidden + dot_nt(cot3[at : at + count, :], kernels)
    grad = grad_hidden * sigma * (1.0 + act * (1.0 - sigma))
    grad_act[...] = jnp.where(keep, grad, 0.0).astype(BF16)

    same = identity()
    flipped_grad = transposed(cells(grad_act, INNER[0] - begin))
    for i in range(3):
        share = dot(flipped_grad, cells(fine3, INNER[0] + PITCH * (i - 1)))
        share = (share * SCALE).astype(BF16)
        for j in range(3):
            block = dot_nt(same, share[:, j * 256 : j * 256 + 256]).astype(BF16)
            k = 3 * i + j
            shares[k // 4, :, k % 4] = block.reshape(8, 32, 128)
    shares[2, :, 1] = skip_share[...]
    flipped_cot = transposed(cells(cot3, INNER[0], slice(128, 256)))
    found = []
    for i in range(3):
        share = dot(flipped_cot, cells(hidden3, INNER[0] + PITCH * (i - 1) - HIDDEN[0]))
        share = (share * SCALE).astype(BF16)
        found += [share[:, j * 128 : j * 128 + 128] for j in range(3)]
    found.append(jnp.zeros((128, 128), BF16))
    for k in range(5):
        both = jnp.concatenate(found[2 * k : 2 * k + 2], axis=1)
        block = dot_nt(pairs_t[...], both).astype(BF16)
        b = 10 + k
        shares[b // 4, :, b % 4] = block.reshape(8, 32, 128)
    shares[3, :, 3] = jnp.zeros((8, 32, 128), BF16)


def field_kernel(
    bounds, weights, second, fine3, cot3, hidden3, grad_act, down, spread_t, result, coarse_gradient
):
    skip = first_block(weights, 9)
    begin, end = INNER
    total = dot(fine3[begin:end, 256:512], skip)
    for i in range(3):
        kernels = jnp.concatenate([second[3 * i + j] for j in range(3)], axis=0)
        at = begin + PITCH * (i - 1) - HIDDEN[0]
        total = total + dot(hidden3[at : at + end - begin, :], kernels)
    total = total.astype(BF16)
    for r in range(8):
        result[r] = total[r * PITCH : r * PITCH + 64]

    grad3 = shifted(grad_act[...].astype(F32))
    begin, end = MIDDLE
    count = end - begin
    back = dot_nt(cot3[begin:end, 128:256], skip)
    for i in range(3):
        kernels = jnp.concatenate([first_block(weights, 3 * i + 2 - j) for j in range(3)], axis=1)
        at = begin - PITCH * (i - 1) - WIDE[0]
        back = back + dot_nt(grad3[at : at + count], kernels)
    fine_gradient = jnp.where(inside(bounds, begin, (count, 256)), back, 0.0).astype(BF16)
    for j in range(4):
        part = dot(down[...], fine_gradient[2 * j * PITCH : 2 * j * PITCH + 4 * PITCH + 16])
        coarse_gradient[j] = dot(part.astype(BF16), spread_t[...]).astype(BF16)


def call(kernel, outs, *operands):
    vmem = pl.BlockSpec(memory_space=pltpu.VMEM)
    smem = pl.BlockSpec(memory_space=pltpu.SMEM)
    return pl.pallas_call(
        kernel,
        out_shape=[jax.ShapeDtypeStruct(shape, BF16) for shape in outs],
        in_specs=[smem] + [vmem] * (len(operands) - 1),
        out_specs=[vmem] * len(outs),
        compiler_params=pltpu.CompilerParams(vmem_limit_bytes=40 * 1024 * 1024),
    )(*operands)


def neighbours(low_side, high_side, axis, periodic):
    count = lax.axis_size(axis)
    up = [(i, i + 1) for i in range(count - 1)] + ([(count - 1, 0)] if periodic else [])
    down = [(b, a) for a, b in up]
    return lax.ppermute(high_side, axis, up), lax.ppermute(low_side, axis, down)


def coarse_field(coarse):
    low, high = neighbours(coarse[:2], coarse[-2:], LAT, False)
    tall = jnp.concatenate([low, coarse, high], axis=0)
    left, right = neighbours(tall[:, :2], tall[:, -2:], LON, True)
    gap = jnp.zeros((8, 12, 256), BF16)
    wide = jnp.concatenate([tall, right, gap, left], axis=1)
    return jnp.pad(wide, ((1, 1), (0, 0), (0, 0))).reshape(480, 256)


def cot_field(cotangent):
    low, high = neighbours(cotangent[:3], cotangent[-3:], LAT, False)
    tall = jnp.concatenate([low, cotangent, high], axis=0)
    left, right = neighbours(tall[:, :3], tall[:, -3:], LON, True)
    after = ((0, 1), (0, 0), (0, 0))
    gap = jnp.zeros((15, 10, 128), BF16)
    wide = jnp.concatenate(
        [jnp.pad(right, ((1, 0), (0, 0), (0, 0))), gap, jnp.pad(left, after), jnp.pad(tall, after)],
        axis=1,
    )
    return wide.reshape(15 * PITCH, 128)[:LENGTH]


def gathered(w_first, w_second, w_skip):
    pairs = jnp.pad(w_second.reshape(9, 128), ((0, 3), (0, 0))).reshape(6, 2, 128)
    mine = jnp.concatenate([w_first, w_skip[None], pairs], axis=0)
    piece = lax.dynamic_slice_in_dim(mine, 4 * lax.axis_index(LAT), 4, 0)
    sent = jnp.broadcast_to(piece[None], (16, 4, 2, 128))
    came = lax.all_to_all(sent, "z", 0, 0, tiled=True)
    block = came.transpose(1, 0, 2, 3).reshape(4, 32, 128)
    sent = jnp.broadcast_to(block[None], (32, 4, 32, 128))
    return lax.all_to_all(sent, PLANE, 0, 0, tiled=True).reshape(4, 8, 4, 32, 128)


def summed(shares):
    came = lax.all_to_all(shares.reshape(32, 4, 32, 128), PLANE, 0, 0, tiled=True)
    part = jnp.sum(came.astype(F32), axis=0).astype(BF16)
    part = part.reshape(4, 16, 2, 128).transpose(1, 0, 2, 3)
    sent = jnp.broadcast_to(part[None], (4, 16, 4, 2, 128)).reshape(64, 4, 2, 128)
    came = lax.all_to_all(sent, LAT + ("z",), 0, 0, tiled=True)
    return jnp.sum(came.reshape(4, 16, 4, 2, 128).astype(F32), axis=1).reshape(16, 2, 128)


def on_device(coarse, w_first, w_second, w_skip, cotangent):
    spread, pairs = channel_orders()
    spread, spread_t, pairs, pairs_t, up, down = (
        jnp.asarray(m, BF16)
        for m in (spread, spread.T, pairs, pairs.T, upsampling_matrices(), decimation_matrix())
    )
    lat = lax.axis_index(LAT)
    bounds = jnp.stack([jnp.where(lat == 0, 248, 0), jnp.where(lat == 3, 888, LENGTH)]).astype(jnp.int32)

    weights = gathered(w_first, w_second, w_skip)
    fine3, cot3, skip_share = call(
        prepare_kernel,
        [(LENGTH, 768), (LENGTH, 384), (8, 32, 128)],
        bounds, coarse_field(coarse), cot_field(cotangent), up, spread,
    )
    shares, hidden3, grad_act, second = call(
        gradient_kernel,
        [(4, 8, 4, 32, 128), (HIDDEN[1] - HIDDEN[0], 384), (WIDE[1] - WIDE[0], 128), (10, 128, 128)],
        bounds, weights, fine3, cot3, skip_share, pairs, pairs_t,
    )
    grads = summed(shares)
    result, coarse_gradient = call(
        field_kernel,
        [(8, 64, 128), (4, 32, 256)],
        bounds, weights, second, fine3, cot3, hidden3, grad_act, down, spread_t,
    )
    grad_second = grads[10:15].reshape(10, 1, 128)[:9]
    return result, coarse_gradient, grads[:9], grad_second, grads[9]


def solution(mesh):
    axes = ("xl", "core", "z", "xh", "y")
    fine = Mesh(mesh.devices.reshape(2, 2, 16, 2, 4), axes)
    field, taps, plain = P(LAT, LON, None), P(None, LON, None), P(LON, None)
    return jax.shard_map(
        on_device,
        mesh=fine,
        in_specs=(field, taps, taps, plain, field),
        out_specs=(field, field, taps, taps, plain),
        check_vma=False,
    )
```

time: 1960 us -> 141 us (0.07)
  the two profiles are of different devices: /device:TPU:2 before, /device:TPU:1 now
where the time goes in v1:
time: 141 us; the launch traced here: 140 us
  starting transfers between devices  68 us (48%)
  blocking collectives  21.3 us (15%)
  local copies, waits for them, and re-layouts  17.6 us (12%)
  waiting for transfers between devices  17.4 us (12%)
  Pallas kernels  10.2 us (7%)
  other arithmetic  3.99 us (3%)
    ppermute x4, starting transfers between devices, neighbours(): lax.ppermute(low_side, axis, down)  25.1 us
    all_to_all x1, blocking collectives, summed(): lax.all_to_all(shares.reshape(32, 4, 32, 128), PLANE, 0, 0, tiled=True)  21.3 us
    all_to_all x1, starting transfers between devices, gathered(): came = lax.all_to_all(sent, 'z', 0, 0, tiled=True)  15.7 us
    all_to_all x1, starting transfers between devices, summed(): came = lax.all_to_all(sent, LAT + ('z',), 0, 0, tiled=True)  11.5 us
    ppermute x4, starting transfers between devices, neighbours(): lax.ppermute(high_side, axis, up)  10.5 us
    unnamed x38, local copies, waits for them, and re-layouts  10.5 us
    pallas_call x3, Pallas kernels, call(): pl.pallas_call(kernel, out_shape=[jax.ShapeDtypeStruct(shape, BF16) for s...  10.2 us
    all_to_all x1, waiting for transfers between devices, summed(): came = lax.all_to_all(sent, LAT + ('z',), 0, 0, tiled=True)  9.3 us
  transfers between devices with their start and end apart: 11, of which 2 were waited for; matrix products, arithmetic and copies ran while one was open for 3% of the time, Pallas kernels for 4%

profile of v1, /device:TPU:1, one launch (start us, length us, event | category | flops | bytes accessed | tf_op | source)
XLA Modules:
  0.0 139.6 jit_solution(15838519322517257391)
XLA Ops:
  1.4 0.7 fusion.8
  2.7 15.7 %all-to-all-start = ((bf16[16,4,2,128]{3,2,1,0:T(2,128)(2,1)}), bf16[16,4,2,128]{3,2,1,0:T(2,128)(2,1)S(1)}, u32[]{:S(2)}, u32[]{:S(2)}) async-start(bf16[16,4,2,128]{3,2,1,0:T(2,128)(2,1)} %broadcast_in_dim.29), calls=%async_computation | async-start | bytes 65536 | tf_op jit(solution)/shard_map/all_to_all | solution.py:250
  18.5 0.8 fusion.12
  19.2 2.9 %collective-permute-start.1 = (bf16[2,32,256]{2,1,0:T(8,128)(2,1)S(1)}, bf16[2,32,256]{2,1,0:T(8,128)(2,1)S(1)}, u32[]{:S(2)}, u32[]{:S(2)}) collective-permute-start(bf16[2,32,256]{2,1,0:T(8,128)(2,1)S(1)} %get-tuple-element.64), channel_id=1, source_target_pairs={{128,0},{256,128},{384,256},{129,1},{257,129},{385,257},{130,2},{2... | collective-permute-start | bytes 98312 | tf_op jit(solution)/shard_map/ppermute | solution.py:220
  22.1 3.0 %collective-permute-start = (bf16[2,32,256]{2,1,0:T(8,128)(2,1)S(1)}, bf16[2,32,256]{2,1,0:T(8,128)(2,1)S(1)}, u32[]{:S(2)}, u32[]{:S(2)}) collective-permute-start(bf16[2,32,256]{2,1,0:T(8,128)(2,1)S(1)} %get-tuple-element.65), channel_id=1, source_target_pairs={{0,128},{128,256},{256,384},{1,129},{129,257},{257,385},{2,130},{1... | collective-permute-start | bytes 98312 | tf_op jit(solution)/shard_map/ppermute | solution.py:220
  25.1 0.8 fusion.10
  25.9 1.9 %collective-permute-start.5 = (bf16[3,64,128]{2,1,0:T(8,128)(2,1)S(1)}, bf16[3,64,128]{2,1,0:T(8,128)(2,1)S(1)}, u32[]{:S(2)}, u32[]{:S(2)}) collective-permute-start(bf16[3,64,128]{2,1,0:T(8,128)(2,1)S(1)} %get-tuple-element.60), channel_id=1, source_target_pairs={{128,0},{256,128},{384,256},{129,1},{257,129},{385,257},{130,2},{2... | collective-permute-start | bytes 147464 | tf_op jit(solution)/shard_map/ppermute | solution.py:220
  27.9 3.6 %collective-permute-start.4 = (bf16[3,64,128]{2,1,0:T(8,128)(2,1)S(1)}, bf16[3,64,128]{2,1,0:T(8,128)(2,1)S(1)}, u32[]{:S(2)}, u32[]{:S(2)}) collective-permute-start(bf16[3,64,128]{2,1,0:T(8,128)(2,1)S(1)} %get-tuple-element.61), channel_id=1, source_target_pairs={{0,128},{128,256},{256,384},{1,129},{129,257},{257,385},{2,130},{1... | collective-permute-start | bytes 147464 | tf_op jit(solution)/shard_map/ppermute | solution.py:220
  31.8 0.8 constant_dynamic-update-slice_fusion.1
  32.7 9.5 %collective-permute-start.2 = (bf16[8,2,256]{2,1,0:T(2,128)(2,1)S(1)}, bf16[8,2,256]{2,1,0:T(2,128)(2,1)S(1)}, u32[]{:S(2)}, u32[]{:S(2)}) collective-permute-start(bf16[8,2,256]{2,1,0:T(2,128)(2,1)S(1)} %get-tuple-element.62), channel_id=1, source_target_pairs={{1,0},{2,1},{3,2},{4,3},{5,4},{6,5},{7,6},{8,7},{9,8},{10,9},{11,1... | collective-permute-start | bytes 24584 | tf_op jit(solution)/shard_map/ppermute | solution.py:220
  42.2 1.9 %collective-permute-start.3 = (bf16[8,2,256]{2,1,0:T(2,128)(2,1)S(1)}, bf16[8,2,256]{2,1,0:T(2,128)(2,1)S(1)}, u32[]{:S(2)}, u32[]{:S(2)}) collective-permute-start(bf16[8,2,256]{2,1,0:T(2,128)(2,1)S(1)} %get-tuple-element.63), channel_id=1, source_target_pairs={{0,1},{1,2},{2,3},{3,4},{4,5},{5,6},{6,7},{7,8},{8,9},{9,10},{10,1... | collective-permute-start | bytes 24584 | tf_op jit(solution)/shard_map/ppermute | solution.py:220
  44.2 1.2 broadcast_in_dim.31
  45.4 5.2 %all-to-all-start.1 = ((bf16[32,4,32,128]{3,2,1,0:T(8,128)(2,1)}), bf16[32,4,32,128]{3,2,1,0:T(8,128)(2,1)S(1)}, u32[]{:S(2)}, u32[]{:S(2)}) async-start(bf16[32,4,32,128]{3,2,1,0:T(8,128)(2,1)} %broadcast_in_dim.31), calls=%async_computation.1 | async-start | bytes 2097152 | tf_op jit(solution)/shard_map/all_to_all | solution.py:253
  50.8 10.8 %collective-permute-start.6 = (bf16[14,3,128]{2,1,0:T(4,128)(2,1)S(1)}, bf16[14,3,128]{2,1,0:T(4,128)(2,1)S(1)}, u32[]{:S(2)}, u32[]{:S(2)}) collective-permute-start(bf16[14,3,128]{2,1,0:T(4,128)(2,1)S(1)} %get-tuple-element.58), channel_id=1, source_target_pairs={{1,0},{2,1},{3,2},{4,3},{5,4},{6,5},{7,6},{8,7},{9,8},{10,9},{11,1... | collective-permute-start | bytes 32264 | tf_op jit(solution)/shard_map/ppermute | solution.py:220
  61.6 1.9 %collective-permute-start.7 = (bf16[14,3,128]{2,1,0:T(4,128)(2,1)S(1)}, bf16[14,3,128]{2,1,0:T(4,128)(2,1)S(1)}, u32[]{:S(2)}, u32[]{:S(2)}) collective-permute-start(bf16[14,3,128]{2,1,0:T(4,128)(2,1)S(1)} %get-tuple-element.59), channel_id=1, source_target_pairs={{0,1},{1,2},{2,3},{3,4},{4,5},{5,6},{6,7},{7,8},{8,9},{9,10},{10,1... | collective-permute-start | bytes 32264 | tf_op jit(solution)/shard_map/ppermute | solution.py:220
  63.7 8.1 %collective-permute-done.7 = bf16[14,3,128]{2,1,0:T(4,128)(2,1)S(1)} collective-permute-done((bf16[14,3,128]{2,1,0:T(4,128)(2,1)S(1)}, bf16[14,3,128]{2,1,0:T(4,128)(2,1)S(1)}, u32[]{:S(2)}, u32[]{:S(2)}) %collective-permute-start.7) | collective-permute-done | bytes 10784 | tf_op jit(solution)/shard_map/ppermute | solution.py:220
  71.9 2.0 %shard_map.146 = (bf16[1136,768]{1,0:T(8,128)(2,1)S(1)}, bf16[1136,384]{1,0:T(8,128)(2,1)S(1)}, bf16[8,32,128]{2,1,0:T(8,128)(2,1)S(1)}) custom-call(s32[2]{0:T(128)S(1)} %pad_add_fusion.bounds, bf16[480,256]{1,0:T(8,128)(2,1)S(1)} %bitcast.24, bf16[1136,128]{1,0:T(8,128)(2,1)S(1)} %slice.56.cot, bf16[2,240,144]{2,1,0:T(8,128)(2,1)S(1)} %copy-done.7, ...), custom_call_target="tpu_custom_call" | custom-call | tf_op jit(solution)/shard_map/pallas_call | solution.py:207
  73.9 0.9 copy-done
  75.5 1.2 copy-done.1
  76.6 0.9 copy-done.10
  77.5 0.8 copy-done.13
  78.4 4.9 %shard_map.147 = (bf16[4,8,4,32,128]{4,3,2,1,0:T(8,128)(2,1)S(1)}, bf16[784,384]{1,0:T(8,128)(2,1)S(1)}, bf16[976,128]{1,0:T(8,128)(2,1)S(1)}, bf16[10,128,128]{2,1,0:T(8,128)(2,1)S(1)}) custom-call(s32[2]{0:T(128)S(1)} %pad_add_fusion.bounds, bf16[4,8,4,32,128]{4,3,2,1,0:T(8,128)(2,1)S(1)} %bitcast.21, bf16[1136,768]{1,0:T(8,128)(2,1)S(1)} %get-tuple-element.14.fine3, ...), custom_call_target="tpu_custom_call" | custom-call | tf_op jit(solution)/shard_map/pallas_call | solution.py:207
  84.7 21.3 %all_to_all.20 = bf16[32,4,32,128]{3,2,1,0:T(8,128)(2,1)} all-to-all(bf16[32,4,32,128]{3,2,1,0:T(8,128)(2,1)S(1)} %bitcast.23), channel_id=1, replica_groups=mesh['xl'=2,'core'=2,'z'=16,'xh'=2,'y'=4] {'xl','core','xh','y'}, dimensions={0} | all-to-all | bytes 2097152 | tf_op jit(solution)/shard_map/all_to_all | solution.py:257
  106.0 2.0 %reduce_sum.21 = bf16[4,32,128]{2,1,0:T(8,128)(2,1)} reduce(bf16[32,4,32,128]{3,2,1,0:T(8,128)(2,1)} %all_to_all.20, bf16[]{:T(256)} %constant.41.clone.1), dimensions={0}, to_apply=%region_0.1 | reduce | flops 507904 | bytes 1081346 | tf_op jit(solution)/shard_map/reduce_sum | solution.py:258
  108.0 0.8 copy.36
  109.5 11.5 %all-to-all-start.3 = ((bf16[64,4,2,128]{3,2,1,0:T(2,128)(2,1)}), bf16[64,4,2,128]{3,2,1,0:T(2,128)(2,1)}, u32[]{:S(2)}, u32[]{:S(2)}) async-start(bf16[64,4,2,128]{3,2,1,0:T(2,128)(2,1)} %bitcast.26), calls=%async_computation.3 | async-start | bytes 262144 | tf_op jit(solution)/shard_map/all_to_all | solution.py:261
  121.0 1.2 copy-done.2
  122.2 1.0 copy-done.4
  123.1 0.9 copy-done.6
  124.1 3.4 %shard_map.148 = (bf16[8,64,128]{2,1,0:T(8,128)(2,1)}, bf16[4,32,256]{2,1,0:T(8,128)(2,1)}) custom-call(s32[2]{0:T(128)S(1)} %pad_add_fusion.bounds, bf16[4,8,4,32,128]{4,3,2,1,0:T(8,128)(2,1)S(1)} %bitcast.22, bf16[10,128,128]{2,1,0:T(8,128)(2,1)S(1)} %copy-done.4, bf16[1136,768]{1,0:T(8,128)(2,1)S(1)} %get-tuple-element.14.fine3, ...), custom_call_target="tpu_custom_call" | custom-call | tf_op jit(solution)/shard_map/pallas_call | solution.py:207
  127.5 9.3 %all-to-all-done.3 = bf16[64,4,2,128]{3,2,1,0:T(2,128)(2,1)} async-done(((bf16[64,4,2,128]{3,2,1,0:T(2,128)(2,1)}), bf16[64,4,2,128]{3,2,1,0:T(2,128)(2,1)}, u32[]{:S(2)}, u32[]{:S(2)}) %all-to-all-start.3) | async-done | bytes 131104 | tf_op jit(solution)/shard_map/all_to_all | solution.py:261
  136.8 1.0 convert_reduce_fusion
  (61 shorter events, 6.6 us)
Async XLA Ops:
  2.7 41.4 %all-to-all-start = ((bf16[16,4,2,128]{3,2,1,0:T(2,128)(2,1)}), bf16[16,4,2,128]{3,2,1,0:T(2,128)(2,1)S(1)}, u32[]{:S(2)}, u32[]{:S(2)}) async-start(bf16[16,4,2,128]{3,2,1,0:T(2,128)(2,1)} %broadcast_in_dim.29), calls=%async_computation | async-start | bytes 65536 | tf_op jit(solution)/shard_map/all_to_all | solution.py:250
  19.2 13.4 %collective-permute-start.1 = (bf16[2,32,256]{2,1,0:T(8,128)(2,1)S(1)}, bf16[2,32,256]{2,1,0:T(8,128)(2,1)S(1)}, u32[]{:S(2)}, u32[]{:S(2)}) collective-permute-start(bf16[2,32,256]{2,1,0:T(8,128)(2,1)S(1)} %get-tuple-element.64), channel_id=1, source_target_pairs={{128,0},{256,128},{384,256},{129,1},{257,129},{385,257},{130,2},{2... | collective-permute-start | bytes 98312 | tf_op jit(solution)/shard_map/ppermute | solution.py:220
  22.1 9.7 %collective-permute-start = (bf16[2,32,256]{2,1,0:T(8,128)(2,1)S(1)}, bf16[2,32,256]{2,1,0:T(8,128)(2,1)S(1)}, u32[]{:S(2)}, u32[]{:S(2)}) collective-permute-start(bf16[2,32,256]{2,1,0:T(8,128)(2,1)S(1)} %get-tuple-element.65), channel_id=1, source_target_pairs={{0,128},{128,256},{256,384},{1,129},{129,257},{257,385},{2,130},{1... | collective-permute-start | bytes 98312 | tf_op jit(solution)/shard_map/ppermute | solution.py:220
  25.9 24.8 %collective-permute-start.5 = (bf16[3,64,128]{2,1,0:T(8,128)(2,1)S(1)}, bf16[3,64,128]{2,1,0:T(8,128)(2,1)S(1)}, u32[]{:S(2)}, u32[]{:S(2)}) collective-permute-start(bf16[3,64,128]{2,1,0:T(8,128)(2,1)S(1)} %get-tuple-element.60), channel_id=1, source_target_pairs={{128,0},{256,128},{384,256},{129,1},{257,129},{385,257},{130,2},{2... | collective-permute-start | bytes 147464 | tf_op jit(solution)/shard_map/ppermute | solution.py:220
  27.9 22.8 %collective-permute-start.4 = (bf16[3,64,128]{2,1,0:T(8,128)(2,1)S(1)}, bf16[3,64,128]{2,1,0:T(8,128)(2,1)S(1)}, u32[]{:S(2)}, u32[]{:S(2)}) collective-permute-start(bf16[3,64,128]{2,1,0:T(8,128)(2,1)S(1)} %get-tuple-element.61), channel_id=1, source_target_pairs={{0,128},{128,256},{256,384},{1,129},{129,257},{257,385},{2,130},{1... | collective-permute-start | bytes 147464 | tf_op jit(solution)/shard_map/ppermute | solution.py:220
  32.6 18.1 %copy-start.15 = (bf16[8,64,128]{2,1,0:T(8,128)(2,1)S(1)}, bf16[8,64,128]{2,1,0:T(8,128)(2,1)}, u32[]{:S(2)}) copy-start(bf16[8,64,128]{2,1,0:T(8,128)(2,1)} %param.15) | copy-start | bytes 393220
  32.7 30.9 %collective-permute-start.2 = (bf16[8,2,256]{2,1,0:T(2,128)(2,1)S(1)}, bf16[8,2,256]{2,1,0:T(2,128)(2,1)S(1)}, u32[]{:S(2)}, u32[]{:S(2)}) collective-permute-start(bf16[8,2,256]{2,1,0:T(2,128)(2,1)S(1)} %get-tuple-element.62), channel_id=1, source_target_pairs={{1,0},{2,1},{3,2},{4,3},{5,4},{6,5},{7,6},{8,7},{9,8},{10,9},{11,1... | collective-permute-start | bytes 24584 | tf_op jit(solution)/shard_map/ppermute | solution.py:220
  42.2 21.3 %collective-permute-start.3 = (bf16[8,2,256]{2,1,0:T(2,128)(2,1)S(1)}, bf16[8,2,256]{2,1,0:T(2,128)(2,1)S(1)}, u32[]{:S(2)}, u32[]{:S(2)}) collective-permute-start(bf16[8,2,256]{2,1,0:T(2,128)(2,1)S(1)} %get-tuple-element.63), channel_id=1, source_target_pairs={{0,1},{1,2},{2,3},{3,4},{4,5},{5,6},{6,7},{7,8},{8,9},{9,10},{10,1... | collective-permute-start | bytes 24584 | tf_op jit(solution)/shard_map/ppermute | solution.py:220
  45.4 30.1 %all-to-all-start.1 = ((bf16[32,4,32,128]{3,2,1,0:T(8,128)(2,1)}), bf16[32,4,32,128]{3,2,1,0:T(8,128)(2,1)S(1)}, u32[]{:S(2)}, u32[]{:S(2)}) async-start(bf16[32,4,32,128]{3,2,1,0:T(8,128)(2,1)} %broadcast_in_dim.31), calls=%async_computation.1 | async-start | bytes 2097152 | tf_op jit(solution)/shard_map/all_to_all | solution.py:253
  50.6 21.3 %copy-start.7 = (bf16[2,240,144]{2,1,0:T(8,128)(2,1)S(1)}, bf16[2,240,144]{2,1,0:T(8,128)(2,1)}, u32[]{:S(2)}) copy-start(bf16[2,240,144]{2,1,0:T(8,128)(2,1)} %constant.49.clone.up) | copy-start | bytes 414724
  50.6 21.3 %copy-start.11 = (bf16[256,256]{1,0:T(8,128)(2,1)S(1)}, bf16[256,256]{1,0:T(8,128)(2,1)}, u32[]{:S(2)}) copy-start(bf16[256,256]{1,0:T(8,128)(2,1)} %constant.45.clone.spread) | copy-start | bytes 393220
  50.6 24.9 %copy-start.9 = (bf16[256,256]{1,0:T(8,128)(2,1)S(1)}, bf16[256,256]{1,0:T(8,128)(2,1)}, u32[]{:S(2)}) copy-start(bf16[256,256]{1,0:T(8,128)(2,1)} %constant.48.clone.pairs_t) | copy-start | bytes 393220
  50.8 12.9 %collective-permute-start.6 = (bf16[14,3,128]{2,1,0:T(4,128)(2,1)S(1)}, bf16[14,3,128]{2,1,0:T(4,128)(2,1)S(1)}, u32[]{:S(2)}, u32[]{:S(2)}) collective-permute-start(bf16[14,3,128]{2,1,0:T(4,128)(2,1)S(1)} %get-tuple-element.58), channel_id=1, source_target_pairs={{1,0},{2,1},{3,2},{4,3},{5,4},{6,5},{7,6},{8,7},{9,8},{10,9},{11,1... | collective-permute-start | bytes 32264 | tf_op jit(solution)/shard_map/ppermute | solution.py:220
  61.6 10.2 %collective-permute-start.7 = (bf16[14,3,128]{2,1,0:T(4,128)(2,1)S(1)}, bf16[14,3,128]{2,1,0:T(4,128)(2,1)S(1)}, u32[]{:S(2)}, u32[]{:S(2)}) collective-permute-start(bf16[14,3,128]{2,1,0:T(4,128)(2,1)S(1)} %get-tuple-element.59), channel_id=1, source_target_pairs={{0,1},{1,2},{2,3},{3,4},{4,5},{5,6},{6,7},{7,8},{8,9},{9,10},{10,1... | collective-permute-start | bytes 32264 | tf_op jit(solution)/shard_map/ppermute | solution.py:220
  73.9 0.9 copy-start
  74.8 0.6 copy-start.12
  75.5 1.2 copy-start.1
  76.6 0.9 copy-start.10
  77.5 0.8 copy-start.13
  83.2 0.7 copy-start.3
  84.0 0.7 copy-start.5
  84.7 36.3 %copy-start.8 = (bf16[256,256]{1,0:T(8,128)(2,1)S(1)}, bf16[256,256]{1,0:T(8,128)(2,1)}, u32[]{:S(2)}) copy-start(bf16[256,256]{1,0:T(8,128)(2,1)} %constant.46.clone.spread_t) | copy-start | bytes 393220
  84.7 36.3 %copy-start.14 = (bf16[32,336]{1,0:T(8,128)(2,1)S(1)}, bf16[32,336]{1,0:T(8,128)(2,1)}, u32[]{:S(2)}) copy-start(bf16[32,336]{1,0:T(8,128)(2,1)} %constant.50.clone.down) | copy-start | bytes 64516
  109.5 27.3 %all-to-all-start.3 = ((bf16[64,4,2,128]{3,2,1,0:T(2,128)(2,1)}), bf16[64,4,2,128]{3,2,1,0:T(2,128)(2,1)}, u32[]{:S(2)}, u32[]{:S(2)}) async-start(bf16[64,4,2,128]{3,2,1,0:T(2,128)(2,1)} %bitcast.26), calls=%async_computation.3 | async-start | bytes 262144 | tf_op jit(solution)/shard_map/all_to_all | solution.py:261
  121.0 1.2 copy-start.2
  122.2 1.0 copy-start.4
  123.1 0.9 copy-start.6

commit v2 on v1

v2 whole, which is shorter than its diff:
```python
import jax
import jax.numpy as jnp
import numpy as np
from jax import lax
from jax.experimental import pallas as pl
from jax.experimental.pallas import tpu as pltpu
from jax.sharding import Mesh, PartitionSpec as P

PITCH = 80
LENGTH = 14 * PITCH + 16
WIDE = (PITCH, 12 * PITCH + 96)
MIDDLE = (2 * PITCH, 12 * PITCH + 16)
HIDDEN = (2 * PITCH + 16, 12 * PITCH)
INNER = (256, 880)
F32 = jnp.float32
BF16 = jnp.bfloat16
SCALE = 1.0 / 512.0
LAT = ("xl", "core")
LON = ("z", "xh", "y")
PLANE = ("xl", "core", "xh", "y")


def upsampling_matrices():
    taps = {}
    for parity in range(2):
        for dc in (-1, 0, 1):
            for u in range(PITCH):
                row, col = (parity - 1, 64 + u + dc) if u < 8 else (parity, u - 16 + dc)
                if not -3 <= col <= 66:
                    continue
                for wr, m in ((0.75, row // 2), (0.25, row // 2 + (1 if row % 2 else -1))):
                    for wc, n in ((0.75, col // 2), (0.25, col // 2 + (1 if col % 2 else -1))):
                        taps[parity, (dc + 1) * PITCH + u, (m + 1) * 48 + n % 48] = wr * wc
    out = np.zeros((2, 3 * PITCH, 144), np.float32)
    for place, weight in taps.items():
        out[place] = weight
    return out


def decimation_matrix():
    out = np.zeros((32, 4 * PITCH + 16), np.float32)
    weights = (0.25, 0.75, 0.75, 0.25)
    for j in range(32):
        for a in range(4):
            for b in range(4):
                out[j, a * PITCH + 16 + 2 * j - 1 + b] = weights[a] * weights[b]
    return out


def spread_row(column):
    return ((column >> 1) & 15) * 16 + (column >> 5) * 2 + (column & 1)


def pair_row(column):
    return (column & 1) * 128 + ((column >> 1) & 15) * 8 + (column >> 5)


def block_row(row):
    return ((row >> 1) & 15) * 8 + (row >> 5) * 2 + (row & 1)


def permutation(size, place, by_column):
    rows = lax.broadcasted_iota(jnp.int32, (size, size), 0)
    columns = lax.broadcasted_iota(jnp.int32, (size, size), 1)
    same = rows == place(columns) if by_column else columns == place(rows)
    return jnp.where(same, 1.0, 0.0).astype(BF16)


def dot(a, b):
    return lax.dot_general(a, b, (((1,), (0,)), ((), ())), preferred_element_type=F32)


def dot_nt(a, b):
    return lax.dot_general(a, b, (((1,), (1,)), ((), ())), preferred_element_type=F32)


def inside(bounds_ref, begin, shape):
    place = lax.broadcasted_iota(jnp.int32, shape, 0) + begin
    return (place >= bounds_ref[0]) & (place < bounds_ref[1])


def shifted(field):
    count = field.shape[0]
    return jnp.concatenate(
        [
            pltpu.roll(field, 1, 0).astype(BF16),
            field.astype(BF16),
            pltpu.roll(field, count - 1, 0).astype(BF16),
        ],
        axis=1,
    )


def cells(ref, begin, lanes=slice(None)):
    return jnp.concatenate(
        [ref[begin + PITCH * r : begin + PITCH * r + 64, lanes] for r in range(8)], axis=0
    )


def transposed(field):
    return field.astype(F32).T.astype(BF16)


def identity():
    return permutation(256, lambda row: row, True)


def copied(pairs, semaphores):
    copies = [pltpu.make_async_copy(a, b, semaphores.at[i]) for i, (a, b) in enumerate(pairs)]
    for copy in copies:
        copy.start()
    return copies


def finish(copies):
    for copy in copies:
        copy.wait()


def pack_kernel(lat, first, second, skip, sent, rows, first_here, second_here, skip_here, semaphores):
    copies = copied([(first, first_here), (second, second_here), (skip, skip_here)], semaphores)
    rows[...] = jnp.zeros((32, 128), F32)
    finish(copies)
    for k in range(9):
        rows[2 * k : 2 * k + 2] = first_here[k].astype(F32)
    rows[20:29] = second_here[...].astype(F32)
    rows[18:20] = skip_here[...].astype(F32)
    piece = rows[pl.ds(pl.multiple_of(lat[0] * 8, 8), 8)].astype(BF16)
    sent[...] = jnp.broadcast_to(piece[None], (16, 8, 128))


def either(flag, a, b):
    return jnp.where(flag, a.astype(F32), b.astype(F32)).astype(BF16)


def exchanged(swap, moves, out_a, out_b, semaphores):
    @pl.when(swap)
    def _():
        finish(copied(moves(out_b, out_a), semaphores))

    @pl.when(jnp.logical_not(swap))
    def _():
        finish(copied(moves(out_a, out_b), semaphores))


def lat_edge_kernel(spots, coarse, cot, out_a, out_b, semaphores):
    def moves(up, down):
        found = []
        for out, first, second in ((up, 5, 2), (down, 0, 0)):
            found.append((cot.at[first : first + 3], out.at[0:3]))
            for h in range(2):
                lanes = slice(128 * h, 128 * h + 128)
                found.append((coarse.at[second : second + 2, :, lanes], out.at[3:5, 32 * h : 32 * h + 32]))
        return found

    exchanged(spots[1] == 1, moves, out_a, out_b, semaphores)


def edge_at(m, h):
    return 16 + 8 * h + m


def lon_edge_kernel(spots, coarse, cot, lat_a, lat_b, out_a, out_b, semaphores):
    def side_by_side(low, high):
        def moves(up, down):
            found = []
            for out, c, w in ((up, 48, 16), (down, 0, 0)):
                wide, narrow = slice(c, c + 16), slice(w, w + 16)
                found.append((cot.at[:, wide], out.at[3:11]))
                found.append((low.at[0:3, wide], out.at[0:3]))
                found.append((high.at[0:3, wide], out.at[11:14]))
                for h in range(2):
                    lanes, part = slice(128 * h, 128 * h + 128), slice(32 * h + w, 32 * h + w + 16)
                    found.append((coarse.at[:, narrow, lanes], out.at[edge_at(0, h) : edge_at(4, h)]))
                    found.append((low.at[3:5, part], out.at[edge_at(-2, h) : edge_at(0, h)]))
                    found.append((high.at[3:5, part], out.at[edge_at(4, h) : edge_at(6, h)]))
            return found

        exchanged(spots[0] == 1, moves, out_a, out_b, semaphores)

    @pl.when(spots[1] == 1)
    def _():
        side_by_side(lat_a, lat_b)

    @pl.when(spots[1] == 0)
    def _():
        side_by_side(lat_b, lat_a)


def spread_kernel(came, sent):
    order = permutation(128, block_row, False)
    block = dot(order, came[...].reshape(128, 128)).astype(BF16)
    sent[...] = jnp.broadcast_to(block[None], (32, 128, 128))


def cot_parts(cot, low, high, left, right, r):
    ref, k = (low, r + 3) if r < 0 else (cot, r) if r < 8 else (high, r - 8)
    return ref[k], left[r + 3], right[r + 3]


def coarse_parts(coarse, low, high, left, right, m, h):
    e = edge_at(m, h)
    if 0 <= m < 4:
        return coarse[m, :, 128 * h : 128 * h + 128], left[e], right[e]
    ref, k = (low, 5 + m) if m < 0 else (high, m - 1)
    return ref[k, 32 * h : 32 * h + 32], left[e], right[e]


def prepare(bounds, coarse, cot, low, high, left, right, up, fine3, cot3, grid, field):
    nearer = lax.broadcasted_iota(jnp.int32, (16, 128), 0) < 8

    def edge(a, b):
        return jnp.where(nearer, a.astype(F32), b.astype(F32))

    grid[0:48] = jnp.zeros((48, 256), BF16)
    grid[432:480] = jnp.zeros((48, 256), BF16)
    for m in range(-2, 6):
        at = (m + 3) * 48
        for h in range(2):
            lanes = slice(128 * h, 128 * h + 128)
            middle, before, after = coarse_parts(coarse, low, high, left, right, m, h)
            grid[at : at + 32, lanes] = middle
            grid[at + 32 : at + 48, lanes] = edge(after, before).astype(BF16)
    after = jnp.zeros((16, 128), BF16)
    for r in range(-3, 11):
        at = (r + 3) * PITCH
        middle, before, following = cot_parts(cot, low, high, left, right, r)
        field[at : at + 16] = edge(after, before)
        field[at + 16 : at + 80] = middle.astype(F32)
        after = following
    field[14 * PITCH :] = edge(after, jnp.zeros((16, 128), BF16))
    cot3[...] = shifted(field[...])

    ordered = dot(grid[...], permutation(256, spread_row, True)).astype(BF16)
    for r in range(-3, 12):
        j, parity = divmod(r, 2)
        block = dot(up[parity], ordered[(j + 2) * 48 : (j + 2) * 48 + 144])
        begin = (r + 3) * PITCH
        rows = min(PITCH, LENGTH - begin)
        keep = inside(bounds, begin, (rows, 256))
        for k in range(3):
            part = block[k * PITCH : k * PITCH + rows]
            fine3[begin : begin + rows, k * 256 : k * 256 + 256] = jnp.where(keep, part, 0.0).astype(BF16)


def plane_sum_kernel(came, sent):
    total = came[0].astype(F32)
    for k in range(1, 32):
        total = total + came[k].astype(F32)
    order = permutation(128, block_row, True)
    block = dot(order, total.astype(BF16)).astype(BF16).reshape(16, 8, 128)
    for k in range(2):
        sent[:, k] = block


def column_sum_kernel(came, total):
    part = came[0].astype(F32)
    for k in range(1, 16):
        part = part + came[k].astype(F32)
    total[...] = part


def final_kernel(core, mine, other, first, second, skip):
    low = core[0] == 0
    pieces = []
    for k in range(2):
        pieces += [jnp.where(low, mine[k], other[k]), jnp.where(low, other[k], mine[k])]
    total = jnp.concatenate(pieces, axis=0)
    for k in range(9):
        first[k] = total[2 * k : 2 * k + 2]
        second[k] = total[20 + k : 21 + k]
    skip[...] = total[18:20]


def first_block(weights, k):
    return weights[k // 4, :, k % 4].reshape(256, 128)


def main_kernel(
    bounds, spots, weights_far, coarse_far, cot_far, lat_a_far, lat_b_far, lon_a_far, lon_b_far, up_far,
    shares_far, second_far, fine_far, cot_kept, hidden_far, grad_far,
    weights, coarse, cot, lat_a, lat_b, lon_a, lon_b, up,
    low, high, left, right, shares, fine3, cot3, grid, field, second, hidden3, grad_act, semaphores,
):
    far = (weights_far, coarse_far, cot_far, lat_a_far, lat_b_far, lon_a_far, lon_b_far, up_far)
    here = (weights, coarse, cot, lat_a, lat_b, lon_a, lon_b, up)
    copies = copied(list(zip(far, here))[::-1], semaphores)
    kept = []

    def send(source, target):
        at = len(copies) + len(kept)
        kept.extend(copied([(source, target)], semaphores.at[at : at + 1]))

    def share_block(b, block):
        shares[b // 4, :, b % 4] = block.astype(BF16).reshape(8, 32, 128)
        send(shares.at[b // 4, :, b % 4], shares_far.at[b // 4, :, b % 4])

    pairs, pairs_t = permutation(256, pair_row, True), permutation(256, pair_row, False)
    same = identity()
    finish(copies[:-1])
    odd, second_core = spots[0] == 1, spots[1] == 1
    left[...] = either(odd, lon_a[...], lon_b[...])
    right[...] = either(odd, lon_b[...], lon_a[...])
    low[...] = either(second_core, lat_a[...], lat_b[...])
    high[...] = either(second_core, lat_b[...], lat_a[...])
    prepare(bounds, coarse, cot, low, high, left, right, up, fine3, cot3, grid, field)
    send(fine3.at[INNER[0] : INNER[1], 256:512], fine_far)
    send(cot3.at[MIDDLE[0] : MIDDLE[1], 128:256], cot_kept)
    flipped_cot = transposed(cells(cot3, INNER[0], slice(128, 256)))
    share = (dot(flipped_cot, cells(fine3, INNER[0], slice(256, 512))) * SCALE).astype(BF16)
    share_block(9, dot_nt(same, share))
    share_block(15, jnp.zeros((256, 128), F32))
    finish(copies[-1:])
    for k in range(5):
        block = dot(pairs, first_block(weights, 10 + k)).astype(BF16)
        second[2 * k] = block[:128]
        second[2 * k + 1] = block[128:]
    send(second, second_far)
    begin, end = WIDE
    count = end - begin
    act = jnp.zeros((count, 128), F32)
    for i in range(3):
        kernels = jnp.concatenate([first_block(weights, 3 * i + j) for j in range(3)], axis=0)
        at = begin + PITCH * (i - 1)
        act = act + dot(fine3[at : at + count, :], kernels)
    keep = inside(bounds, begin, (count, 128))
    sigma = jax.nn.sigmoid(act)
    hidden = jnp.where(keep, act * sigma, 0.0)
    hidden3[...] = shifted(hidden)[HIDDEN[0] - begin : HIDDEN[1] - begin]
    send(hidden3, hidden_far)
    grad_hidden = jnp.zeros((count, 128), F32)
    for i in range(3):
        kernels = jnp.concatenate([second[3 * i + 2 - j] for j in range(3)], axis=1)
        at = begin - PITCH * (i - 1)
        grad_hidden = grad_hidden + dot_nt(cot3[at : at + count, :], kernels)
    grad = grad_hidden * sigma * (1.0 + act * (1.0 - sigma))
    grad_act[...] = jnp.where(keep, grad, 0.0).astype(BF16)
    send(grad_act, grad_far)

    found = []
    for i in range(3):
        share = dot(flipped_cot, cells(hidden3, INNER[0] + PITCH * (i - 1) - HIDDEN[0]))
        share = (share * SCALE).astype(BF16)
        found += [share[:, j * 128 : j * 128 + 128] for j in range(3)]
    found.append(jnp.zeros((128, 128), BF16))
    for k in range(5):
        both = jnp.concatenate(found[2 * k : 2 * k + 2], axis=1)
        share_block(10 + k, dot_nt(pairs_t, both))
    flipped_grad = transposed(cells(grad_act, INNER[0] - begin))
    for i in range(3):
        share = dot(flipped_grad, cells(fine3, INNER[0] + PITCH * (i - 1)))
        share = (share * SCALE).astype(BF16)
        for j in range(3):
            share_block(3 * i + j, dot_nt(same, share[:, j * 256 : j * 256 + 256]))
    finish(kept)


def field_kernel(
    bounds, weights, second, fine, cot, hidden3, grad_act, down, result, coarse_gradient
):
    skip = first_block(weights, 9)
    begin, end = INNER
    total = dot(fine[...], skip)
    for i in range(3):
        kernels = jnp.concatenate([second[3 * i + j] for j in range(3)], axis=0)
        at = begin + PITCH * (i - 1) - HIDDEN[0]
        total = total + dot(hidden3[at : at + end - begin, :], kernels)
    total = total.astype(BF16)
    for r in range(8):
        result[r] = total[r * PITCH : r * PITCH + 64]

    grad3 = shifted(grad_act[...].astype(F32))
    begin, end = MIDDLE
    count = end - begin
    back = dot_nt(cot[...], skip)
    for i in range(3):
        kernels = jnp.concatenate([first_block(weights, 3 * i + 2 - j) for j in range(3)], axis=1)
        at = begin - PITCH * (i - 1) - WIDE[0]
        back = back + dot_nt(grad3[at : at + count], kernels)
    fine_gradient = jnp.where(inside(bounds, begin, (count, 256)), back, 0.0).astype(BF16)
    spread_t = permutation(256, spread_row, False)
    for j in range(4):
        part = dot(down[...], fine_gradient[2 * j * PITCH : 2 * j * PITCH + 4 * PITCH + 16])
        coarse_gradient[j] = dot(part.astype(BF16), spread_t).astype(BF16)


def call(kernel, outs, *operands, spaces="", scratch=(), semaphores=0, dtype=BF16, vmem=16):
    kinds = dict(s=pltpu.SMEM, h=pltpu.HBM, v=pltpu.VMEM)
    specs = [pl.BlockSpec(memory_space=kinds[k]) for k in spaces]
    return pl.pallas_call(
        kernel,
        out_shape=[jax.ShapeDtypeStruct(shape, dtype) for shape in outs],
        in_specs=specs[: len(operands)],
        out_specs=specs[len(operands) :],
        scratch_shapes=[pltpu.VMEM(*s) for s in scratch]
        + ([pltpu.SemaphoreType.DMA((semaphores,))] if semaphores else []),
        compiler_params=pltpu.CompilerParams(vmem_limit_bytes=vmem * 1024 * 1024),
    )(*operands)


def pairwise(first, second, axis, periodic):
    count = lax.axis_size(axis)
    ends = [(i, (i + 1) % count) for i in range(count if periodic else count - 1)]
    steps = [[(a, b), (b, a)] for a, b in ends]
    return (
        lax.ppermute(first, axis, [p for step in steps[0::2] for p in step]),
        lax.ppermute(second, axis, [p for step in steps[1::2] for p in step]),
    )


def on_device(coarse, w_first, w_second, w_skip, cotangent):
    up, down = jnp.asarray(upsampling_matrices(), BF16), jnp.asarray(decimation_matrix(), BF16)
    lat = lax.axis_index(LAT).astype(jnp.int32)
    bounds = jnp.stack([jnp.where(lat == 0, 248, 0), jnp.where(lat == 3, 888, LENGTH)]).astype(jnp.int32)

    spots = jnp.stack([lax.axis_index("y") % 2, lax.axis_index("core")]).astype(jnp.int32)
    (sent,) = call(
        pack_kernel, [(16, 8, 128)], lat[None], w_first, w_second.reshape(9, 128), w_skip,
        spaces="shhhv", vmem=60,
        scratch=[((32, 128), F32), ((9, 2, 128), BF16), ((9, 128), BF16), ((2, 128), BF16)],
        semaphores=3,
    )
    came = lax.all_to_all(sent, "z", 0, 0, tiled=True)
    edges = call(
        lat_edge_kernel, [(5, 64, 128)] * 2, spots, coarse, cotangent,
        spaces="shhvv", semaphores=6, vmem=60,
    )
    lat_a, lat_b = pairwise(*edges, LAT, False)
    came, lat_a, lat_b = lax.optimization_barrier((came, lat_a, lat_b))
    (sent,) = call(spread_kernel, [(32, 128, 128)], came, spaces="vv")
    sent, lat_a, lat_b = lax.optimization_barrier((sent, lat_a, lat_b))
    weights = lax.all_to_all(sent, PLANE, 0, 0, tiled=True).reshape(4, 8, 4, 32, 128)
    edges = call(
        lon_edge_kernel, [(30, 16, 128)] * 2, spots, coarse, cotangent, lat_a, lat_b,
        spaces="shhhhvv", semaphores=18, vmem=60,
    )
    lon_a, lon_b = pairwise(*edges, LON, True)
    blocks = (4, 8, 4, 32, 128)
    kept = [
        (10, 128, 128), (INNER[1] - INNER[0], 256), (MIDDLE[1] - MIDDLE[0], 128),
        (HIDDEN[1] - HIDDEN[0], 384), (WIDE[1] - WIDE[0], 128),
    ]
    shares, second, fine, cot_kept, hidden3, grad_act = call(
        main_kernel, [blocks] + kept,
        bounds, spots, weights, coarse, cotangent, lat_a, lat_b, lon_a, lon_b, up,
        spaces="sshhhhhhhh" + "hhhhhh",
        scratch=[
            (shape, BF16)
            for shape in [
                blocks, (4, 32, 256), (8, 64, 128), (5, 64, 128), (5, 64, 128), (30, 16, 128), (30, 16, 128),
                (2, 240, 144), (5, 64, 128), (5, 64, 128), (30, 16, 128), (30, 16, 128), blocks, (LENGTH, 768), (LENGTH, 384), (480, 256),
            ]
        ]
        + [((LENGTH, 128), F32)]
        + [(shape, BF16) for shape in (kept[0], kept[3], kept[4])],
        semaphores=8 + 5 + 16,
        vmem=60,
    )
    came = lax.all_to_all(shares.reshape(32, 128, 128), PLANE, 0, 0, tiled=True)
    (sent,) = call(plane_sum_kernel, [(16, 2, 8, 128)], came, spaces="vv")
    came = lax.all_to_all(sent.reshape(32, 8, 128), ("z", "xl"), 0, 0, tiled=True)
    result, coarse_gradient = call(
        field_kernel, [(8, 64, 128), (4, 32, 256)],
        bounds, weights, second, fine, cot_kept, hidden3, grad_act, down,
        spaces="svvvvvvvvv",
    )
    came, result, coarse_gradient = lax.optimization_barrier((came, result, coarse_gradient))
    (mine,) = call(column_sum_kernel, [(2, 8, 128)], came.reshape(16, 2, 8, 128), spaces="vv", dtype=F32)
    other = lax.ppermute(mine, "core", [(0, 1), (1, 0)])
    grads = call(
        final_kernel, [(9, 2, 128), (9, 1, 128), (2, 128)],
        lax.axis_index("core").astype(jnp.int32)[None], mine, other,
        spaces="svvvvv", dtype=F32,
    )
    return result, coarse_gradient, *grads


def solution(mesh):
    axes = ("xl", "core", "z", "xh", "y")
    fine = Mesh(mesh.devices.reshape(2, 2, 16, 2, 4), axes)
    field, taps, plain = P(LAT, LON, None), P(None, LON, None), P(LON, None)
    return jax.shard_map(
        on_device,
        mesh=fine,
        in_specs=(field, taps, taps, plain, field),
        out_specs=(field, field, taps, taps, plain),
        check_vma=False,
    )
```

time: 141 us -> 120 us (0.85)
  local copies, waits for them, and re-layouts: 17.6 us -> 1.66 us
  starting transfers between devices: 68 us -> 55.7 us
  Pallas kernels: 10.2 us -> 20.8 us
  other arithmetic: 3.99 us -> 1.18 us
    ppermute x8 -> x5, starting transfers between devices: 35.6 us -> 20.9 us  [the longest x2 10.1 us: pairwise(): lax.ppermute(second, axis, [p for step in steps[1::2] for p in step])]
    pallas_call x3 -> x9, Pallas kernels: 10.2 us -> 20.8 us  [call(): pl.pallas_call(kernel, out_shape=[jax.ShapeDtypeStruct(shape, dtype) for...]
    unnamed x38 -> x26, local copies, waits for them, and re-layouts: 10.5 us -> 1.66 us
    reduce_sum x2 -> x0, other arithmetic: 2.96 us -> none  [the longest x1 2.01 us: summed(): part = jnp.sum(came.astype(F32), axis=0).astype(BF16)]
    broadcast_in_dim x5 -> x0, local copies, waits for them, and re-layouts: 2.57 us -> none  [the longest x1 1.22 us: gathered(): sent = jnp.broadcast_to(block[None], (32, 4, 32, 128))]
    all_to_all x3, starting transfers between devices: 32.4 us -> 34.9 us  [the longest x1 15.8 us: on_device(): came = lax.all_to_all(sent, 'z', 0, 0, tiled=True)]
    slice x7 -> x0, local copies, waits for them, and re-layouts: 2.27 us -> none  [the longest x1 0.83 us: cot_field(): low, high = neighbours(cotangent[:3], cotangent[-3:], LAT, False)]
    ppermute x8 -> x5, waiting for transfers between devices: 8.11 us -> 8.54 us  [the longest x2 4.54 us: pairwise(): lax.ppermute(second, axis, [p for step in steps[1::2] for p in step])]
  transfers between devices with their start and end apart: 11 -> 8, of which waited for: 2 -> 5; matrix products, arithmetic and copies ran while one was open for 3% -> 1% of each run, Pallas kernels for 4% -> 7%
where the time goes in v2:
time: 120 us
  starting transfers between devices  55.7 us (46%)
  blocking collectives  22.4 us (19%)
  Pallas kernels  20.8 us (17%)
  waiting for transfers between devices  17 us (14%)
  local copies, waits for them, and re-layouts  1.66 us (1%)
    all_to_all x1, blocking collectives, on_device(): came = lax.all_to_all(shares.reshape(32, 128, 128), PLANE, 0, 0, tiled=True)  22.4 us
    pallas_call x9, Pallas kernels, call(): pl.pallas_call(kernel, out_shape=[jax.ShapeDtypeStruct(shape, dtype) for...  20.8 us
    all_to_all x1, starting transfers between devices, on_device(): came = lax.all_to_all(sent, 'z', 0, 0, tiled=True)  15.8 us
    all_to_all x1, starting transfers between devices, on_device(): lax.all_to_all(sent.reshape(32, 8, 128), ('z', 'xl'), 0, 0, tiled=True)  10.5 us
    ppermute x2, starting transfers between devices, pairwise(): lax.ppermute(second, axis, [p for step in steps[1::2] for p in step])  10.1 us
    all_to_all x1, starting transfers between devices, on_device(): lax.all_to_all(sent, PLANE, 0, 0, tiled=True).reshape(4, 8, 4, 32, 128)  8.59 us
    all_to_all x1, waiting for transfers between devices, on_device(): lax.all_to_all(sent.reshape(32, 8, 128), ('z', 'xl'), 0, 0, tiled=True)  8.46 us
    ppermute x2, starting transfers between devices, pairwise(): lax.ppermute(first, axis, [p for step in steps[0::2] for p in step])  6.13 us
  transfers between devices with their start and end apart: 8, of which 5 were waited for; matrix products, arithmetic and copies ran while one was open for 1% of the time, Pallas kernels for 7%

profile of v2, /device:TPU:1, one launch (start us, length us, event | category | flops | bytes accessed | tf_op | source)
XLA Modules:
  0.0 119.6 jit_solution(12614587635205548269)
XLA Ops:
  0.6 1.4 %shard_map.110 = bf16[16,8,128]{2,1,0:T(8,128)(2,1)} custom-call(s32[1]{0:T(128)} %bitcast.4.lat, bf16[9,2,128]{2,1,0:T(2,128)(2,1)} %first.1, bf16[9,128]{1,0:T(8,128)(2,1)} %bitcast.14, bf16[2,128]{1,0:T(2,128)(2,1)} %skip.1), custom_call_target="tpu_custom_call" | custom-call | tf_op jit(solution)/shard_map/pallas_call | solution.py:390
  2.0 15.8 %all-to-all-start = ((bf16[16,8,128]{2,1,0:T(8,128)(2,1)}), bf16[16,8,128]{2,1,0:T(8,128)(2,1)S(1)}, u32[]{:S(2)}, u32[]{:S(2)}) async-start(bf16[16,8,128]{2,1,0:T(8,128)(2,1)} %shard_map.110), calls=%async_computation | async-start | bytes 65536 | tf_op jit(solution)/shard_map/all_to_all | solution.py:423
  17.8 0.6 pad_add_fusion.1.spots
  18.4 2.2 %shard_map.111 = (bf16[5,64,128]{2,1,0:T(8,128)(2,1)}, bf16[5,64,128]{2,1,0:T(8,128)(2,1)}) custom-call(s32[2]{0:T(128)} %pad_add_fusion.1.spots, bf16[4,32,256]{2,1,0:T(8,128)(2,1)} %coarse_far.1, bf16[8,64,128]{2,1,0:T(8,128)(2,1)} %cot_far.1), custom_call_target="tpu_custom_call" | custom-call | tf_op jit(solution)/shard_map/pallas_call | solution.py:390
  20.6 2.9 %collective-permute-start = (bf16[5,64,128]{2,1,0:T(8,128)(2,1)}, bf16[5,64,128]{2,1,0:T(8,128)(2,1)S(1)}, u32[]{:S(2)}, u32[]{:S(2)}) collective-permute-start(bf16[5,64,128]{2,1,0:T(8,128)(2,1)} %get-tuple-element.29), channel_id=1, source_target_pairs={{0,128},{128,0},{256,384},{384,256},{1,129},{129,1},{257,385},{385... | collective-permute-start | bytes 245768 | tf_op jit(solution)/shard_map/ppermute | solution.py:406
  23.5 3.0 %collective-permute-start.1 = (bf16[5,64,128]{2,1,0:T(8,128)(2,1)}, bf16[5,64,128]{2,1,0:T(8,128)(2,1)S(1)}, u32[]{:S(2)}, u32[]{:S(2)}) collective-permute-start(bf16[5,64,128]{2,1,0:T(8,128)(2,1)} %get-tuple-element.30), channel_id=1, source_target_pairs={{128,256},{256,128},{129,257},{257,129},{130,258},{258,130},{131,2... | collective-permute-start | bytes 245768 | tf_op jit(solution)/shard_map/ppermute | solution.py:407
  26.5 0.0 collective-permute-done.lat_a.lat_a_far
  26.6 0.0 copy-start.9
  26.6 3.2 %collective-permute-done.1.lat_b.lat_b_far = bf16[5,64,128]{2,1,0:T(8,128)(2,1)S(1)} collective-permute-done((bf16[5,64,128]{2,1,0:T(8,128)(2,1)}, bf16[5,64,128]{2,1,0:T(8,128)(2,1)S(1)}, u32[]{:S(2)}, u32[]{:S(2)}) %collective-permute-start.1) | collective-permute-done | bytes 81952 | tf_op jit(solution)/shard_map/ppermute | solution.py:407
  29.8 0.0 all-to-all-done.came
  29.8 1.3 %shard_map.112 = bf16[32,128,128]{2,1,0:T(8,128)(2,1)} custom-call(bf16[16,8,128]{2,1,0:T(8,128)(2,1)S(1)} %all-to-all-done.came), custom_call_target="tpu_custom_call" | custom-call | tf_op jit(solution)/shard_map/pallas_call | solution.py:390
  31.1 8.6 %all-to-all-start.1 = ((bf16[32,128,128]{2,1,0:T(8,128)(2,1)}), bf16[32,128,128]{2,1,0:T(8,128)(2,1)S(1)}, u32[]{:S(2)}, u32[]{:S(2)}) async-start(bf16[32,128,128]{2,1,0:T(8,128)(2,1)} %shard_map.112), calls=%async_computation.1 | async-start | bytes 2097152 | tf_op jit(solution)/shard_map/all_to_all | solution.py:432
  39.7 2.5 %shard_map.113 = (bf16[30,16,128]{2,1,0:T(8,128)(2,1)}, bf16[30,16,128]{2,1,0:T(8,128)(2,1)}) custom-call(s32[2]{0:T(128)} %pad_add_fusion.1.spots, bf16[4,32,256]{2,1,0:T(8,128)(2,1)} %coarse_far.1, bf16[8,64,128]{2,1,0:T(8,128)(2,1)} %cot_far.1, bf16[5,64,128]{2,1,0:T(8,128)(2,1)} %copy-done.9, bf16[5,64,128]{2,1,0:T(8,128)(2,1)} %copy-done.10), custom_call_target="tpu_custom_call" | custom-call | tf_op jit(solution)/shard_map/pallas_call | solution.py:390
  42.2 3.2 %collective-permute-start.2 = (bf16[30,16,128]{2,1,0:T(8,128)(2,1)}, bf16[30,16,128]{2,1,0:T(8,128)(2,1)S(1)}, u32[]{:S(2)}, u32[]{:S(2)}) collective-permute-start(bf16[30,16,128]{2,1,0:T(8,128)(2,1)} %get-tuple-element.37), channel_id=1, source_target_pairs={{0,1},{1,0},{2,3},{3,2},{4,5},{5,4},{6,7},{7,6},{8,9},{9,8},{10,11... | collective-permute-start | bytes 368648 | tf_op jit(solution)/shard_map/ppermute | solution.py:406
  45.4 7.0 %collective-permute-start.3 = (bf16[30,16,128]{2,1,0:T(8,128)(2,1)}, bf16[30,16,128]{2,1,0:T(8,128)(2,1)S(1)}, u32[]{:S(2)}, u32[]{:S(2)}) collective-permute-start(bf16[30,16,128]{2,1,0:T(8,128)(2,1)} %get-tuple-element.38), channel_id=1, source_target_pairs={{1,2},{2,1},{3,4},{4,3},{5,6},{6,5},{7,8},{8,7},{9,10},{10,9},{11,... | collective-permute-start | bytes 368648 | tf_op jit(solution)/shard_map/ppermute | solution.py:407
  52.5 0.6 pad_add_fusion.bounds
  53.0 3.2 %collective-permute-done.2.lon_a_far = bf16[30,16,128]{2,1,0:T(8,128)(2,1)S(1)} collective-permute-done((bf16[30,16,128]{2,1,0:T(8,128)(2,1)}, bf16[30,16,128]{2,1,0:T(8,128)(2,1)S(1)}, u32[]{:S(2)}, u32[]{:S(2)}) %collective-permute-start.2) | collective-permute-done | bytes 122912 | tf_op jit(solution)/shard_map/ppermute | solution.py:406
  56.2 1.3 %collective-permute-done.3.lon_b_far = bf16[30,16,128]{2,1,0:T(8,128)(2,1)S(1)} collective-permute-done((bf16[30,16,128]{2,1,0:T(8,128)(2,1)}, bf16[30,16,128]{2,1,0:T(8,128)(2,1)S(1)}, u32[]{:S(2)}, u32[]{:S(2)}) %collective-permute-start.3) | collective-permute-done | bytes 122912 | tf_op jit(solution)/shard_map/ppermute | solution.py:407
  57.6 0.0 all-to-all-done.1
  57.6 0.6 copy-done.12
  58.2 0.4 copy-done
  58.6 8.5 %shard_map.114 = (bf16[4,8,4,32,128]{4,3,2,1,0:T(8,128)(2,1)}, bf16[10,128,128]{2,1,0:T(8,128)(2,1)}, bf16[624,256]{1,0:T(8,128)(2,1)}, bf16[816,128]{1,0:T(8,12...) custom-call(s32[2]{0:T(128)} %pad_add_fusion.bounds, s32[2]{0:T(128)} %pad_add_fusion.1.spots, ...), custom_call_target="tpu_custom_call" | custom-call | tf_op jit(solution)/shard_map/pallas_call | solution.py:390
  67.2 22.4 %all_to_all.20.came = bf16[32,128,128]{2,1,0:T(8,128)(2,1)S(1)} all-to-all(bf16[32,128,128]{2,1,0:T(8,128)(2,1)} %bitcast.13), channel_id=1, replica_groups=mesh['xl'=2,'core'=2,'z'=16,'xh'=2,'y'=4] {'xl','core','xh','y'}, dimensions={0} | all-to-all | bytes 2097152 | tf_op jit(solution)/shard_map/all_to_all | solution.py:459
  89.5 0.9 shard_map.115
  90.4 10.5 %all-to-all-start.3 = ((bf16[32,8,128]{2,1,0:T(8,128)(2,1)}), bf16[32,8,128]{2,1,0:T(8,128)(2,1)S(1)}, u32[]{:S(2)}, u32[]{:S(2)}) async-start(bf16[32,8,128]{2,1,0:T(8,128)(2,1)} %bitcast.8), calls=%async_computation.3 | async-start | bytes 131072 | tf_op jit(solution)/shard_map/all_to_all | solution.py:461
  100.9 0.0 copy-start.8
  101.0 0.6 copy-done.8
  101.6 3.4 %shard_map.116 = (bf16[8,64,128]{2,1,0:T(8,128)(2,1)}, bf16[4,32,256]{2,1,0:T(8,128)(2,1)}) custom-call(s32[2]{0:T(128)S(1)} %copy-done.8, bf16[4,8,4,32,128]{4,3,2,1,0:T(8,128)(2,1)S(1)} %bitcast.11, bf16[10,128,128]{2,1,0:T(8,128)(2,1)S(1)} %copy-done.3, bf16[624,256]{1,0:T(8,128)(2,1)S(1)} %copy-done.4, bf16[816,128]{1,0:T(8,128)(2,1)S(1)} %copy-done.6, ...), custom_call_target="tpu_custom_call" | custom-call | tf_op jit(solution)/shard_map/pallas_call | solution.py:390
  105.0 8.5 %all-to-all-done.3 = bf16[32,8,128]{2,1,0:T(8,128)(2,1)S(1)} async-done(((bf16[32,8,128]{2,1,0:T(8,128)(2,1)}), bf16[32,8,128]{2,1,0:T(8,128)(2,1)S(1)}, u32[]{:S(2)}, u32[]{:S(2)}) %all-to-all-start.3) | async-done | bytes 65568 | tf_op jit(solution)/shard_map/all_to_all | solution.py:461
  113.5 4.7 %collective-permute-start.4 = (f32[2,8,128]{2,1,0:T(8,128)S(1)}, f32[2,8,128]{2,1,0:T(8,128)S(1)}, u32[]{:S(2)}, u32[]{:S(2)}) collective-permute-start(f32[2,8,128]{2,1,0:T(8,128)S(1)} %shard_map.117.mine), channel_id=1, source_target_pairs={{0,128},{128,0},{1,129},{129,1},{2,130},{130,2},{3,131},{131,3},{4... | collective-permute-start | bytes 24584 | tf_op jit(solution)/shard_map/ppermute | solution.py:469
  118.2 0.8 collective-permute-done.4.other
  119.0 0.6 shard_map.118
  (22 shorter events, 0.1 us)
Async XLA Ops:
  2.0 27.8 %all-to-all-start = ((bf16[16,8,128]{2,1,0:T(8,128)(2,1)}), bf16[16,8,128]{2,1,0:T(8,128)(2,1)S(1)}, u32[]{:S(2)}, u32[]{:S(2)}) async-start(bf16[16,8,128]{2,1,0:T(8,128)(2,1)} %shard_map.110), calls=%async_computation | async-start | bytes 65536 | tf_op jit(solution)/shard_map/all_to_all | solution.py:423
  20.6 5.9 %collective-permute-start = (bf16[5,64,128]{2,1,0:T(8,128)(2,1)}, bf16[5,64,128]{2,1,0:T(8,128)(2,1)S(1)}, u32[]{:S(2)}, u32[]{:S(2)}) collective-permute-start(bf16[5,64,128]{2,1,0:T(8,128)(2,1)} %get-tuple-element.29), channel_id=1, source_target_pairs={{0,128},{128,0},{256,384},{384,256},{1,129},{129,1},{257,385},{385... | collective-permute-start | bytes 245768 | tf_op jit(solution)/shard_map/ppermute | solution.py:406
  23.5 6.3 %collective-permute-start.1 = (bf16[5,64,128]{2,1,0:T(8,128)(2,1)}, bf16[5,64,128]{2,1,0:T(8,128)(2,1)S(1)}, u32[]{:S(2)}, u32[]{:S(2)}) collective-permute-start(bf16[5,64,128]{2,1,0:T(8,128)(2,1)} %get-tuple-element.30), channel_id=1, source_target_pairs={{128,256},{256,128},{129,257},{257,129},{130,258},{258,130},{131,2... | collective-permute-start | bytes 245768 | tf_op jit(solution)/shard_map/ppermute | solution.py:407
  26.6 4.5 %copy-start.9 = (bf16[5,64,128]{2,1,0:T(8,128)(2,1)}, bf16[5,64,128]{2,1,0:T(8,128)(2,1)S(1)}, u32[]{:S(2)}) copy-start(bf16[5,64,128]{2,1,0:T(8,128)(2,1)S(1)} %collective-permute-done.lat_a.lat_a_far) | copy-start | bytes 245764
  29.8 1.3 %copy-start.10 = (bf16[5,64,128]{2,1,0:T(8,128)(2,1)}, bf16[5,64,128]{2,1,0:T(8,128)(2,1)S(1)}, u32[]{:S(2)}) copy-start(bf16[5,64,128]{2,1,0:T(8,128)(2,1)S(1)} %collective-permute-done.1.lat_b.lat_b_far) | copy-start | bytes 245764
  31.1 26.5 %all-to-all-start.1 = ((bf16[32,128,128]{2,1,0:T(8,128)(2,1)}), bf16[32,128,128]{2,1,0:T(8,128)(2,1)S(1)}, u32[]{:S(2)}, u32[]{:S(2)}) async-start(bf16[32,128,128]{2,1,0:T(8,128)(2,1)} %shard_map.112), calls=%async_computation.1 | async-start | bytes 2097152 | tf_op jit(solution)/shard_map/all_to_all | solution.py:432
  42.2 14.1 %collective-permute-start.2 = (bf16[30,16,128]{2,1,0:T(8,128)(2,1)}, bf16[30,16,128]{2,1,0:T(8,128)(2,1)S(1)}, u32[]{:S(2)}, u32[]{:S(2)}) collective-permute-start(bf16[30,16,128]{2,1,0:T(8,128)(2,1)} %get-tuple-element.37), channel_id=1, source_target_pairs={{0,1},{1,0},{2,3},{3,2},{4,5},{5,4},{6,7},{7,6},{8,9},{9,8},{10,11... | collective-permute-start | bytes 368648 | tf_op jit(solution)/shard_map/ppermute | solution.py:406
  45.4 12.2 %collective-permute-start.3 = (bf16[30,16,128]{2,1,0:T(8,128)(2,1)}, bf16[30,16,128]{2,1,0:T(8,128)(2,1)S(1)}, u32[]{:S(2)}, u32[]{:S(2)}) collective-permute-start(bf16[30,16,128]{2,1,0:T(8,128)(2,1)} %get-tuple-element.38), channel_id=1, source_target_pairs={{1,2},{2,1},{3,4},{4,3},{5,6},{6,5},{7,8},{8,7},{9,10},{10,9},{11,... | collective-permute-start | bytes 368648 | tf_op jit(solution)/shard_map/ppermute | solution.py:407
  56.2 1.3 %copy-start.11 = (bf16[30,16,128]{2,1,0:T(8,128)(2,1)}, bf16[30,16,128]{2,1,0:T(8,128)(2,1)S(1)}, u32[]{:S(2)}) copy-start(bf16[30,16,128]{2,1,0:T(8,128)(2,1)S(1)} %collective-permute-done.2.lon_a_far) | copy-start | bytes 368644
  57.6 0.6 copy-start.12
  57.6 1.0 copy-start
  67.1 33.8 %copy-start.2 = (bf16[784,384]{1,0:T(8,128)(2,1)S(1)}, bf16[784,384]{1,0:T(8,128)(2,1)}, u32[]{:S(2)}) copy-start(bf16[784,384]{1,0:T(8,128)(2,1)} %get-tuple-element.43.hidden3) | copy-start | bytes 1806340
  67.1 33.8 %copy-start.3 = (bf16[10,128,128]{2,1,0:T(8,128)(2,1)S(1)}, bf16[10,128,128]{2,1,0:T(8,128)(2,1)}, u32[]{:S(2)}) copy-start(bf16[10,128,128]{2,1,0:T(8,128)(2,1)} %get-tuple-element.40.second) | copy-start | bytes 983044
  67.1 33.8 %copy-start.4 = (bf16[624,256]{1,0:T(8,128)(2,1)S(1)}, bf16[624,256]{1,0:T(8,128)(2,1)}, u32[]{:S(2)}) copy-start(bf16[624,256]{1,0:T(8,128)(2,1)} %get-tuple-element.41.fine) | copy-start | bytes 958468
  67.1 33.8 %copy-start.5 = (bf16[976,128]{1,0:T(8,128)(2,1)S(1)}, bf16[976,128]{1,0:T(8,128)(2,1)}, u32[]{:S(2)}) copy-start(bf16[976,128]{1,0:T(8,128)(2,1)} %get-tuple-element.44.grad_act) | copy-start | bytes 749572
  67.1 33.8 %copy-start.6 = (bf16[816,128]{1,0:T(8,128)(2,1)S(1)}, bf16[816,128]{1,0:T(8,128)(2,1)}, u32[]{:S(2)}) copy-start(bf16[816,128]{1,0:T(8,128)(2,1)} %get-tuple-element.42.cot) | copy-start | bytes 626692
  89.5 11.5 %copy-start.1 = (bf16[32,128,128]{2,1,0:T(8,128)(2,1)S(1)}, bf16[32,128,128]{2,1,0:T(8,128)(2,1)}, u32[]{:S(2)}) copy-start(bf16[32,128,128]{2,1,0:T(8,128)(2,1)} %copy-done) | copy-start | bytes 3145732
  90.4 10.6 %copy-start.7 = (bf16[32,336]{1,0:T(8,128)(2,1)S(1)}, bf16[32,336]{1,0:T(8,128)(2,1)}, u32[]{:S(2)}) copy-start(bf16[32,336]{1,0:T(8,128)(2,1)} %constant.41.clone.down) | copy-start | bytes 64516
  90.4 23.1 %all-to-all-start.3 = ((bf16[32,8,128]{2,1,0:T(8,128)(2,1)}), bf16[32,8,128]{2,1,0:T(8,128)(2,1)S(1)}, u32[]{:S(2)}, u32[]{:S(2)}) async-start(bf16[32,8,128]{2,1,0:T(8,128)(2,1)} %bitcast.8), calls=%async_computation.3 | async-start | bytes 131072 | tf_op jit(solution)/shard_map/all_to_all | solution.py:461
  100.9 0.7 copy-start.8
  113.5 5.5 %collective-permute-start.4 = (f32[2,8,128]{2,1,0:T(8,128)S(1)}, f32[2,8,128]{2,1,0:T(8,128)S(1)}, u32[]{:S(2)}, u32[]{:S(2)}) collective-permute-start(f32[2,8,128]{2,1,0:T(8,128)S(1)} %shard_map.117.mine), channel_id=1, source_target_pairs={{0,128},{128,0},{1,129},{129,1},{2,130},{130,2},{3,131},{131,3},{4... | collective-permute-start | bytes 24584 | tf_op jit(solution)/shard_map/ppermute | solution.py:469

commit v3 on v2

v3 whole, which is shorter than its diff:
```python
import jax
import jax.numpy as jnp
import numpy as np
from jax import lax
from jax.experimental import pallas as pl
from jax.experimental.pallas import tpu as pltpu
from jax.sharding import Mesh, PartitionSpec as P

PITCH = 80
LENGTH = 14 * PITCH + 16
WIDE = (PITCH, 12 * PITCH + 96)
MIDDLE = (2 * PITCH, 12 * PITCH + 16)
HIDDEN = (2 * PITCH + 16, 12 * PITCH)
INNER = (256, 880)
F32 = jnp.float32
BF16 = jnp.bfloat16
SCALE = 1.0 / 512.0
LAT = ("xl", "core")
LON = ("z", "xh", "y")
PLANE = ("xl", "core", "xh", "y")


def upsampling_matrices():
    taps = {}
    for parity in range(2):
        for dc in (-1, 0, 1):
            for u in range(PITCH):
                row, col = (parity - 1, 64 + u + dc) if u < 8 else (parity, u - 16 + dc)
                if not -3 <= col <= 66:
                    continue
                for wr, m in ((0.75, row // 2), (0.25, row // 2 + (1 if row % 2 else -1))):
                    for wc, n in ((0.75, col // 2), (0.25, col // 2 + (1 if col % 2 else -1))):
                        taps[parity, (dc + 1) * PITCH + u, (m + 1) * 48 + n % 48] = wr * wc
    out = np.zeros((2, 3 * PITCH, 144), np.float32)
    for place, weight in taps.items():
        out[place] = weight
    return out


def decimation_matrix():
    out = np.zeros((32, 4 * PITCH + 16), np.float32)
    weights = (0.25, 0.75, 0.75, 0.25)
    for j in range(32):
        for a in range(4):
            for b in range(4):
                out[j, a * PITCH + 16 + 2 * j - 1 + b] = weights[a] * weights[b]
    return out


def spread_row(column):
    return ((column >> 1) & 15) * 16 + (column >> 5) * 2 + (column & 1)


def pair_row(column):
    return (column & 1) * 128 + ((column >> 1) & 15) * 8 + (column >> 5)


def block_row(row):
    return ((row >> 1) & 15) * 8 + (row >> 5) * 2 + (row & 1)


def permutation(size, place, by_column):
    rows = lax.broadcasted_iota(jnp.int32, (size, size), 0)
    columns = lax.broadcasted_iota(jnp.int32, (size, size), 1)
    same = rows == place(columns) if by_column else columns == place(rows)
    return jnp.where(same, 1.0, 0.0).astype(BF16)


def lat_place():
    return lax.axis_index("xl") * 2 + lax.axis_index("core")


def in_odd_column():
    return lax.rem(lax.axis_index("y"), 2) == 1


def in_second_core():
    return lax.axis_index("core") == 1


def dot(a, b):
    return lax.dot_general(a, b, (((1,), (0,)), ((), ())), preferred_element_type=F32)


def dot_nt(a, b):
    return lax.dot_general(a, b, (((1,), (1,)), ((), ())), preferred_element_type=F32)


def inside(begin, shape):
    lat = lat_place()
    low, high = jnp.where(lat == 0, 248, 0), jnp.where(lat == 3, 888, LENGTH)
    place = lax.broadcasted_iota(jnp.int32, shape, 0) + begin
    return (place >= low) & (place < high)


def shifted(field):
    count = field.shape[0]
    return jnp.concatenate(
        [
            pltpu.roll(field, 1, 0).astype(BF16),
            field.astype(BF16),
            pltpu.roll(field, count - 1, 0).astype(BF16),
        ],
        axis=1,
    )


def cells(ref, begin, lanes=slice(None)):
    return jnp.concatenate(
        [ref[begin + PITCH * r : begin + PITCH * r + 64, lanes] for r in range(8)], axis=0
    )


def transposed(field):
    return field.astype(F32).T.astype(BF16)


def identity():
    return permutation(256, lambda row: row, True)


def copied(pairs, semaphores):
    copies = [pltpu.make_async_copy(a, b, semaphores.at[i]) for i, (a, b) in enumerate(pairs)]
    for copy in copies:
        copy.start()
    return copies


def finish(copies):
    for copy in copies:
        copy.wait()


def either(flag, a, b):
    return jnp.where(flag, a.astype(F32), b.astype(F32)).astype(BF16)


def exchanged(swap, moves, out_a, out_b, semaphores):
    @pl.when(swap)
    def _():
        finish(copied(moves(out_b, out_a), semaphores))

    @pl.when(jnp.logical_not(swap))
    def _():
        finish(copied(moves(out_a, out_b), semaphores))


def front_kernel(
    first, second, skip, coarse, cot, sent, out_a, out_b, rows, first_here, second_here, skip_here, semaphores
):
    def moves(up, down):
        found = []
        for out, r, m in ((up, 5, 2), (down, 0, 0)):
            found.append((cot.at[r : r + 3], out.at[0:3]))
            for h in range(2):
                lanes = slice(128 * h, 128 * h + 128)
                found.append((coarse.at[m : m + 2, :, lanes], out.at[3:5, 32 * h : 32 * h + 32]))
        return found

    copies = copied([(first, first_here), (second, second_here), (skip, skip_here)], semaphores.at[6:9])
    rows[...] = jnp.zeros((32, 128), F32)
    exchanged(in_second_core(), moves, out_a, out_b, semaphores)
    finish(copies)
    for k in range(9):
        rows[2 * k : 2 * k + 2] = first_here[k].astype(F32)
    rows[20:29] = second_here[...].astype(F32)
    rows[18:20] = skip_here[...].astype(F32)
    piece = rows[pl.ds(pl.multiple_of(lat_place() * 8, 8), 8)].astype(BF16)
    sent[...] = jnp.broadcast_to(piece[None], (16, 8, 128))


def edge_at(m, h):
    return 16 + 8 * h + m


def lon_edge_kernel(coarse, cot, lat_a, lat_b, out_a, out_b, low, high):
    odd = in_odd_column()
    sides(lat_a, lat_b, low, high, in_second_core())
    ups, downs = [None] * 30, [None] * 30
    for r in range(-3, 11):
        ref, k = cot_row(cot, low, high, r)
        ups[r + 3] = ref[k, 48:64].astype(F32)[8:]
        downs[r + 3] = ref[k, 0:16].astype(F32)[:8]
    for m in range(-2, 6):
        for h in range(2):
            row = coarse_row(coarse, low, high, m, h).astype(F32)
            ups[edge_at(m, h)] = row[24:32]
            downs[edge_at(m, h)] = row[0:8]
    for k in range(15):
        up = jnp.concatenate(ups[2 * k : 2 * k + 2], axis=0)
        down = jnp.concatenate(downs[2 * k : 2 * k + 2], axis=0)
        out_a[k] = either(odd, down, up)
        out_b[k] = either(odd, up, down)


def sides(first, second, low, high, swap):
    low[...] = either(swap, first[...], second[...])
    high[...] = either(swap, second[...], first[...])


def cot_row(cot, low, high, r):
    return (low, r + 3) if r < 0 else (cot, r) if r < 8 else (high, r - 8)


def coarse_row(coarse, low, high, m, h):
    if 0 <= m < 4:
        return coarse[m, :, 128 * h : 128 * h + 128]
    ref, k = (low, 5 + m) if m < 0 else (high, m - 1)
    return ref[k, 32 * h : 32 * h + 32]


def spread_kernel(came, sent):
    order = permutation(128, block_row, False)
    block = dot(order, came[...].reshape(128, 128)).astype(BF16)
    sent[...] = jnp.broadcast_to(block[None], (32, 128, 128))


def prepare(coarse, cot, low, high, left, right, up, fine3, cot3, grid, field):
    empty = jnp.zeros((8, 128), F32)

    def group(ref, e):
        return ref[e // 2].astype(F32)[8 * (e % 2) : 8 * (e % 2) + 8]

    grid[0:48] = jnp.zeros((48, 256), BF16)
    grid[432:480] = jnp.zeros((48, 256), BF16)
    for m in range(-2, 6):
        at = (m + 3) * 48
        for h in range(2):
            lanes = slice(128 * h, 128 * h + 128)
            middle, e = coarse_row(coarse, low, high, m, h), edge_at(m, h)
            grid[at : at + 32, lanes] = middle
            margin = jnp.concatenate([group(right, e), group(left, e)], axis=0)
            grid[at + 32 : at + 48, lanes] = margin.astype(BF16)
    after = empty
    for r in range(-3, 11):
        at = (r + 3) * PITCH
        ref, k = cot_row(cot, low, high, r)
        field[at : at + 16] = jnp.concatenate([after, group(left, r + 3)], axis=0)
        field[at + 16 : at + 80] = ref[k].astype(F32)
        after = group(right, r + 3)
    field[14 * PITCH :] = jnp.concatenate([after, empty], axis=0)
    cot3[...] = shifted(field[...])

    ordered = dot(grid[...], permutation(256, spread_row, True)).astype(BF16)
    for r in range(-3, 12):
        j, parity = divmod(r, 2)
        block = dot(up[parity], ordered[(j + 2) * 48 : (j + 2) * 48 + 144])
        begin = (r + 3) * PITCH
        rows = min(PITCH, LENGTH - begin)
        keep = inside(begin, (rows, 256))
        for k in range(3):
            part = block[k * PITCH : k * PITCH + rows]
            fine3[begin : begin + rows, k * 256 : k * 256 + 256] = jnp.where(keep, part, 0.0).astype(BF16)


def plane_sum_kernel(came, sent):
    total = came[0].astype(F32)
    for k in range(1, 32):
        total = total + came[k].astype(F32)
    order = permutation(128, block_row, True)
    block = dot(order, total.astype(BF16)).astype(BF16).reshape(16, 8, 128)
    for k in range(2):
        sent[:, k] = block


def column_sum_kernel(came, total):
    part = came[0].astype(F32)
    for k in range(1, 16):
        part = part + came[k].astype(F32)
    total[...] = part


def final_kernel(mine, other, first, second, skip):
    low = jnp.logical_not(in_second_core())
    pieces = []
    for k in range(2):
        pieces += [jnp.where(low, mine[k], other[k]), jnp.where(low, other[k], mine[k])]
    total = jnp.concatenate(pieces, axis=0)
    for k in range(9):
        first[k] = total[2 * k : 2 * k + 2]
        second[k] = total[20 + k : 21 + k]
    skip[...] = total[18:20]


def first_block(weights, k):
    return weights[k // 4, :, k % 4].reshape(256, 128)


def main_kernel(
    weights, coarse, cot, lat_a, lat_b, lon_a, lon_b, up,
    shares, second, fine, cot_kept, hidden3, grad_act,
    low, high, left, right, fine3, cot3, grid, field,
):
    def share_block(b, block):
        shares[b // 4, :, b % 4] = block.astype(BF16).reshape(8, 32, 128)

    pairs, pairs_t = permutation(256, pair_row, True), permutation(256, pair_row, False)
    same = identity()
    sides(lat_a, lat_b, low, high, in_second_core())
    sides(lon_a, lon_b, left, right, in_odd_column())
    prepare(coarse, cot, low, high, left, right, up, fine3, cot3, grid, field)
    fine[...] = fine3[INNER[0] : INNER[1], 256:512]
    cot_kept[...] = cot3[MIDDLE[0] : MIDDLE[1], 128:256]
    flipped_cot = transposed(cells(cot3, INNER[0], slice(128, 256)))
    share = (dot(flipped_cot, cells(fine3, INNER[0], slice(256, 512))) * SCALE).astype(BF16)
    share_block(9, dot_nt(same, share))
    share_block(15, jnp.zeros((256, 128), F32))
    for k in range(5):
        block = dot(pairs, first_block(weights, 10 + k)).astype(BF16)
        second[2 * k] = block[:128]
        second[2 * k + 1] = block[128:]
    begin, end = WIDE
    count = end - begin
    act = jnp.zeros((count, 128), F32)
    for i in range(3):
        kernels = jnp.concatenate([first_block(weights, 3 * i + j) for j in range(3)], axis=0)
        at = begin + PITCH * (i - 1)
        act = act + dot(fine3[at : at + count, :], kernels)
    keep = inside(begin, (count, 128))
    sigma = jax.nn.sigmoid(act)
    hidden = jnp.where(keep, act * sigma, 0.0)
    hidden3[...] = shifted(hidden)[HIDDEN[0] - begin : HIDDEN[1] - begin]
    grad_hidden = jnp.zeros((count, 128), F32)
    for i in range(3):
        kernels = jnp.concatenate([second[3 * i + 2 - j] for j in range(3)], axis=1)
        at = begin - PITCH * (i - 1)
        grad_hidden = grad_hidden + dot_nt(cot3[at : at + count, :], kernels)
    grad = grad_hidden * sigma * (1.0 + act * (1.0 - sigma))
    grad_act[...] = jnp.where(keep, grad, 0.0).astype(BF16)

    found = []
    for i in range(3):
        share = dot(flipped_cot, cells(hidden3, INNER[0] + PITCH * (i - 1) - HIDDEN[0]))
        share = (share * SCALE).astype(BF16)
        found += [share[:, j * 128 : j * 128 + 128] for j in range(3)]
    found.append(jnp.zeros((128, 128), BF16))
    for k in range(5):
        both = jnp.concatenate(found[2 * k : 2 * k + 2], axis=1)
        share_block(10 + k, dot_nt(pairs_t, both))
    flipped_grad = transposed(cells(grad_act, INNER[0] - begin))
    for i in range(3):
        share = dot(flipped_grad, cells(fine3, INNER[0] + PITCH * (i - 1)))
        share = (share * SCALE).astype(BF16)
        for j in range(3):
            share_block(3 * i + j, dot_nt(same, share[:, j * 256 : j * 256 + 256]))


def field_kernel(
    weights, second, fine, cot, hidden3, grad_act, down, result, coarse_gradient
):
    skip = first_block(weights, 9)
    begin, end = INNER
    total = dot(fine[...], skip)
    for i in range(3):
        kernels = jnp.concatenate([second[3 * i + j] for j in range(3)], axis=0)
        at = begin + PITCH * (i - 1) - HIDDEN[0]
        total = total + dot(hidden3[at : at + end - begin, :], kernels)
    total = total.astype(BF16)
    for r in range(8):
        result[r] = total[r * PITCH : r * PITCH + 64]

    grad3 = shifted(grad_act[...].astype(F32))
    begin, end = MIDDLE
    count = end - begin
    back = dot_nt(cot[...], skip)
    for i in range(3):
        kernels = jnp.concatenate([first_block(weights, 3 * i + 2 - j) for j in range(3)], axis=1)
        at = begin - PITCH * (i - 1) - WIDE[0]
        back = back + dot_nt(grad3[at : at + count], kernels)
    fine_gradient = jnp.where(inside(begin, (count, 256)), back, 0.0).astype(BF16)
    spread_t = permutation(256, spread_row, False)
    for j in range(4):
        part = dot(down[...], fine_gradient[2 * j * PITCH : 2 * j * PITCH + 4 * PITCH + 16])
        coarse_gradient[j] = dot(part.astype(BF16), spread_t).astype(BF16)


def call(kernel, outs, *operands, spaces="", scratch=(), semaphores=0, dtype=BF16, vmem=16):
    kinds = dict(h=pltpu.HBM, v=pltpu.VMEM)
    specs = [pl.BlockSpec(memory_space=kinds[k]) for k in spaces]
    return pl.pallas_call(
        kernel,
        out_shape=[jax.ShapeDtypeStruct(shape, dtype) for shape in outs],
        in_specs=specs[: len(operands)],
        out_specs=specs[len(operands) :],
        scratch_shapes=[pltpu.VMEM(*s) for s in scratch]
        + ([pltpu.SemaphoreType.DMA((semaphores,))] if semaphores else []),
        compiler_params=pltpu.CompilerParams(vmem_limit_bytes=vmem * 1024 * 1024),
    )(*operands)


def pairwise(first, second, axis, periodic):
    count = lax.axis_size(axis)
    ends = [(i, (i + 1) % count) for i in range(count if periodic else count - 1)]
    steps = [[(a, b), (b, a)] for a, b in ends]
    return (
        lax.ppermute(first, axis, [p for step in steps[0::2] for p in step]),
        lax.ppermute(second, axis, [p for step in steps[1::2] for p in step]),
    )


def on_device(coarse, w_first, w_second, w_skip, cotangent):
    up, down = jnp.asarray(upsampling_matrices(), BF16), jnp.asarray(decimation_matrix(), BF16)
    sent, *edges = call(
        front_kernel, [(16, 8, 128)] + [(5, 64, 128)] * 2,
        w_first, w_second.reshape(9, 128), w_skip, coarse, cotangent,
        spaces="hhhhhvvv", vmem=60,
        scratch=[((32, 128), F32), ((9, 2, 128), BF16), ((9, 128), BF16), ((2, 128), BF16)],
        semaphores=9,
    )
    came = lax.all_to_all(sent, "z", 0, 0, tiled=True)
    lat_a, lat_b = pairwise(*edges, LAT, False)
    came, lat_a, lat_b = lax.optimization_barrier((came, lat_a, lat_b))
    (sent,) = call(spread_kernel, [(32, 128, 128)], came, spaces="vv")
    sent, lat_a, lat_b = lax.optimization_barrier((sent, lat_a, lat_b))
    weights = lax.all_to_all(sent, PLANE, 0, 0, tiled=True).reshape(4, 8, 4, 32, 128)
    edges = call(
        lon_edge_kernel, [(15, 16, 128)] * 2, coarse, cotangent, lat_a, lat_b,
        spaces="vvvvvv", scratch=[((5, 64, 128), BF16)] * 2,
    )
    lon_a, lon_b = pairwise(*edges, LON, True)
    blocks = (4, 8, 4, 32, 128)
    kept = [
        (10, 128, 128), (INNER[1] - INNER[0], 256), (MIDDLE[1] - MIDDLE[0], 128),
        (HIDDEN[1] - HIDDEN[0], 384), (WIDE[1] - WIDE[0], 128),
    ]
    shares, second, fine, cot_kept, hidden3, grad_act = call(
        main_kernel, [blocks] + kept,
        weights, coarse, cotangent, lat_a, lat_b, lon_a, lon_b, up,
        spaces="v" * 14,
        scratch=[
            (shape, BF16)
            for shape in [
                (5, 64, 128), (5, 64, 128), (15, 16, 128), (15, 16, 128), (LENGTH, 768), (LENGTH, 384), (480, 256),
            ]
        ]
        + [((LENGTH, 128), F32)],
    )
    came = lax.all_to_all(shares.reshape(32, 128, 128), PLANE, 0, 0, tiled=True)
    (sent,) = call(plane_sum_kernel, [(16, 2, 8, 128)], came, spaces="vv")
    came = lax.all_to_all(sent.reshape(32, 8, 128), ("z", "xl"), 0, 0, tiled=True)
    result, coarse_gradient = call(
        field_kernel, [(8, 64, 128), (4, 32, 256)],
        weights, second, fine, cot_kept, hidden3, grad_act, down,
        spaces="vvvvvvvvv",
    )
    came, result, coarse_gradient = lax.optimization_barrier((came, result, coarse_gradient))
    (mine,) = call(column_sum_kernel, [(2, 8, 128)], came.reshape(16, 2, 8, 128), spaces="vv", dtype=F32)
    other = lax.ppermute(mine, "core", [(0, 1), (1, 0)])
    grads = call(
        final_kernel, [(9, 2, 128), (9, 1, 128), (2, 128)],
        mine, other, spaces="vvvvv", dtype=F32,
    )
    return result, coarse_gradient, *grads


def solution(mesh):
    axes = ("xl", "core", "z", "xh", "y")
    fine = Mesh(mesh.devices.reshape(2, 2, 16, 2, 4), axes)
    field, taps, plain = P(LAT, LON, None), P(None, LON, None), P(LON, None)
    return jax.shard_map(
        on_device,
        mesh=fine,
        in_specs=(field, taps, taps, plain, field),
        out_specs=(field, field, taps, taps, plain),
        check_vma=False,
    )
```

time: 120 us -> 111 us (0.925)
  Pallas kernels: 20.8 us -> 12.9 us
  waiting for transfers between devices: 17 us -> 22 us
  starting transfers between devices: 55.7 us -> 53.2 us
  local copies, waits for them, and re-layouts: 1.66 us -> 0.02 us
    pallas_call x9 -> x8, Pallas kernels: 20.8 us -> 12.9 us  [call(): pl.pallas_call(kernel, out_shape=[jax.ShapeDtypeStruct(shape, dtype) for...]
    all_to_all x1, starting transfers between devices: 10.5 us -> 7.64 us  [on_device(): lax.all_to_all(sent.reshape(32, 8, 128), ('z', 'xl'), 0, 0, tiled=True)]
    all_to_all x1, waiting for transfers between devices: 0.01 us -> 2.34 us  [on_device(): came = lax.all_to_all(sent, 'z', 0, 0, tiled=True)]
    unnamed x26 -> x8, local copies, waits for them, and re-layouts: 1.66 us -> 0.02 us
  transfers between devices with their start and end apart: 8 -> 8, of which waited for: 5 -> 7; matrix products, arithmetic and copies ran while one was open for 1% -> 0% of each run, Pallas kernels for 7% -> 3%
where the time goes in v3:
time: 111 us
  starting transfers between devices  53.2 us (48%)
  waiting for transfers between devices  22 us (20%)
  blocking collectives  21.9 us (20%)
  Pallas kernels  12.9 us (12%)
    all_to_all x1, blocking collectives, on_device(): came = lax.all_to_all(shares.reshape(32, 128, 128), PLANE, 0, 0, tiled=True)  21.9 us
    all_to_all x1, starting transfers between devices, on_device(): came = lax.all_to_all(sent, 'z', 0, 0, tiled=True)  15.8 us
    pallas_call x8, Pallas kernels, call(): pl.pallas_call(kernel, out_shape=[jax.ShapeDtypeStruct(shape, dtype) for...  12.9 us
    all_to_all x1, waiting for transfers between devices, on_device(): lax.all_to_all(sent.reshape(32, 8, 128), ('z', 'xl'), 0, 0, tiled=True)  9.66 us
    ppermute x2, starting transfers between devices, pairwise(): lax.ppermute(second, axis, [p for step in steps[1::2] for p in step])  9.59 us
    all_to_all x1, starting transfers between devices, on_device(): lax.all_to_all(sent, PLANE, 0, 0, tiled=True).reshape(4, 8, 4, 32, 128)  9.26 us
    all_to_all x1, starting transfers between devices, on_device(): lax.all_to_all(sent.reshape(32, 8, 128), ('z', 'xl'), 0, 0, tiled=True)  7.64 us
    ppermute x2, starting transfers between devices, pairwise(): lax.ppermute(first, axis, [p for step in steps[0::2] for p in step])  6.29 us
  transfers between devices with their start and end apart: 8, of which 7 were waited for; matrix products, arithmetic and copies ran while one was open for 0% of the time, Pallas kernels for 3%

profile of v3, /device:TPU:1, one launch (start us, length us, event | category | flops | bytes accessed | tf_op | source)
XLA Modules:
  0.0 110.8 jit_solution(9354126936800700805)
XLA Ops:
  0.6 1.7 %shard_map.110 = (bf16[16,8,128]{2,1,0:T(8,128)(2,1)}, bf16[5,64,128]{2,1,0:T(8,128)(2,1)}, bf16[5,64,128]{2,1,0:T(8,128)(2,1)}) custom-call(bf16[9,2,128]{2,1,0:T(2,128)(2,1)} %first.1, bf16[9,128]{1,0:T(8,128)(2,1)} %bitcast.9, bf16[2,128]{1,0:T(2,128)(2,1)} %skip.1, bf16[4,32,256]{2,1,0:T(8,128)(2,1)} %coarse.5, bf16[8,64,128]{2,1,0:T(8,128)(2,1)} %cot.5), custom_call_target="tpu_custom_call" | custom-call | tf_op jit(solution)/shard_map/pallas_call | solution.py:380
  2.3 15.8 %all-to-all-start = ((bf16[16,8,128]{2,1,0:T(8,128)(2,1)}), bf16[16,8,128]{2,1,0:T(8,128)(2,1)S(1)}, u32[]{:S(2)}, u32[]{:S(2)}) async-start(bf16[16,8,128]{2,1,0:T(8,128)(2,1)} %get-tuple-element.30), calls=%async_computation | async-start | bytes 65536 | tf_op jit(solution)/shard_map/all_to_all | solution.py:410
  18.1 2.9 %collective-permute-start = (bf16[5,64,128]{2,1,0:T(8,128)(2,1)}, bf16[5,64,128]{2,1,0:T(8,128)(2,1)S(1)}, u32[]{:S(2)}, u32[]{:S(2)}) collective-permute-start(bf16[5,64,128]{2,1,0:T(8,128)(2,1)} %get-tuple-element.31), channel_id=1, source_target_pairs={{0,128},{128,0},{256,384},{384,256},{1,129},{129,1},{257,385},{385... | collective-permute-start | bytes 245768 | tf_op jit(solution)/shard_map/ppermute | solution.py:396
  20.9 3.0 %collective-permute-start.1 = (bf16[5,64,128]{2,1,0:T(8,128)(2,1)}, bf16[5,64,128]{2,1,0:T(8,128)(2,1)S(1)}, u32[]{:S(2)}, u32[]{:S(2)}) collective-permute-start(bf16[5,64,128]{2,1,0:T(8,128)(2,1)} %get-tuple-element.32), channel_id=1, source_target_pairs={{128,256},{256,128},{129,257},{257,129},{130,258},{258,130},{131,2... | collective-permute-start | bytes 245768 | tf_op jit(solution)/shard_map/ppermute | solution.py:397
  24.0 0.0 collective-permute-done.lat_a
  24.0 3.2 %collective-permute-done.1.lat_b = bf16[5,64,128]{2,1,0:T(8,128)(2,1)S(1)} collective-permute-done((bf16[5,64,128]{2,1,0:T(8,128)(2,1)}, bf16[5,64,128]{2,1,0:T(8,128)(2,1)S(1)}, u32[]{:S(2)}, u32[]{:S(2)}) %collective-permute-start.1) | collective-permute-done | bytes 81952 | tf_op jit(solution)/shard_map/ppermute | solution.py:397
  27.2 2.3 %all-to-all-done.came = bf16[16,8,128]{2,1,0:T(8,128)(2,1)S(1)} async-done(((bf16[16,8,128]{2,1,0:T(8,128)(2,1)}), bf16[16,8,128]{2,1,0:T(8,128)(2,1)S(1)}, u32[]{:S(2)}, u32[]{:S(2)}) %all-to-all-start) | async-done | bytes 32800 | tf_op jit(solution)/shard_map/all_to_all | solution.py:410
  29.5 1.2 %shard_map.111 = bf16[32,128,128]{2,1,0:T(8,128)(2,1)} custom-call(bf16[16,8,128]{2,1,0:T(8,128)(2,1)S(1)} %all-to-all-done.came), custom_call_target="tpu_custom_call" | custom-call | tf_op jit(solution)/shard_map/pallas_call | solution.py:380
  30.8 0.0 copy-start
  30.8 0.0 copy-start.1
  30.8 9.3 %all-to-all-start.1 = ((bf16[32,128,128]{2,1,0:T(8,128)(2,1)}), bf16[32,128,128]{2,1,0:T(8,128)(2,1)S(1)}, u32[]{:S(2)}, u32[]{:S(2)}) async-start(bf16[32,128,128]{2,1,0:T(8,128)(2,1)} %shard_map.111), calls=%async_computation.1 | async-start | bytes 2097152 | tf_op jit(solution)/shard_map/all_to_all | solution.py:415
  40.0 0.0 copy-done
  40.1 0.0 copy-done.1
  40.1 0.0 copy-start.2
  40.1 0.1 shard_map.112
  40.2 3.4 %collective-permute-start.2 = (bf16[15,16,128]{2,1,0:T(8,128)(2,1)S(1)}, bf16[15,16,128]{2,1,0:T(8,128)(2,1)S(1)}, u32[]{:S(2)}, u32[]{:S(2)}) collective-permute-start(bf16[15,16,128]{2,1,0:T(8,128)(2,1)S(1)} %get-tuple-element.39), channel_id=1, source_target_pairs={{0,1},{1,0},{2,3},{3,2},{4,5},{5,4},{6,7},{7,6},{8,9},{9,8},{10,11... | collective-permute-start | bytes 184328 | tf_op jit(solution)/shard_map/ppermute | solution.py:396
  43.6 6.6 %collective-permute-start.3 = (bf16[15,16,128]{2,1,0:T(8,128)(2,1)S(1)}, bf16[15,16,128]{2,1,0:T(8,128)(2,1)S(1)}, u32[]{:S(2)}, u32[]{:S(2)}) collective-permute-start(bf16[15,16,128]{2,1,0:T(8,128)(2,1)S(1)} %get-tuple-element.40), channel_id=1, source_target_pairs={{1,2},{2,1},{3,4},{4,3},{5,6},{6,5},{7,8},{8,7},{9,10},{10,9},{11,... | collective-permute-start | bytes 184328 | tf_op jit(solution)/shard_map/ppermute | solution.py:397
  50.2 3.7 %collective-permute-done.2.lon_a = bf16[15,16,128]{2,1,0:T(8,128)(2,1)S(1)} collective-permute-done((bf16[15,16,128]{2,1,0:T(8,128)(2,1)S(1)}, bf16[15,16,128]{2,1,0:T(8,128)(2,1)S(1)}, u32[]{:S(2)}, u32[]{:S(2)}) %collective-permute-start.2) | collective-permute-done | bytes 61472 | tf_op jit(solution)/shard_map/ppermute | solution.py:396
  53.8 1.3 %collective-permute-done.3.lon_b = bf16[15,16,128]{2,1,0:T(8,128)(2,1)S(1)} collective-permute-done((bf16[15,16,128]{2,1,0:T(8,128)(2,1)S(1)}, bf16[15,16,128]{2,1,0:T(8,128)(2,1)S(1)}, u32[]{:S(2)}, u32[]{:S(2)}) %collective-permute-start.3) | collective-permute-done | bytes 61472 | tf_op jit(solution)/shard_map/ppermute | solution.py:397
  55.2 1.0 all-to-all-done.1
  56.2 0.0 copy-done.2
  56.2 5.5 %shard_map.113 = (bf16[4,8,4,32,128]{4,3,2,1,0:T(8,128)(2,1)S(1)}, bf16[10,128,128]{2,1,0:T(8,128)(2,1)S(1)}, bf16[624,256]{1,0:T(8,128)(2,1)S(1)}, bf16[816,128...) custom-call(bf16[4,8,4,32,128]{4,3,2,1,0:T(8,128)(2,1)S(1)} %bitcast.5, ...), custom_call_target="tpu_custom_call" | custom-call | tf_op jit(solution)/shard_map/pallas_call | solution.py:380
  61.7 21.9 %all_to_all.20.came = bf16[32,128,128]{2,1,0:T(8,128)(2,1)S(1)} all-to-all(bf16[32,128,128]{2,1,0:T(8,128)(2,1)S(1)} %bitcast.7), channel_id=1, replica_groups=mesh['xl'=2,'core'=2,'z'=16,'xh'=2,'y'=4] {'xl','core','xh','y'}, dimensions={0} | all-to-all | bytes 2097152 | tf_op jit(solution)/shard_map/all_to_all | solution.py:438
  83.6 0.9 shard_map.114
  84.5 0.0 copy-start.3
  84.5 7.6 %all-to-all-start.3 = ((bf16[32,8,128]{2,1,0:T(8,128)(2,1)}), bf16[32,8,128]{2,1,0:T(8,128)(2,1)S(1)}, u32[]{:S(2)}, u32[]{:S(2)}) async-start(bf16[32,8,128]{2,1,0:T(8,128)(2,1)} %bitcast.3), calls=%async_computation.3 | async-start | bytes 131072 | tf_op jit(solution)/shard_map/all_to_all | solution.py:440
  92.1 0.0 copy-done.3
  92.1 2.9 %shard_map.115 = (bf16[8,64,128]{2,1,0:T(8,128)(2,1)}, bf16[4,32,256]{2,1,0:T(8,128)(2,1)}) custom-call(bf16[4,8,4,32,128]{4,3,2,1,0:T(8,128)(2,1)S(1)} %bitcast.6, bf16[10,128,128]{2,1,0:T(8,128)(2,1)S(1)} %get-tuple-element.42.second, bf16[624,256]{1,0:T(8,128)(2,1)S(1)} %get-tuple-element.43.fine, bf16[816,128]{1,0:T(8,128)(2,1)S(1)} %get-tuple-element.44.cot, ...), custom_call_target="tpu_custom_call" | custom-call | tf_op jit(solution)/shard_map/pallas_call | solution.py:380
  95.0 9.7 %all-to-all-done.3 = bf16[32,8,128]{2,1,0:T(8,128)(2,1)S(1)} async-done(((bf16[32,8,128]{2,1,0:T(8,128)(2,1)}), bf16[32,8,128]{2,1,0:T(8,128)(2,1)S(1)}, u32[]{:S(2)}, u32[]{:S(2)}) %all-to-all-start.3) | async-done | bytes 65568 | tf_op jit(solution)/shard_map/all_to_all | solution.py:440
  104.7 4.7 %collective-permute-start.4 = (f32[2,8,128]{2,1,0:T(8,128)S(1)}, f32[2,8,128]{2,1,0:T(8,128)S(1)}, u32[]{:S(2)}, u32[]{:S(2)}) collective-permute-start(f32[2,8,128]{2,1,0:T(8,128)S(1)} %shard_map.116.mine), channel_id=1, source_target_pairs={{0,128},{128,0},{1,129},{129,1},{2,130},{130,2},{3,131},{131,3},{4... | collective-permute-start | bytes 24584 | tf_op jit(solution)/shard_map/ppermute | solution.py:448
  109.4 0.8 collective-permute-done.4.other
  110.2 0.6 shard_map.117
  (1 shorter events, 0.0 us)
Async XLA Ops:
  2.3 27.2 %all-to-all-start = ((bf16[16,8,128]{2,1,0:T(8,128)(2,1)}), bf16[16,8,128]{2,1,0:T(8,128)(2,1)S(1)}, u32[]{:S(2)}, u32[]{:S(2)}) async-start(bf16[16,8,128]{2,1,0:T(8,128)(2,1)} %get-tuple-element.30), calls=%async_computation | async-start | bytes 65536 | tf_op jit(solution)/shard_map/all_to_all | solution.py:410
  18.1 5.9 %collective-permute-start = (bf16[5,64,128]{2,1,0:T(8,128)(2,1)}, bf16[5,64,128]{2,1,0:T(8,128)(2,1)S(1)}, u32[]{:S(2)}, u32[]{:S(2)}) collective-permute-start(bf16[5,64,128]{2,1,0:T(8,128)(2,1)} %get-tuple-element.31), channel_id=1, source_target_pairs={{0,128},{128,0},{256,384},{384,256},{1,129},{129,1},{257,385},{385... | collective-permute-start | bytes 245768 | tf_op jit(solution)/shard_map/ppermute | solution.py:396
  20.9 6.3 %collective-permute-start.1 = (bf16[5,64,128]{2,1,0:T(8,128)(2,1)}, bf16[5,64,128]{2,1,0:T(8,128)(2,1)S(1)}, u32[]{:S(2)}, u32[]{:S(2)}) collective-permute-start(bf16[5,64,128]{2,1,0:T(8,128)(2,1)} %get-tuple-element.32), channel_id=1, source_target_pairs={{128,256},{256,128},{129,257},{257,129},{130,258},{258,130},{131,2... | collective-permute-start | bytes 245768 | tf_op jit(solution)/shard_map/ppermute | solution.py:397
  30.8 9.3 %copy-start = (bf16[8,64,128]{2,1,0:T(8,128)(2,1)S(1)}, bf16[8,64,128]{2,1,0:T(8,128)(2,1)}, u32[]{:S(2)}) copy-start(bf16[8,64,128]{2,1,0:T(8,128)(2,1)} %cot.5) | copy-start | bytes 393220
  30.8 9.3 %copy-start.1 = (bf16[4,32,256]{2,1,0:T(8,128)(2,1)S(1)}, bf16[4,32,256]{2,1,0:T(8,128)(2,1)}, u32[]{:S(2)}) copy-start(bf16[4,32,256]{2,1,0:T(8,128)(2,1)} %coarse.5) | copy-start | bytes 196612
  30.8 25.4 %all-to-all-start.1 = ((bf16[32,128,128]{2,1,0:T(8,128)(2,1)}), bf16[32,128,128]{2,1,0:T(8,128)(2,1)S(1)}, u32[]{:S(2)}, u32[]{:S(2)}) async-start(bf16[32,128,128]{2,1,0:T(8,128)(2,1)} %shard_map.111), calls=%async_computation.1 | async-start | bytes 2097152 | tf_op jit(solution)/shard_map/all_to_all | solution.py:415
  40.1 16.1 %copy-start.2 = (bf16[2,240,144]{2,1,0:T(8,128)(2,1)S(1)}, bf16[2,240,144]{2,1,0:T(8,128)(2,1)}, u32[]{:S(2)}) copy-start(bf16[2,240,144]{2,1,0:T(8,128)(2,1)} %constant.4.clone.up) | copy-start | bytes 414724
  40.2 13.7 %collective-permute-start.2 = (bf16[15,16,128]{2,1,0:T(8,128)(2,1)S(1)}, bf16[15,16,128]{2,1,0:T(8,128)(2,1)S(1)}, u32[]{:S(2)}, u32[]{:S(2)}) collective-permute-start(bf16[15,16,128]{2,1,0:T(8,128)(2,1)S(1)} %get-tuple-element.39), channel_id=1, source_target_pairs={{0,1},{1,0},{2,3},{3,2},{4,5},{5,4},{6,7},{7,6},{8,9},{9,8},{10,11... | collective-permute-start | bytes 184328 | tf_op jit(solution)/shard_map/ppermute | solution.py:396
  43.6 11.6 %collective-permute-start.3 = (bf16[15,16,128]{2,1,0:T(8,128)(2,1)S(1)}, bf16[15,16,128]{2,1,0:T(8,128)(2,1)S(1)}, u32[]{:S(2)}, u32[]{:S(2)}) collective-permute-start(bf16[15,16,128]{2,1,0:T(8,128)(2,1)S(1)} %get-tuple-element.40), channel_id=1, source_target_pairs={{1,2},{2,1},{3,4},{4,3},{5,6},{6,5},{7,8},{8,7},{9,10},{10,9},{11,... | collective-permute-start | bytes 184328 | tf_op jit(solution)/shard_map/ppermute | solution.py:397
  84.5 7.6 %copy-start.3 = (bf16[32,336]{1,0:T(8,128)(2,1)S(1)}, bf16[32,336]{1,0:T(8,128)(2,1)}, u32[]{:S(2)}) copy-start(bf16[32,336]{1,0:T(8,128)(2,1)} %constant.5.clone.down) | copy-start | bytes 64516
  84.5 20.2 %all-to-all-start.3 = ((bf16[32,8,128]{2,1,0:T(8,128)(2,1)}), bf16[32,8,128]{2,1,0:T(8,128)(2,1)S(1)}, u32[]{:S(2)}, u32[]{:S(2)}) async-start(bf16[32,8,128]{2,1,0:T(8,128)(2,1)} %bitcast.3), calls=%async_computation.3 | async-start | bytes 131072 | tf_op jit(solution)/shard_map/all_to_all | solution.py:440
  104.7 5.5 %collective-permute-start.4 = (f32[2,8,128]{2,1,0:T(8,128)S(1)}, f32[2,8,128]{2,1,0:T(8,128)S(1)}, u32[]{:S(2)}, u32[]{:S(2)}) collective-permute-start(f32[2,8,128]{2,1,0:T(8,128)S(1)} %shard_map.116.mine), channel_id=1, source_target_pairs={{0,128},{128,0},{1,129},{129,1},{2,130},{130,2},{3,131},{131,3},{4... | collective-permute-start | bytes 24584 | tf_op jit(solution)/shard_map/ppermute | solution.py:448

commit v4 on v3

--- a/solution.py
+++ b/solution.py
@@ -176,19 +176,19 @@
 def lon_edge_kernel(coarse, cot, lat_a, lat_b, out_a, out_b, low, high):
     odd = in_odd_column()
     sides(lat_a, lat_b, low, high, in_second_core())
-    ups, downs = [None] * 30, [None] * 30
+    ups, downs = [jnp.zeros((4, 128), F32)] * 32, [jnp.zeros((4, 128), F32)] * 32
     for r in range(-3, 11):
         ref, k = cot_row(cot, low, high, r)
-        ups[r + 3] = ref[k, 48:64].astype(F32)[8:]
-        downs[r + 3] = ref[k, 0:16].astype(F32)[:8]
+        ups[r + 3] = ref[k, 48:64].astype(F32)[12:]
+        downs[r + 3] = ref[k, 0:16].astype(F32)[:4]
     for m in range(-2, 6):
         for h in range(2):
             row = coarse_row(coarse, low, high, m, h).astype(F32)
-            ups[edge_at(m, h)] = row[24:32]
-            downs[edge_at(m, h)] = row[0:8]
-    for k in range(15):
-        up = jnp.concatenate(ups[2 * k : 2 * k + 2], axis=0)
-        down = jnp.concatenate(downs[2 * k : 2 * k + 2], axis=0)
+            ups[edge_at(m, h)] = row[28:32]
+            downs[edge_at(m, h)] = row[0:4]
+    for k in range(8):
+        up = jnp.concatenate(ups[4 * k : 4 * k + 4], axis=0)
+        down = jnp.concatenate(downs[4 * k : 4 * k + 4], axis=0)
         out_a[k] = either(odd, down, up)
         out_b[k] = either(odd, up, down)
 
@@ -216,10 +216,10 @@
 
 
 def prepare(coarse, cot, low, high, left, right, up, fine3, cot3, grid, field):
-    empty = jnp.zeros((8, 128), F32)
+    empty = jnp.zeros((4, 128), F32)
 
     def group(ref, e):
-        return ref[e // 2].astype(F32)[8 * (e % 2) : 8 * (e % 2) + 8]
+        return ref[e // 4].astype(F32)[4 * (e % 4) : 4 * (e % 4) + 4]
 
     grid[0:48] = jnp.zeros((48, 256), BF16)
     grid[432:480] = jnp.zeros((48, 256), BF16)
@@ -229,16 +229,16 @@
             lanes = slice(128 * h, 128 * h + 128)
             middle, e = coarse_row(coarse, low, high, m, h), edge_at(m, h)
             grid[at : at + 32, lanes] = middle
-            margin = jnp.concatenate([group(right, e), group(left, e)], axis=0)
+            margin = jnp.concatenate([group(right, e), empty, empty, group(left, e)], axis=0)
             grid[at + 32 : at + 48, lanes] = margin.astype(BF16)
     after = empty
     for r in range(-3, 11):
         at = (r + 3) * PITCH
         ref, k = cot_row(cot, low, high, r)
-        field[at : at + 16] = jnp.concatenate([after, group(left, r + 3)], axis=0)
+        field[at : at + 16] = jnp.concatenate([after, empty, empty, group(left, r + 3)], axis=0)
         field[at + 16 : at + 80] = ref[k].astype(F32)
         after = group(right, r + 3)
-    field[14 * PITCH :] = jnp.concatenate([after, empty], axis=0)
+    field[14 * PITCH :] = jnp.concatenate([after, empty, empty, empty], axis=0)
     cot3[...] = shifted(field[...])
 
     ordered = dot(grid[...], permutation(256, spread_row, True)).astype(BF16)
@@ -409,12 +409,11 @@
     )
     came = lax.all_to_all(sent, "z", 0, 0, tiled=True)
     lat_a, lat_b = pairwise(*edges, LAT, False)
-    came, lat_a, lat_b = lax.optimization_barrier((came, lat_a, lat_b))
     (sent,) = call(spread_kernel, [(32, 128, 128)], came, spaces="vv")
     sent, lat_a, lat_b = lax.optimization_barrier((sent, lat_a, lat_b))
     weights = lax.all_to_all(sent, PLANE, 0, 0, tiled=True).reshape(4, 8, 4, 32, 128)
     edges = call(
-        lon_edge_kernel, [(15, 16, 128)] * 2, coarse, cotangent, lat_a, lat_b,
+        lon_edge_kernel, [(8, 16, 128)] * 2, coarse, cotangent, lat_a, lat_b,
         spaces="vvvvvv", scratch=[((5, 64, 128), BF16)] * 2,
     )
     lon_a, lon_b = pairwise(*edges, LON, True)
@@ -430,7 +429,7 @@
         scratch=[
             (shape, BF16)
             for shape in [
-                (5, 64, 128), (5, 64, 128), (15, 16, 128), (15, 16, 128), (LENGTH, 768), (LENGTH, 384), (480, 256),
+                (5, 64, 128), (5, 64, 128), (8, 16, 128), (8, 16, 128), (LENGTH, 768), (LENGTH, 384), (480, 256),
             ]
         ]
         + [((LENGTH, 128), F32)],

time: 111 us -> 109 us (0.982)
  starting transfers between devices: 53.2 us -> 51.8 us
    all_to_all x1, waiting for transfers between devices: 2.34 us -> 5.58 us  [on_device(): came = lax.all_to_all(sent, 'z', 0, 0, tiled=True)]
    ppermute x2, waiting for transfers between devices: 4.56 us -> 1.7 us  [pairwise(): lax.ppermute(second, axis, [p for step in steps[1::2] for p in step])]
    all_to_all x1, starting transfers between devices: 7.64 us -> 6.24 us  [on_device(): lax.all_to_all(sent.reshape(32, 8, 128), ('z', 'xl'), 0, 0, tiled=True)]
  transfers between devices with their start and end apart: 8 -> 8, of which waited for: 7 -> 6; matrix products, arithmetic and copies ran while one was open for 0% -> 0% of each run, Pallas kernels for 3% -> 4%
where the time goes in v4:
time: 109 us
  starting transfers between devices  51.8 us (48%)
  waiting for transfers between devices  22 us (20%)
  blocking collectives  21.4 us (20%)
  Pallas kernels  12.9 us (12%)
    all_to_all x1, blocking collectives, on_device(): came = lax.all_to_all(shares.reshape(32, 128, 128), PLANE, 0, 0, tiled=True)  21.4 us
    all_to_all x1, starting transfers between devices, on_device(): came = lax.all_to_all(sent, 'z', 0, 0, tiled=True)  15.8 us
    pallas_call x8, Pallas kernels, call(): pl.pallas_call(kernel, out_shape=[jax.ShapeDtypeStruct(shape, dtype) for...  12.9 us
    all_to_all x1, waiting for transfers between devices, on_device(): lax.all_to_all(sent.reshape(32, 8, 128), ('z', 'xl'), 0, 0, tiled=True)  9.65 us
    ppermute x2, starting transfers between devices, pairwise(): lax.ppermute(second, axis, [p for step in steps[1::2] for p in step])  9.59 us
    all_to_all x1, starting transfers between devices, on_device(): lax.all_to_all(sent, PLANE, 0, 0, tiled=True).reshape(4, 8, 4, 32, 128)  9.28 us
    ppermute x2, starting transfers between devices, pairwise(): lax.ppermute(first, axis, [p for step in steps[0::2] for p in step])  6.29 us
    all_to_all x1, starting transfers between devices, on_device(): lax.all_to_all(sent.reshape(32, 8, 128), ('z', 'xl'), 0, 0, tiled=True)  6.24 us
  transfers between devices with their start and end apart: 8, of which 6 were waited for; matrix products, arithmetic and copies ran while one was open for 0% of the time, Pallas kernels for 4%

profile of v4, /device:TPU:1, one launch (start us, length us, event | category | flops | bytes accessed | tf_op | source)
XLA Modules:
  0.0 108.8 jit_solution(4922571349123347021)
XLA Ops:
  0.6 1.7 %shard_map.110 = (bf16[16,8,128]{2,1,0:T(8,128)(2,1)}, bf16[5,64,128]{2,1,0:T(8,128)(2,1)}, bf16[5,64,128]{2,1,0:T(8,128)(2,1)}) custom-call(bf16[9,2,128]{2,1,0:T(2,128)(2,1)} %first.1, bf16[9,128]{1,0:T(8,128)(2,1)} %bitcast.9, bf16[2,128]{1,0:T(2,128)(2,1)} %skip.1, bf16[4,32,256]{2,1,0:T(8,128)(2,1)} %coarse.5, bf16[8,64,128]{2,1,0:T(8,128)(2,1)} %cot.5), custom_call_target="tpu_custom_call" | custom-call | tf_op jit(solution)/shard_map/pallas_call | solution.py:380
  2.3 15.8 %all-to-all-start = ((bf16[16,8,128]{2,1,0:T(8,128)(2,1)}), bf16[16,8,128]{2,1,0:T(8,128)(2,1)S(1)}, u32[]{:S(2)}, u32[]{:S(2)}) async-start(bf16[16,8,128]{2,1,0:T(8,128)(2,1)} %get-tuple-element.27), calls=%async_computation | async-start | bytes 65536 | tf_op jit(solution)/shard_map/all_to_all | solution.py:410
  18.1 2.9 %collective-permute-start = (bf16[5,64,128]{2,1,0:T(8,128)(2,1)}, bf16[5,64,128]{2,1,0:T(8,128)(2,1)S(1)}, u32[]{:S(2)}, u32[]{:S(2)}) collective-permute-start(bf16[5,64,128]{2,1,0:T(8,128)(2,1)} %get-tuple-element.28), channel_id=1, source_target_pairs={{0,128},{128,0},{256,384},{384,256},{1,129},{129,1},{257,385},{385... | collective-permute-start | bytes 245768 | tf_op jit(solution)/shard_map/ppermute | solution.py:396
  20.9 3.0 %collective-permute-start.1 = (bf16[5,64,128]{2,1,0:T(8,128)(2,1)}, bf16[5,64,128]{2,1,0:T(8,128)(2,1)S(1)}, u32[]{:S(2)}, u32[]{:S(2)}) collective-permute-start(bf16[5,64,128]{2,1,0:T(8,128)(2,1)} %get-tuple-element.29), channel_id=1, source_target_pairs={{128,256},{256,128},{129,257},{257,129},{130,258},{258,130},{131,2... | collective-permute-start | bytes 245768 | tf_op jit(solution)/shard_map/ppermute | solution.py:397
  24.0 5.6 %all-to-all-done.came = bf16[16,8,128]{2,1,0:T(8,128)(2,1)S(1)} async-done(((bf16[16,8,128]{2,1,0:T(8,128)(2,1)}), bf16[16,8,128]{2,1,0:T(8,128)(2,1)S(1)}, u32[]{:S(2)}, u32[]{:S(2)}) %all-to-all-start) | async-done | bytes 32800 | tf_op jit(solution)/shard_map/all_to_all | solution.py:410
  29.5 1.2 %shard_map.111 = bf16[32,128,128]{2,1,0:T(8,128)(2,1)} custom-call(bf16[16,8,128]{2,1,0:T(8,128)(2,1)S(1)} %all-to-all-done.came), custom_call_target="tpu_custom_call" | custom-call | tf_op jit(solution)/shard_map/pallas_call | solution.py:380
  30.8 0.0 copy-start
  30.8 0.0 copy-start.1
  30.8 0.0 collective-permute-done.lat_a
  30.8 0.0 collective-permute-done.1.lat_b
  30.8 9.3 %all-to-all-start.1 = ((bf16[32,128,128]{2,1,0:T(8,128)(2,1)}), bf16[32,128,128]{2,1,0:T(8,128)(2,1)S(1)}, u32[]{:S(2)}, u32[]{:S(2)}) async-start(bf16[32,128,128]{2,1,0:T(8,128)(2,1)} %shard_map.111), calls=%async_computation.1 | async-start | bytes 2097152 | tf_op jit(solution)/shard_map/all_to_all | solution.py:414
  40.1 0.0 copy-done
  40.1 0.0 copy-done.1
  40.1 0.0 copy-start.2
  40.1 0.1 shard_map.112
  40.2 3.4 %collective-permute-start.2 = (bf16[8,16,128]{2,1,0:T(8,128)(2,1)S(1)}, bf16[8,16,128]{2,1,0:T(8,128)(2,1)S(1)}, u32[]{:S(2)}, u32[]{:S(2)}) collective-permute-start(bf16[8,16,128]{2,1,0:T(8,128)(2,1)S(1)} %get-tuple-element.33), channel_id=1, source_target_pairs={{0,1},{1,0},{2,3},{3,2},{4,5},{5,4},{6,7},{7,6},{8,9},{9,8},{10,11... | collective-permute-start | bytes 98312 | tf_op jit(solution)/shard_map/ppermute | solution.py:396
  43.6 6.6 %collective-permute-start.3 = (bf16[8,16,128]{2,1,0:T(8,128)(2,1)S(1)}, bf16[8,16,128]{2,1,0:T(8,128)(2,1)S(1)}, u32[]{:S(2)}, u32[]{:S(2)}) collective-permute-start(bf16[8,16,128]{2,1,0:T(8,128)(2,1)S(1)} %get-tuple-element.34), channel_id=1, source_target_pairs={{1,2},{2,1},{3,4},{4,3},{5,6},{6,5},{7,8},{8,7},{9,10},{10,9},{11,... | collective-permute-start | bytes 98312 | tf_op jit(solution)/shard_map/ppermute | solution.py:397
  50.2 2.7 %collective-permute-done.2.lon_a = bf16[8,16,128]{2,1,0:T(8,128)(2,1)S(1)} collective-permute-done((bf16[8,16,128]{2,1,0:T(8,128)(2,1)S(1)}, bf16[8,16,128]{2,1,0:T(8,128)(2,1)S(1)}, u32[]{:S(2)}, u32[]{:S(2)}) %collective-permute-start.2) | collective-permute-done | bytes 32800 | tf_op jit(solution)/shard_map/ppermute | solution.py:396
  52.9 1.7 %collective-permute-done.3.lon_b = bf16[8,16,128]{2,1,0:T(8,128)(2,1)S(1)} collective-permute-done((bf16[8,16,128]{2,1,0:T(8,128)(2,1)S(1)}, bf16[8,16,128]{2,1,0:T(8,128)(2,1)S(1)}, u32[]{:S(2)}, u32[]{:S(2)}) %collective-permute-start.3) | collective-permute-done | bytes 32800 | tf_op jit(solution)/shard_map/ppermute | solution.py:397
  54.6 1.6 %all-to-all-done.1 = bf16[32,128,128]{2,1,0:T(8,128)(2,1)S(1)} async-done(((bf16[32,128,128]{2,1,0:T(8,128)(2,1)}), bf16[32,128,128]{2,1,0:T(8,128)(2,1)S(1)}, u32[]{:S(2)}, u32[]{:S(2)}) %all-to-all-start.1) | async-done | bytes 1048608 | tf_op jit(solution)/shard_map/all_to_all | solution.py:414
  56.1 0.0 copy-done.2
  56.1 5.5 %shard_map.113 = (bf16[4,8,4,32,128]{4,3,2,1,0:T(8,128)(2,1)S(1)}, bf16[10,128,128]{2,1,0:T(8,128)(2,1)S(1)}, bf16[624,256]{1,0:T(8,128)(2,1)S(1)}, bf16[816,128...) custom-call(bf16[4,8,4,32,128]{4,3,2,1,0:T(8,128)(2,1)S(1)} %bitcast.5, ...), custom_call_target="tpu_custom_call" | custom-call | tf_op jit(solution)/shard_map/pallas_call | solution.py:380
  61.6 21.4 %all_to_all.20.came = bf16[32,128,128]{2,1,0:T(8,128)(2,1)S(1)} all-to-all(bf16[32,128,128]{2,1,0:T(8,128)(2,1)S(1)} %bitcast.7), channel_id=1, replica_groups=mesh['xl'=2,'core'=2,'z'=16,'xh'=2,'y'=4] {'xl','core','xh','y'}, dimensions={0} | all-to-all | bytes 2097152 | tf_op jit(solution)/shard_map/all_to_all | solution.py:437
  83.0 0.9 shard_map.114
  83.9 0.0 copy-start.3
  83.9 6.2 %all-to-all-start.3 = ((bf16[32,8,128]{2,1,0:T(8,128)(2,1)}), bf16[32,8,128]{2,1,0:T(8,128)(2,1)S(1)}, u32[]{:S(2)}, u32[]{:S(2)}) async-start(bf16[32,8,128]{2,1,0:T(8,128)(2,1)} %bitcast.3), calls=%async_computation.3 | async-start | bytes 131072 | tf_op jit(solution)/shard_map/all_to_all | solution.py:439
  90.1 0.0 copy-done.3
  90.1 2.9 %shard_map.115 = (bf16[8,64,128]{2,1,0:T(8,128)(2,1)}, bf16[4,32,256]{2,1,0:T(8,128)(2,1)}) custom-call(bf16[4,8,4,32,128]{4,3,2,1,0:T(8,128)(2,1)S(1)} %bitcast.6, bf16[10,128,128]{2,1,0:T(8,128)(2,1)S(1)} %get-tuple-element.36.second, bf16[624,256]{1,0:T(8,128)(2,1)S(1)} %get-tuple-element.37.fine, bf16[816,128]{1,0:T(8,128)(2,1)S(1)} %get-tuple-element.38.cot, ...), custom_call_target="tpu_custom_call" | custom-call | tf_op jit(solution)/shard_map/pallas_call | solution.py:380
  93.0 9.7 %all-to-all-done.3 = bf16[32,8,128]{2,1,0:T(8,128)(2,1)S(1)} async-done(((bf16[32,8,128]{2,1,0:T(8,128)(2,1)}), bf16[32,8,128]{2,1,0:T(8,128)(2,1)S(1)}, u32[]{:S(2)}, u32[]{:S(2)}) %all-to-all-start.3) | async-done | bytes 65568 | tf_op jit(solution)/shard_map/all_to_all | solution.py:439
  102.7 4.7 %collective-permute-start.4 = (f32[2,8,128]{2,1,0:T(8,128)S(1)}, f32[2,8,128]{2,1,0:T(8,128)S(1)}, u32[]{:S(2)}, u32[]{:S(2)}) collective-permute-start(f32[2,8,128]{2,1,0:T(8,128)S(1)} %shard_map.116.mine), channel_id=1, source_target_pairs={{0,128},{128,0},{1,129},{129,1},{2,130},{130,2},{3,131},{131,3},{4... | collective-permute-start | bytes 24584 | tf_op jit(solution)/shard_map/ppermute | solution.py:447
  107.4 0.8 collective-permute-done.4.other
  108.2 0.6 shard_map.117
  (1 shorter events, 0.0 us)
Async XLA Ops:
  2.3 27.2 %all-to-all-start = ((bf16[16,8,128]{2,1,0:T(8,128)(2,1)}), bf16[16,8,128]{2,1,0:T(8,128)(2,1)S(1)}, u32[]{:S(2)}, u32[]{:S(2)}) async-start(bf16[16,8,128]{2,1,0:T(8,128)(2,1)} %get-tuple-element.27), calls=%async_computation | async-start | bytes 65536 | tf_op jit(solution)/shard_map/all_to_all | solution.py:410
  18.1 12.7 %collective-permute-start = (bf16[5,64,128]{2,1,0:T(8,128)(2,1)}, bf16[5,64,128]{2,1,0:T(8,128)(2,1)S(1)}, u32[]{:S(2)}, u32[]{:S(2)}) collective-permute-start(bf16[5,64,128]{2,1,0:T(8,128)(2,1)} %get-tuple-element.28), channel_id=1, source_target_pairs={{0,128},{128,0},{256,384},{384,256},{1,129},{129,1},{257,385},{385... | collective-permute-start | bytes 245768 | tf_op jit(solution)/shard_map/ppermute | solution.py:396
  20.9 9.8 %collective-permute-start.1 = (bf16[5,64,128]{2,1,0:T(8,128)(2,1)}, bf16[5,64,128]{2,1,0:T(8,128)(2,1)S(1)}, u32[]{:S(2)}, u32[]{:S(2)}) collective-permute-start(bf16[5,64,128]{2,1,0:T(8,128)(2,1)} %get-tuple-element.29), channel_id=1, source_target_pairs={{128,256},{256,128},{129,257},{257,129},{130,258},{258,130},{131,2... | collective-permute-start | bytes 245768 | tf_op jit(solution)/shard_map/ppermute | solution.py:397
  30.8 9.3 %copy-start = (bf16[8,64,128]{2,1,0:T(8,128)(2,1)S(1)}, bf16[8,64,128]{2,1,0:T(8,128)(2,1)}, u32[]{:S(2)}) copy-start(bf16[8,64,128]{2,1,0:T(8,128)(2,1)} %cot.5) | copy-start | bytes 393220
  30.8 9.3 %copy-start.1 = (bf16[4,32,256]{2,1,0:T(8,128)(2,1)S(1)}, bf16[4,32,256]{2,1,0:T(8,128)(2,1)}, u32[]{:S(2)}) copy-start(bf16[4,32,256]{2,1,0:T(8,128)(2,1)} %coarse.5) | copy-start | bytes 196612
  30.8 25.3 %all-to-all-start.1 = ((bf16[32,128,128]{2,1,0:T(8,128)(2,1)}), bf16[32,128,128]{2,1,0:T(8,128)(2,1)S(1)}, u32[]{:S(2)}, u32[]{:S(2)}) async-start(bf16[32,128,128]{2,1,0:T(8,128)(2,1)} %shard_map.111), calls=%async_computation.1 | async-start | bytes 2097152 | tf_op jit(solution)/shard_map/all_to_all | solution.py:414
  40.1 16.0 %copy-start.2 = (bf16[2,240,144]{2,1,0:T(8,128)(2,1)S(1)}, bf16[2,240,144]{2,1,0:T(8,128)(2,1)}, u32[]{:S(2)}) copy-start(bf16[2,240,144]{2,1,0:T(8,128)(2,1)} %constant.4.clone.up) | copy-start | bytes 414724
  40.2 12.7 %collective-permute-start.2 = (bf16[8,16,128]{2,1,0:T(8,128)(2,1)S(1)}, bf16[8,16,128]{2,1,0:T(8,128)(2,1)S(1)}, u32[]{:S(2)}, u32[]{:S(2)}) collective-permute-start(bf16[8,16,128]{2,1,0:T(8,128)(2,1)S(1)} %get-tuple-element.33), channel_id=1, source_target_pairs={{0,1},{1,0},{2,3},{3,2},{4,5},{5,4},{6,7},{7,6},{8,9},{9,8},{10,11... | collective-permute-start | bytes 98312 | tf_op jit(solution)/shard_map/ppermute | solution.py:396
  43.6 11.0 %collective-permute-start.3 = (bf16[8,16,128]{2,1,0:T(8,128)(2,1)S(1)}, bf16[8,16,128]{2,1,0:T(8,128)(2,1)S(1)}, u32[]{:S(2)}, u32[]{:S(2)}) collective-permute-start(bf16[8,16,128]{2,1,0:T(8,128)(2,1)S(1)} %get-tuple-element.34), channel_id=1, source_target_pairs={{1,2},{2,1},{3,4},{4,3},{5,6},{6,5},{7,8},{8,7},{9,10},{10,9},{11,... | collective-permute-start | bytes 98312 | tf_op jit(solution)/shard_map/ppermute | solution.py:397
  83.9 6.3 %copy-start.3 = (bf16[32,336]{1,0:T(8,128)(2,1)S(1)}, bf16[32,336]{1,0:T(8,128)(2,1)}, u32[]{:S(2)}) copy-start(bf16[32,336]{1,0:T(8,128)(2,1)} %constant.5.clone.down) | copy-start | bytes 64516
  83.9 18.8 %all-to-all-start.3 = ((bf16[32,8,128]{2,1,0:T(8,128)(2,1)}), bf16[32,8,128]{2,1,0:T(8,128)(2,1)S(1)}, u32[]{:S(2)}, u32[]{:S(2)}) async-start(bf16[32,8,128]{2,1,0:T(8,128)(2,1)} %bitcast.3), calls=%async_computation.3 | async-start | bytes 131072 | tf_op jit(solution)/shard_map/all_to_all | solution.py:439
  102.7 5.5 %collective-permute-start.4 = (f32[2,8,128]{2,1,0:T(8,128)S(1)}, f32[2,8,128]{2,1,0:T(8,128)S(1)}, u32[]{:S(2)}, u32[]{:S(2)}) collective-permute-start(f32[2,8,128]{2,1,0:T(8,128)S(1)} %shard_map.116.mine), channel_id=1, source_target_pairs={{0,128},{128,0},{1,129},{129,1},{2,130},{130,2},{3,131},{131,3},{4... | collective-permute-start | bytes 24584 | tf_op jit(solution)/shard_map/ppermute | solution.py:447

commit v5 on v4

--- a/solution.py
+++ b/solution.py
@@ -17,7 +17,7 @@
 SCALE = 1.0 / 512.0
 LAT = ("xl", "core")
 LON = ("z", "xh", "y")
-PLANE = ("xl", "core", "xh", "y")
+PLANE = ("xh", "y", "xl", "core")
 
 
 def upsampling_matrices():
@@ -283,7 +283,7 @@
 
 
 def first_block(weights, k):
-    return weights[k // 4, :, k % 4].reshape(256, 128)
+    return weights[:, k // 4, k % 4].reshape(256, 128)
 
 
 def main_kernel(
@@ -292,7 +292,7 @@
     low, high, left, right, fine3, cot3, grid, field,
 ):
     def share_block(b, block):
-        shares[b // 4, :, b % 4] = block.astype(BF16).reshape(8, 32, 128)
+        shares[:, b // 4, b % 4] = block.astype(BF16).reshape(8, 32, 128)
 
     pairs, pairs_t = permutation(256, pair_row, True), permutation(256, pair_row, False)
     same = identity()
@@ -411,13 +411,13 @@
     lat_a, lat_b = pairwise(*edges, LAT, False)
     (sent,) = call(spread_kernel, [(32, 128, 128)], came, spaces="vv")
     sent, lat_a, lat_b = lax.optimization_barrier((sent, lat_a, lat_b))
-    weights = lax.all_to_all(sent, PLANE, 0, 0, tiled=True).reshape(4, 8, 4, 32, 128)
+    weights = lax.all_to_all(sent, PLANE, 0, 0, tiled=True).reshape(8, 4, 4, 32, 128)
     edges = call(
         lon_edge_kernel, [(8, 16, 128)] * 2, coarse, cotangent, lat_a, lat_b,
         spaces="vvvvvv", scratch=[((5, 64, 128), BF16)] * 2,
     )
     lon_a, lon_b = pairwise(*edges, LON, True)
-    blocks = (4, 8, 4, 32, 128)
+    blocks = (8, 4, 4, 32, 128)
     kept = [
         (10, 128, 128), (INNER[1] - INNER[0], 256), (MIDDLE[1] - MIDDLE[0], 128),
         (HIDDEN[1] - HIDDEN[0], 384), (WIDE[1] - WIDE[0], 128),

time: 109 us -> 109 us (level)
  waiting for transfers between devices: 22 us -> 23.1 us
    ppermute x2, waiting for transfers between devices: 2.68 us -> 0.01 us  [pairwise(): lax.ppermute(first, axis, [p for step in steps[0::2] for p in step])]
    ppermute x2, waiting for transfers between devices: 1.7 us -> 4.02 us  [pairwise(): lax.ppermute(second, axis, [p for step in steps[1::2] for p in step])]
    all_to_all x1, waiting for transfers between devices: 1.57 us -> 3.08 us  [on_device(): lax.all_to_all(sent, PLANE, 0, 0, tiled=True).reshape(8, 4, 4, 32, 128)]
  transfers between devices with their start and end apart: 8 -> 8, of which waited for: 6 -> 5; matrix products, arithmetic and copies ran while one was open for 0% -> 0% of each run, Pallas kernels for 4% -> 4%
where the time goes in v5:
time: 109 us
  starting transfers between devices  51.1 us (47%)
  waiting for transfers between devices  23.1 us (21%)
  blocking collectives  20.9 us (19%)
  Pallas kernels  12.9 us (12%)
    all_to_all x1, blocking collectives, on_device(): came = lax.all_to_all(shares.reshape(32, 128, 128), PLANE, 0, 0, tiled=True)  20.9 us
    all_to_all x1, starting transfers between devices, on_device(): came = lax.all_to_all(sent, 'z', 0, 0, tiled=True)  15.8 us
    pallas_call x8, Pallas kernels, call(): pl.pallas_call(kernel, out_shape=[jax.ShapeDtypeStruct(shape, dtype) for...  12.9 us
    all_to_all x1, waiting for transfers between devices, on_device(): lax.all_to_all(sent.reshape(32, 8, 128), ('z', 'xl'), 0, 0, tiled=True)  9.66 us
    ppermute x2, starting transfers between devices, pairwise(): lax.ppermute(second, axis, [p for step in steps[1::2] for p in step])  9.64 us
    all_to_all x1, starting transfers between devices, on_device(): lax.all_to_all(sent, PLANE, 0, 0, tiled=True).reshape(8, 4, 4, 32, 128)  9.27 us
    ppermute x2, starting transfers between devices, pairwise(): lax.ppermute(first, axis, [p for step in steps[0::2] for p in step])  6.29 us
    all_to_all x1, starting transfers between devices, on_device(): lax.all_to_all(sent.reshape(32, 8, 128), ('z', 'xl'), 0, 0, tiled=True)  6.2 us
  transfers between devices with their start and end apart: 8, of which 5 were waited for; matrix products, arithmetic and copies ran while one was open for 0% of the time, Pallas kernels for 4%

profile of v5, /device:TPU:1, one launch (start us, length us, event | category | flops | bytes accessed | tf_op | source)
XLA Modules:
  0.0 108.8 jit_solution(4596432763368786156)
XLA Ops:
  0.6 1.7 %shard_map.110 = (bf16[16,8,128]{2,1,0:T(8,128)(2,1)}, bf16[5,64,128]{2,1,0:T(8,128)(2,1)}, bf16[5,64,128]{2,1,0:T(8,128)(2,1)}) custom-call(bf16[9,2,128]{2,1,0:T(2,128)(2,1)} %first.1, bf16[9,128]{1,0:T(8,128)(2,1)} %bitcast.9, bf16[2,128]{1,0:T(2,128)(2,1)} %skip.1, bf16[4,32,256]{2,1,0:T(8,128)(2,1)} %coarse.5, bf16[8,64,128]{2,1,0:T(8,128)(2,1)} %cot.5), custom_call_target="tpu_custom_call" | custom-call | tf_op jit(solution)/shard_map/pallas_call | solution.py:380
  2.3 15.8 %all-to-all-start = ((bf16[16,8,128]{2,1,0:T(8,128)(2,1)}), bf16[16,8,128]{2,1,0:T(8,128)(2,1)S(1)}, u32[]{:S(2)}, u32[]{:S(2)}) async-start(bf16[16,8,128]{2,1,0:T(8,128)(2,1)} %get-tuple-element.27), calls=%async_computation | async-start | bytes 65536 | tf_op jit(solution)/shard_map/all_to_all | solution.py:410
  18.1 2.9 %collective-permute-start = (bf16[5,64,128]{2,1,0:T(8,128)(2,1)}, bf16[5,64,128]{2,1,0:T(8,128)(2,1)S(1)}, u32[]{:S(2)}, u32[]{:S(2)}) collective-permute-start(bf16[5,64,128]{2,1,0:T(8,128)(2,1)} %get-tuple-element.28), channel_id=1, source_target_pairs={{0,128},{128,0},{256,384},{384,256},{1,129},{129,1},{257,385},{385... | collective-permute-start | bytes 245768 | tf_op jit(solution)/shard_map/ppermute | solution.py:396
  20.9 3.0 %collective-permute-start.1 = (bf16[5,64,128]{2,1,0:T(8,128)(2,1)}, bf16[5,64,128]{2,1,0:T(8,128)(2,1)S(1)}, u32[]{:S(2)}, u32[]{:S(2)}) collective-permute-start(bf16[5,64,128]{2,1,0:T(8,128)(2,1)} %get-tuple-element.29), channel_id=1, source_target_pairs={{128,256},{256,128},{129,257},{257,129},{130,258},{258,130},{131,2... | collective-permute-start | bytes 245768 | tf_op jit(solution)/shard_map/ppermute | solution.py:397
  24.0 5.6 %all-to-all-done.came = bf16[16,8,128]{2,1,0:T(8,128)(2,1)S(1)} async-done(((bf16[16,8,128]{2,1,0:T(8,128)(2,1)}), bf16[16,8,128]{2,1,0:T(8,128)(2,1)S(1)}, u32[]{:S(2)}, u32[]{:S(2)}) %all-to-all-start) | async-done | bytes 32800 | tf_op jit(solution)/shard_map/all_to_all | solution.py:410
  29.5 1.2 %shard_map.111 = bf16[32,128,128]{2,1,0:T(8,128)(2,1)} custom-call(bf16[16,8,128]{2,1,0:T(8,128)(2,1)S(1)} %all-to-all-done.came), custom_call_target="tpu_custom_call" | custom-call | tf_op jit(solution)/shard_map/pallas_call | solution.py:380
  30.8 0.0 copy-start
  30.8 0.0 copy-start.1
  30.8 0.0 collective-permute-done.lat_a
  30.8 0.0 collective-permute-done.1.lat_b
  30.8 9.3 %all-to-all-start.1 = ((bf16[32,128,128]{2,1,0:T(8,128)(2,1)}), bf16[32,128,128]{2,1,0:T(8,128)(2,1)S(1)}, u32[]{:S(2)}, u32[]{:S(2)}) async-start(bf16[32,128,128]{2,1,0:T(8,128)(2,1)} %shard_map.111), calls=%async_computation.1 | async-start | bytes 2097152 | tf_op jit(solution)/shard_map/all_to_all | solution.py:414
  40.1 0.0 copy-done
  40.1 0.0 copy-done.1
  40.1 0.0 copy-start.2
  40.1 0.1 shard_map.112
  40.2 3.4 %collective-permute-start.2 = (bf16[8,16,128]{2,1,0:T(8,128)(2,1)S(1)}, bf16[8,16,128]{2,1,0:T(8,128)(2,1)S(1)}, u32[]{:S(2)}, u32[]{:S(2)}) collective-permute-start(bf16[8,16,128]{2,1,0:T(8,128)(2,1)S(1)} %get-tuple-element.33), channel_id=1, source_target_pairs={{0,1},{1,0},{2,3},{3,2},{4,5},{5,4},{6,7},{7,6},{8,9},{9,8},{10,11... | collective-permute-start | bytes 98312 | tf_op jit(solution)/shard_map/ppermute | solution.py:396
  43.6 6.6 %collective-permute-start.3 = (bf16[8,16,128]{2,1,0:T(8,128)(2,1)S(1)}, bf16[8,16,128]{2,1,0:T(8,128)(2,1)S(1)}, u32[]{:S(2)}, u32[]{:S(2)}) collective-permute-start(bf16[8,16,128]{2,1,0:T(8,128)(2,1)S(1)} %get-tuple-element.34), channel_id=1, source_target_pairs={{1,2},{2,1},{3,4},{4,3},{5,6},{6,5},{7,8},{8,7},{9,10},{10,9},{11,... | collective-permute-start | bytes 98312 | tf_op jit(solution)/shard_map/ppermute | solution.py:397
  50.2 0.0 collective-permute-done.2.lon_a
  50.2 4.0 %collective-permute-done.3.lon_b = bf16[8,16,128]{2,1,0:T(8,128)(2,1)S(1)} collective-permute-done((bf16[8,16,128]{2,1,0:T(8,128)(2,1)S(1)}, bf16[8,16,128]{2,1,0:T(8,128)(2,1)S(1)}, u32[]{:S(2)}, u32[]{:S(2)}) %collective-permute-start.3) | collective-permute-done | bytes 32800 | tf_op jit(solution)/shard_map/ppermute | solution.py:397
  54.3 3.1 %all-to-all-done.1 = bf16[32,128,128]{2,1,0:T(8,128)(2,1)S(1)} async-done(((bf16[32,128,128]{2,1,0:T(8,128)(2,1)}), bf16[32,128,128]{2,1,0:T(8,128)(2,1)S(1)}, u32[]{:S(2)}, u32[]{:S(2)}) %all-to-all-start.1) | async-done | bytes 1048608 | tf_op jit(solution)/shard_map/all_to_all | solution.py:414
  57.3 0.0 copy-done.2
  57.3 5.5 %shard_map.113 = (bf16[8,4,4,32,128]{4,3,2,1,0:T(8,128)(2,1)S(1)}, bf16[10,128,128]{2,1,0:T(8,128)(2,1)S(1)}, bf16[624,256]{1,0:T(8,128)(2,1)S(1)}, bf16[816,128...) custom-call(bf16[8,4,4,32,128]{4,3,2,1,0:T(8,128)(2,1)S(1)} %bitcast.5, ...), custom_call_target="tpu_custom_call" | custom-call | tf_op jit(solution)/shard_map/pallas_call | solution.py:380
  62.8 20.9 %all_to_all.20.came = bf16[32,128,128]{2,1,0:T(8,128)(2,1)S(1)} all-to-all(bf16[32,128,128]{2,1,0:T(8,128)(2,1)S(1)} %bitcast.7), channel_id=1, replica_groups=mesh['xl'=2,'core'=2,'z'=16,'xh'=2,'y'=4] {'xh','y','xl','core'}, dimensions={0} | all-to-all | bytes 2097152 | tf_op jit(solution)/shard_map/all_to_all | solution.py:437
  83.7 0.9 shard_map.114
  84.6 0.0 copy-start.3
  84.6 6.2 %all-to-all-start.3 = ((bf16[32,8,128]{2,1,0:T(8,128)(2,1)}), bf16[32,8,128]{2,1,0:T(8,128)(2,1)S(1)}, u32[]{:S(2)}, u32[]{:S(2)}) async-start(bf16[32,8,128]{2,1,0:T(8,128)(2,1)} %bitcast.3), calls=%async_computation.3 | async-start | bytes 131072 | tf_op jit(solution)/shard_map/all_to_all | solution.py:439
  90.8 0.0 copy-done.3
  90.8 2.9 %shard_map.115 = (bf16[8,64,128]{2,1,0:T(8,128)(2,1)}, bf16[4,32,256]{2,1,0:T(8,128)(2,1)}) custom-call(bf16[8,4,4,32,128]{4,3,2,1,0:T(8,128)(2,1)S(1)} %bitcast.6, bf16[10,128,128]{2,1,0:T(8,128)(2,1)S(1)} %get-tuple-element.36.second, bf16[624,256]{1,0:T(8,128)(2,1)S(1)} %get-tuple-element.37.fine, bf16[816,128]{1,0:T(8,128)(2,1)S(1)} %get-tuple-element.38.cot, ...), custom_call_target="tpu_custom_call" | custom-call | tf_op jit(solution)/shard_map/pallas_call | solution.py:380
  93.7 9.7 %all-to-all-done.3 = bf16[32,8,128]{2,1,0:T(8,128)(2,1)S(1)} async-done(((bf16[32,8,128]{2,1,0:T(8,128)(2,1)}), bf16[32,8,128]{2,1,0:T(8,128)(2,1)S(1)}, u32[]{:S(2)}, u32[]{:S(2)}) %all-to-all-start.3) | async-done | bytes 65568 | tf_op jit(solution)/shard_map/all_to_all | solution.py:439
  103.4 4.0 %collective-permute-start.4 = (f32[2,8,128]{2,1,0:T(8,128)S(1)}, f32[2,8,128]{2,1,0:T(8,128)S(1)}, u32[]{:S(2)}, u32[]{:S(2)}) collective-permute-start(f32[2,8,128]{2,1,0:T(8,128)S(1)} %shard_map.116.mine), channel_id=1, source_target_pairs={{0,128},{128,0},{1,129},{129,1},{2,130},{130,2},{3,131},{131,3},{4... | collective-permute-start | bytes 24584 | tf_op jit(solution)/shard_map/ppermute | solution.py:447
  107.3 0.8 collective-permute-done.4.other
  108.2 0.6 shard_map.117
  (1 shorter events, 0.0 us)
Async XLA Ops:
  2.3 27.2 %all-to-all-start = ((bf16[16,8,128]{2,1,0:T(8,128)(2,1)}), bf16[16,8,128]{2,1,0:T(8,128)(2,1)S(1)}, u32[]{:S(2)}, u32[]{:S(2)}) async-start(bf16[16,8,128]{2,1,0:T(8,128)(2,1)} %get-tuple-element.27), calls=%async_computation | async-start | bytes 65536 | tf_op jit(solution)/shard_map/all_to_all | solution.py:410
  18.1 12.7 %collective-permute-start = (bf16[5,64,128]{2,1,0:T(8,128)(2,1)}, bf16[5,64,128]{2,1,0:T(8,128)(2,1)S(1)}, u32[]{:S(2)}, u32[]{:S(2)}) collective-permute-start(bf16[5,64,128]{2,1,0:T(8,128)(2,1)} %get-tuple-element.28), channel_id=1, source_target_pairs={{0,128},{128,0},{256,384},{384,256},{1,129},{129,1},{257,385},{385... | collective-permute-start | bytes 245768 | tf_op jit(solution)/shard_map/ppermute | solution.py:396
  20.9 9.8 %collective-permute-start.1 = (bf16[5,64,128]{2,1,0:T(8,128)(2,1)}, bf16[5,64,128]{2,1,0:T(8,128)(2,1)S(1)}, u32[]{:S(2)}, u32[]{:S(2)}) collective-permute-start(bf16[5,64,128]{2,1,0:T(8,128)(2,1)} %get-tuple-element.29), channel_id=1, source_target_pairs={{128,256},{256,128},{129,257},{257,129},{130,258},{258,130},{131,2... | collective-permute-start | bytes 245768 | tf_op jit(solution)/shard_map/ppermute | solution.py:397
  30.8 9.3 %copy-start = (bf16[8,64,128]{2,1,0:T(8,128)(2,1)S(1)}, bf16[8,64,128]{2,1,0:T(8,128)(2,1)}, u32[]{:S(2)}) copy-start(bf16[8,64,128]{2,1,0:T(8,128)(2,1)} %cot.5) | copy-start | bytes 393220
  30.8 9.3 %copy-start.1 = (bf16[4,32,256]{2,1,0:T(8,128)(2,1)S(1)}, bf16[4,32,256]{2,1,0:T(8,128)(2,1)}, u32[]{:S(2)}) copy-start(bf16[4,32,256]{2,1,0:T(8,128)(2,1)} %coarse.5) | copy-start | bytes 196612
  30.8 26.6 %all-to-all-start.1 = ((bf16[32,128,128]{2,1,0:T(8,128)(2,1)}), bf16[32,128,128]{2,1,0:T(8,128)(2,1)S(1)}, u32[]{:S(2)}, u32[]{:S(2)}) async-start(bf16[32,128,128]{2,1,0:T(8,128)(2,1)} %shard_map.111), calls=%async_computation.1 | async-start | bytes 2097152 | tf_op jit(solution)/shard_map/all_to_all | solution.py:414
  40.1 17.3 %copy-start.2 = (bf16[2,240,144]{2,1,0:T(8,128)(2,1)S(1)}, bf16[2,240,144]{2,1,0:T(8,128)(2,1)}, u32[]{:S(2)}) copy-start(bf16[2,240,144]{2,1,0:T(8,128)(2,1)} %constant.4.clone.up) | copy-start | bytes 414724
  40.2 10.1 %collective-permute-start.2 = (bf16[8,16,128]{2,1,0:T(8,128)(2,1)S(1)}, bf16[8,16,128]{2,1,0:T(8,128)(2,1)S(1)}, u32[]{:S(2)}, u32[]{:S(2)}) collective-permute-start(bf16[8,16,128]{2,1,0:T(8,128)(2,1)S(1)} %get-tuple-element.33), channel_id=1, source_target_pairs={{0,1},{1,0},{2,3},{3,2},{4,5},{5,4},{6,7},{7,6},{8,9},{9,8},{10,11... | collective-permute-start | bytes 98312 | tf_op jit(solution)/shard_map/ppermute | solution.py:396
  43.6 10.7 %collective-permute-start.3 = (bf16[8,16,128]{2,1,0:T(8,128)(2,1)S(1)}, bf16[8,16,128]{2,1,0:T(8,128)(2,1)S(1)}, u32[]{:S(2)}, u32[]{:S(2)}) collective-permute-start(bf16[8,16,128]{2,1,0:T(8,128)(2,1)S(1)} %get-tuple-element.34), channel_id=1, source_target_pairs={{1,2},{2,1},{3,4},{4,3},{5,6},{6,5},{7,8},{8,7},{9,10},{10,9},{11,... | collective-permute-start | bytes 98312 | tf_op jit(solution)/shard_map/ppermute | solution.py:397
  84.6 6.2 %copy-start.3 = (bf16[32,336]{1,0:T(8,128)(2,1)S(1)}, bf16[32,336]{1,0:T(8,128)(2,1)}, u32[]{:S(2)}) copy-start(bf16[32,336]{1,0:T(8,128)(2,1)} %constant.5.clone.down) | copy-start | bytes 64516
  84.6 18.8 %all-to-all-start.3 = ((bf16[32,8,128]{2,1,0:T(8,128)(2,1)}), bf16[32,8,128]{2,1,0:T(8,128)(2,1)S(1)}, u32[]{:S(2)}, u32[]{:S(2)}) async-start(bf16[32,8,128]{2,1,0:T(8,128)(2,1)} %bitcast.3), calls=%async_computation.3 | async-start | bytes 131072 | tf_op jit(solution)/shard_map/all_to_all | solution.py:439
  103.4 4.8 %collective-permute-start.4 = (f32[2,8,128]{2,1,0:T(8,128)S(1)}, f32[2,8,128]{2,1,0:T(8,128)S(1)}, u32[]{:S(2)}, u32[]{:S(2)}) collective-permute-start(f32[2,8,128]{2,1,0:T(8,128)S(1)} %shard_map.116.mine), channel_id=1, source_target_pairs={{0,128},{128,0},{1,129},{129,1},{2,130},{130,2},{3,131},{131,3},{4... | collective-permute-start | bytes 24584 | tf_op jit(solution)/shard_map/ppermute | solution.py:447

commit v6 on v5

--- a/solution.py
+++ b/solution.py
@@ -311,20 +311,20 @@
         second[2 * k + 1] = block[128:]
     begin, end = WIDE
     count = end - begin
-    act = jnp.zeros((count, 128), F32)
-    for i in range(3):
-        kernels = jnp.concatenate([first_block(weights, 3 * i + j) for j in range(3)], axis=0)
-        at = begin + PITCH * (i - 1)
-        act = act + dot(fine3[at : at + count, :], kernels)
+    rows = [
+        jnp.concatenate([first_block(weights, 3 * i + j) for j in range(3)], axis=0) for i in range(3)
+    ]
+    both = dot(fine3[0 : count + PITCH, :], jnp.concatenate(rows[:2], axis=1))
+    act = both[:count, :128] + both[PITCH:, 128:]
+    act = act + dot(fine3[2 * PITCH : 2 * PITCH + count, :], rows[2])
     keep = inside(begin, (count, 128))
     sigma = jax.nn.sigmoid(act)
     hidden = jnp.where(keep, act * sigma, 0.0)
     hidden3[...] = shifted(hidden)[HIDDEN[0] - begin : HIDDEN[1] - begin]
-    grad_hidden = jnp.zeros((count, 128), F32)
-    for i in range(3):
-        kernels = jnp.concatenate([second[3 * i + 2 - j] for j in range(3)], axis=1)
-        at = begin - PITCH * (i - 1)
-        grad_hidden = grad_hidden + dot_nt(cot3[at : at + count, :], kernels)
+    rows = [jnp.concatenate([second[3 * i + 2 - j] for j in range(3)], axis=1) for i in range(3)]
+    both = dot_nt(cot3[0 : count + PITCH, :], jnp.concatenate(rows[1:], axis=0))
+    grad_hidden = both[PITCH:, :128] + both[:count, 128:]
+    grad_hidden = grad_hidden + dot_nt(cot3[2 * PITCH : 2 * PITCH + count, :], rows[0])
     grad = grad_hidden * sigma * (1.0 + act * (1.0 - sigma))
     grad_act[...] = jnp.where(keep, grad, 0.0).astype(BF16)
 

time: 109 us -> 108 us (level)
  Pallas kernels: 12.9 us -> 11.5 us
    pallas_call x8, Pallas kernels: 12.9 us -> 11.5 us  [call(): pl.pallas_call(kernel, out_shape=[jax.ShapeDtypeStruct(shape, dtype) for...]
where the time goes in v6:
time: 108 us; the launch traced here: 107 us
  starting transfers between devices  51.1 us (47%)
  waiting for transfers between devices  23.1 us (21%)
  blocking collectives  20.9 us (19%)
  Pallas kernels  11.5 us (11%)
    all_to_all x1, blocking collectives, on_device(): came = lax.all_to_all(shares.reshape(32, 128, 128), PLANE, 0, 0, tiled=True)  20.9 us
    all_to_all x1, starting transfers between devices, on_device(): came = lax.all_to_all(sent, 'z', 0, 0, tiled=True)  15.8 us
    pallas_call x8, Pallas kernels, call(): pl.pallas_call(kernel, out_shape=[jax.ShapeDtypeStruct(shape, dtype) for...  11.5 us
    all_to_all x1, waiting for transfers between devices, on_device(): lax.all_to_all(sent.reshape(32, 8, 128), ('z', 'xl'), 0, 0, tiled=True)  9.65 us
    ppermute x2, starting transfers between devices, pairwise(): lax.ppermute(second, axis, [p for step in steps[1::2] for p in step])  9.64 us
    all_to_all x1, starting transfers between devices, on_device(): lax.all_to_all(sent, PLANE, 0, 0, tiled=True).reshape(8, 4, 4, 32, 128)  9.27 us
    ppermute x2, starting transfers between devices, pairwise(): lax.ppermute(first, axis, [p for step in steps[0::2] for p in step])  6.29 us
    all_to_all x1, starting transfers between devices, on_device(): lax.all_to_all(sent.reshape(32, 8, 128), ('z', 'xl'), 0, 0, tiled=True)  6.2 us
  transfers between devices with their start and end apart: 8, of which 5 were waited for; matrix products, arithmetic and copies ran while one was open for 0% of the time, Pallas kernels for 4%

profile of v6, /device:TPU:1, one launch (start us, length us, event | category | flops | bytes accessed | tf_op | source)
XLA Modules:
  0.0 107.4 jit_solution(12431557285895473898)
XLA Ops:
  0.6 1.7 %shard_map.110 = (bf16[16,8,128]{2,1,0:T(8,128)(2,1)}, bf16[5,64,128]{2,1,0:T(8,128)(2,1)}, bf16[5,64,128]{2,1,0:T(8,128)(2,1)}) custom-call(bf16[9,2,128]{2,1,0:T(2,128)(2,1)} %first.1, bf16[9,128]{1,0:T(8,128)(2,1)} %bitcast.9, bf16[2,128]{1,0:T(2,128)(2,1)} %skip.1, bf16[4,32,256]{2,1,0:T(8,128)(2,1)} %coarse.5, bf16[8,64,128]{2,1,0:T(8,128)(2,1)} %cot.5), custom_call_target="tpu_custom_call" | custom-call | tf_op jit(solution)/shard_map/pallas_call | solution.py:380
  2.3 15.8 %all-to-all-start = ((bf16[16,8,128]{2,1,0:T(8,128)(2,1)}), bf16[16,8,128]{2,1,0:T(8,128)(2,1)S(1)}, u32[]{:S(2)}, u32[]{:S(2)}) async-start(bf16[16,8,128]{2,1,0:T(8,128)(2,1)} %get-tuple-element.27), calls=%async_computation | async-start | bytes 65536 | tf_op jit(solution)/shard_map/all_to_all | solution.py:410
  18.1 2.9 %collective-permute-start = (bf16[5,64,128]{2,1,0:T(8,128)(2,1)}, bf16[5,64,128]{2,1,0:T(8,128)(2,1)S(1)}, u32[]{:S(2)}, u32[]{:S(2)}) collective-permute-start(bf16[5,64,128]{2,1,0:T(8,128)(2,1)} %get-tuple-element.28), channel_id=1, source_target_pairs={{0,128},{128,0},{256,384},{384,256},{1,129},{129,1},{257,385},{385... | collective-permute-start | bytes 245768 | tf_op jit(solution)/shard_map/ppermute | solution.py:396
  20.9 3.0 %collective-permute-start.1 = (bf16[5,64,128]{2,1,0:T(8,128)(2,1)}, bf16[5,64,128]{2,1,0:T(8,128)(2,1)S(1)}, u32[]{:S(2)}, u32[]{:S(2)}) collective-permute-start(bf16[5,64,128]{2,1,0:T(8,128)(2,1)} %get-tuple-element.29), channel_id=1, source_target_pairs={{128,256},{256,128},{129,257},{257,129},{130,258},{258,130},{131,2... | collective-permute-start | bytes 245768 | tf_op jit(solution)/shard_map/ppermute | solution.py:397
  24.0 5.6 %all-to-all-done.came = bf16[16,8,128]{2,1,0:T(8,128)(2,1)S(1)} async-done(((bf16[16,8,128]{2,1,0:T(8,128)(2,1)}), bf16[16,8,128]{2,1,0:T(8,128)(2,1)S(1)}, u32[]{:S(2)}, u32[]{:S(2)}) %all-to-all-start) | async-done | bytes 32800 | tf_op jit(solution)/shard_map/all_to_all | solution.py:410
  29.5 1.2 %shard_map.111 = bf16[32,128,128]{2,1,0:T(8,128)(2,1)} custom-call(bf16[16,8,128]{2,1,0:T(8,128)(2,1)S(1)} %all-to-all-done.came), custom_call_target="tpu_custom_call" | custom-call | tf_op jit(solution)/shard_map/pallas_call | solution.py:380
  30.8 0.0 copy-start
  30.8 0.0 copy-start.1
  30.8 0.0 collective-permute-done.lat_a
  30.8 0.0 collective-permute-done.1.lat_b
  30.8 9.3 %all-to-all-start.1 = ((bf16[32,128,128]{2,1,0:T(8,128)(2,1)}), bf16[32,128,128]{2,1,0:T(8,128)(2,1)S(1)}, u32[]{:S(2)}, u32[]{:S(2)}) async-start(bf16[32,128,128]{2,1,0:T(8,128)(2,1)} %shard_map.111), calls=%async_computation.1 | async-start | bytes 2097152 | tf_op jit(solution)/shard_map/all_to_all | solution.py:414
  40.1 0.0 copy-done
  40.1 0.0 copy-done.1
  40.1 0.0 copy-start.2
  40.1 0.1 shard_map.112
  40.2 3.4 %collective-permute-start.2 = (bf16[8,16,128]{2,1,0:T(8,128)(2,1)S(1)}, bf16[8,16,128]{2,1,0:T(8,128)(2,1)S(1)}, u32[]{:S(2)}, u32[]{:S(2)}) collective-permute-start(bf16[8,16,128]{2,1,0:T(8,128)(2,1)S(1)} %get-tuple-element.33), channel_id=1, source_target_pairs={{0,1},{1,0},{2,3},{3,2},{4,5},{5,4},{6,7},{7,6},{8,9},{9,8},{10,11... | collective-permute-start | bytes 98312 | tf_op jit(solution)/shard_map/ppermute | solution.py:396
  43.6 6.6 %collective-permute-start.3 = (bf16[8,16,128]{2,1,0:T(8,128)(2,1)S(1)}, bf16[8,16,128]{2,1,0:T(8,128)(2,1)S(1)}, u32[]{:S(2)}, u32[]{:S(2)}) collective-permute-start(bf16[8,16,128]{2,1,0:T(8,128)(2,1)S(1)} %get-tuple-element.34), channel_id=1, source_target_pairs={{1,2},{2,1},{3,4},{4,3},{5,6},{6,5},{7,8},{8,7},{9,10},{10,9},{11,... | collective-permute-start | bytes 98312 | tf_op jit(solution)/shard_map/ppermute | solution.py:397
  50.2 0.0 collective-permute-done.2.lon_a
  50.2 4.0 %collective-permute-done.3.lon_b = bf16[8,16,128]{2,1,0:T(8,128)(2,1)S(1)} collective-permute-done((bf16[8,16,128]{2,1,0:T(8,128)(2,1)S(1)}, bf16[8,16,128]{2,1,0:T(8,128)(2,1)S(1)}, u32[]{:S(2)}, u32[]{:S(2)}) %collective-permute-start.3) | collective-permute-done | bytes 32800 | tf_op jit(solution)/shard_map/ppermute | solution.py:397
  54.3 3.1 %all-to-all-done.1 = bf16[32,128,128]{2,1,0:T(8,128)(2,1)S(1)} async-done(((bf16[32,128,128]{2,1,0:T(8,128)(2,1)}), bf16[32,128,128]{2,1,0:T(8,128)(2,1)S(1)}, u32[]{:S(2)}, u32[]{:S(2)}) %all-to-all-start.1) | async-done | bytes 1048608 | tf_op jit(solution)/shard_map/all_to_all | solution.py:414
  57.3 0.0 copy-done.2
  57.3 4.1 %shard_map.113 = (bf16[8,4,4,32,128]{4,3,2,1,0:T(8,128)(2,1)S(1)}, bf16[10,128,128]{2,1,0:T(8,128)(2,1)S(1)}, bf16[624,256]{1,0:T(8,128)(2,1)S(1)}, bf16[816,128...) custom-call(bf16[8,4,4,32,128]{4,3,2,1,0:T(8,128)(2,1)S(1)} %bitcast.5, ...), custom_call_target="tpu_custom_call" | custom-call | tf_op jit(solution)/shard_map/pallas_call | solution.py:380
  61.5 20.9 %all_to_all.20.came = bf16[32,128,128]{2,1,0:T(8,128)(2,1)S(1)} all-to-all(bf16[32,128,128]{2,1,0:T(8,128)(2,1)S(1)} %bitcast.7), channel_id=1, replica_groups=mesh['xl'=2,'core'=2,'z'=16,'xh'=2,'y'=4] {'xh','y','xl','core'}, dimensions={0} | all-to-all | bytes 2097152 | tf_op jit(solution)/shard_map/all_to_all | solution.py:437
  82.3 0.9 shard_map.114
  83.2 0.0 copy-start.3
  83.2 6.2 %all-to-all-start.3 = ((bf16[32,8,128]{2,1,0:T(8,128)(2,1)}), bf16[32,8,128]{2,1,0:T(8,128)(2,1)S(1)}, u32[]{:S(2)}, u32[]{:S(2)}) async-start(bf16[32,8,128]{2,1,0:T(8,128)(2,1)} %bitcast.3), calls=%async_computation.3 | async-start | bytes 131072 | tf_op jit(solution)/shard_map/all_to_all | solution.py:439
  89.4 0.0 copy-done.3
  89.4 2.9 %shard_map.115 = (bf16[8,64,128]{2,1,0:T(8,128)(2,1)}, bf16[4,32,256]{2,1,0:T(8,128)(2,1)}) custom-call(bf16[8,4,4,32,128]{4,3,2,1,0:T(8,128)(2,1)S(1)} %bitcast.6, bf16[10,128,128]{2,1,0:T(8,128)(2,1)S(1)} %get-tuple-element.36.second, bf16[624,256]{1,0:T(8,128)(2,1)S(1)} %get-tuple-element.37.fine, bf16[816,128]{1,0:T(8,128)(2,1)S(1)} %get-tuple-element.38.cot, ...), custom_call_target="tpu_custom_call" | custom-call | tf_op jit(solution)/shard_map/pallas_call | solution.py:380
  92.3 9.7 %all-to-all-done.3 = bf16[32,8,128]{2,1,0:T(8,128)(2,1)S(1)} async-done(((bf16[32,8,128]{2,1,0:T(8,128)(2,1)}), bf16[32,8,128]{2,1,0:T(8,128)(2,1)S(1)}, u32[]{:S(2)}, u32[]{:S(2)}) %all-to-all-start.3) | async-done | bytes 65568 | tf_op jit(solution)/shard_map/all_to_all | solution.py:439
  102.0 4.0 %collective-permute-start.4 = (f32[2,8,128]{2,1,0:T(8,128)S(1)}, f32[2,8,128]{2,1,0:T(8,128)S(1)}, u32[]{:S(2)}, u32[]{:S(2)}) collective-permute-start(f32[2,8,128]{2,1,0:T(8,128)S(1)} %shard_map.116.mine), channel_id=1, source_target_pairs={{0,128},{128,0},{1,129},{129,1},{2,130},{130,2},{3,131},{131,3},{4... | collective-permute-start | bytes 24584 | tf_op jit(solution)/shard_map/ppermute | solution.py:447
  106.0 0.8 collective-permute-done.4.other
  106.8 0.6 shard_map.117
  (1 shorter events, 0.0 us)
Async XLA Ops:
  2.3 27.2 %all-to-all-start = ((bf16[16,8,128]{2,1,0:T(8,128)(2,1)}), bf16[16,8,128]{2,1,0:T(8,128)(2,1)S(1)}, u32[]{:S(2)}, u32[]{:S(2)}) async-start(bf16[16,8,128]{2,1,0:T(8,128)(2,1)} %get-tuple-element.27), calls=%async_computation | async-start | bytes 65536 | tf_op jit(solution)/shard_map/all_to_all | solution.py:410
  18.1 12.7 %collective-permute-start = (bf16[5,64,128]{2,1,0:T(8,128)(2,1)}, bf16[5,64,128]{2,1,0:T(8,128)(2,1)S(1)}, u32[]{:S(2)}, u32[]{:S(2)}) collective-permute-start(bf16[5,64,128]{2,1,0:T(8,128)(2,1)} %get-tuple-element.28), channel_id=1, source_target_pairs={{0,128},{128,0},{256,384},{384,256},{1,129},{129,1},{257,385},{385... | collective-permute-start | bytes 245768 | tf_op jit(solution)/shard_map/ppermute | solution.py:396
  20.9 9.8 %collective-permute-start.1 = (bf16[5,64,128]{2,1,0:T(8,128)(2,1)}, bf16[5,64,128]{2,1,0:T(8,128)(2,1)S(1)}, u32[]{:S(2)}, u32[]{:S(2)}) collective-permute-start(bf16[5,64,128]{2,1,0:T(8,128)(2,1)} %get-tuple-element.29), channel_id=1, source_target_pairs={{128,256},{256,128},{129,257},{257,129},{130,258},{258,130},{131,2... | collective-permute-start | bytes 245768 | tf_op jit(solution)/shard_map/ppermute | solution.py:397
  30.8 9.3 %copy-start = (bf16[8,64,128]{2,1,0:T(8,128)(2,1)S(1)}, bf16[8,64,128]{2,1,0:T(8,128)(2,1)}, u32[]{:S(2)}) copy-start(bf16[8,64,128]{2,1,0:T(8,128)(2,1)} %cot.5) | copy-start | bytes 393220
  30.8 9.3 %copy-start.1 = (bf16[4,32,256]{2,1,0:T(8,128)(2,1)S(1)}, bf16[4,32,256]{2,1,0:T(8,128)(2,1)}, u32[]{:S(2)}) copy-start(bf16[4,32,256]{2,1,0:T(8,128)(2,1)} %coarse.5) | copy-start | bytes 196612
  30.8 26.6 %all-to-all-start.1 = ((bf16[32,128,128]{2,1,0:T(8,128)(2,1)}), bf16[32,128,128]{2,1,0:T(8,128)(2,1)S(1)}, u32[]{:S(2)}, u32[]{:S(2)}) async-start(bf16[32,128,128]{2,1,0:T(8,128)(2,1)} %shard_map.111), calls=%async_computation.1 | async-start | bytes 2097152 | tf_op jit(solution)/shard_map/all_to_all | solution.py:414
  40.1 17.3 %copy-start.2 = (bf16[2,240,144]{2,1,0:T(8,128)(2,1)S(1)}, bf16[2,240,144]{2,1,0:T(8,128)(2,1)}, u32[]{:S(2)}) copy-start(bf16[2,240,144]{2,1,0:T(8,128)(2,1)} %constant.4.clone.up) | copy-start | bytes 414724
  40.2 10.1 %collective-permute-start.2 = (bf16[8,16,128]{2,1,0:T(8,128)(2,1)S(1)}, bf16[8,16,128]{2,1,0:T(8,128)(2,1)S(1)}, u32[]{:S(2)}, u32[]{:S(2)}) collective-permute-start(bf16[8,16,128]{2,1,0:T(8,128)(2,1)S(1)} %get-tuple-element.33), channel_id=1, source_target_pairs={{0,1},{1,0},{2,3},{3,2},{4,5},{5,4},{6,7},{7,6},{8,9},{9,8},{10,11... | collective-permute-start | bytes 98312 | tf_op jit(solution)/shard_map/ppermute | solution.py:396
  43.6 10.7 %collective-permute-start.3 = (bf16[8,16,128]{2,1,0:T(8,128)(2,1)S(1)}, bf16[8,16,128]{2,1,0:T(8,128)(2,1)S(1)}, u32[]{:S(2)}, u32[]{:S(2)}) collective-permute-start(bf16[8,16,128]{2,1,0:T(8,128)(2,1)S(1)} %get-tuple-element.34), channel_id=1, source_target_pairs={{1,2},{2,1},{3,4},{4,3},{5,6},{6,5},{7,8},{8,7},{9,10},{10,9},{11,... | collective-permute-start | bytes 98312 | tf_op jit(solution)/shard_map/ppermute | solution.py:397
  83.2 6.2 %copy-start.3 = (bf16[32,336]{1,0:T(8,128)(2,1)S(1)}, bf16[32,336]{1,0:T(8,128)(2,1)}, u32[]{:S(2)}) copy-start(bf16[32,336]{1,0:T(8,128)(2,1)} %constant.5.clone.down) | copy-start | bytes 64516
  83.2 18.8 %all-to-all-start.3 = ((bf16[32,8,128]{2,1,0:T(8,128)(2,1)}), bf16[32,8,128]{2,1,0:T(8,128)(2,1)S(1)}, u32[]{:S(2)}, u32[]{:S(2)}) async-start(bf16[32,8,128]{2,1,0:T(8,128)(2,1)} %bitcast.3), calls=%async_computation.3 | async-start | bytes 131072 | tf_op jit(solution)/shard_map/all_to_all | solution.py:439
  102.0 4.8 %collective-permute-start.4 = (f32[2,8,128]{2,1,0:T(8,128)S(1)}, f32[2,8,128]{2,1,0:T(8,128)S(1)}, u32[]{:S(2)}, u32[]{:S(2)}) collective-permute-start(f32[2,8,128]{2,1,0:T(8,128)S(1)} %shard_map.116.mine), channel_id=1, source_target_pairs={{0,128},{128,0},{1,129},{129,1},{2,130},{130,2},{3,131},{131,3},{4... | collective-permute-start | bytes 24584 | tf_op jit(solution)/shard_map/ppermute | solution.py:447

commit v7 on v6

--- a/solution.py
+++ b/solution.py
@@ -209,10 +209,10 @@
     return ref[k, 32 * h : 32 * h + 32]
 
 
-def spread_kernel(came, sent):
+def spread_kernel(came, sent, block, semaphores):
     order = permutation(128, block_row, False)
-    block = dot(order, came[...].reshape(128, 128)).astype(BF16)
-    sent[...] = jnp.broadcast_to(block[None], (32, 128, 128))
+    block[...] = dot(order, came[...].reshape(128, 128)).astype(BF16)
+    finish(copied([(block, sent.at[k]) for k in range(32)], semaphores))
 
 
 def prepare(coarse, cot, low, high, left, right, up, fine3, cot3, grid, field):
@@ -409,7 +409,9 @@
     )
     came = lax.all_to_all(sent, "z", 0, 0, tiled=True)
     lat_a, lat_b = pairwise(*edges, LAT, False)
-    (sent,) = call(spread_kernel, [(32, 128, 128)], came, spaces="vv")
+    (sent,) = call(
+        spread_kernel, [(32, 128, 128)], came, spaces="vh", scratch=[((128, 128), BF16)], semaphores=32
+    )
     sent, lat_a, lat_b = lax.optimization_barrier((sent, lat_a, lat_b))
     weights = lax.all_to_all(sent, PLANE, 0, 0, tiled=True).reshape(8, 4, 4, 32, 128)
     edges = call(

time: 108 us -> 108 us (level)
  no operation moved by 1% of the time
where the time goes in v7:
time: 108 us; the launch traced here: 107 us
  starting transfers between devices  50.9 us (47%)
  waiting for transfers between devices  23.1 us (21%)
  blocking collectives  20.9 us (19%)
  Pallas kernels  11.7 us (11%)
    all_to_all x1, blocking collectives, on_device(): came = lax.all_to_all(shares.reshape(32, 128, 128), PLANE, 0, 0, tiled=True)  20.9 us
    all_to_all x1, starting transfers between devices, on_device(): came = lax.all_to_all(sent, 'z', 0, 0, tiled=True)  15.8 us
    pallas_call x8, Pallas kernels, call(): pl.pallas_call(kernel, out_shape=[jax.ShapeDtypeStruct(shape, dtype) for...  11.7 us
    all_to_all x1, waiting for transfers between devices, on_device(): lax.all_to_all(sent.reshape(32, 8, 128), ('z', 'xl'), 0, 0, tiled=True)  9.65 us
    ppermute x2, starting transfers between devices, pairwise(): lax.ppermute(second, axis, [p for step in steps[1::2] for p in step])  9.64 us
    all_to_all x1, starting transfers between devices, on_device(): lax.all_to_all(sent, PLANE, 0, 0, tiled=True).reshape(8, 4, 4, 32, 128)  9.27 us
    ppermute x2, starting transfers between devices, pairwise(): lax.ppermute(first, axis, [p for step in steps[0::2] for p in step])  6.29 us
    all_to_all x1, starting transfers between devices, on_device(): lax.all_to_all(sent.reshape(32, 8, 128), ('z', 'xl'), 0, 0, tiled=True)  5.99 us
  transfers between devices with their start and end apart: 8, of which 5 were waited for; matrix products, arithmetic and copies ran while one was open for 0% of the time, Pallas kernels for 4%

profile of v7, /device:TPU:1, one launch (start us, length us, event | category | flops | bytes accessed | tf_op | source)
XLA Modules:
  0.0 107.4 jit_solution(9383229269360175854)
XLA Ops:
  0.6 1.7 %shard_map.110 = (bf16[16,8,128]{2,1,0:T(8,128)(2,1)}, bf16[5,64,128]{2,1,0:T(8,128)(2,1)}, bf16[5,64,128]{2,1,0:T(8,128)(2,1)}) custom-call(bf16[9,2,128]{2,1,0:T(2,128)(2,1)} %first.1, bf16[9,128]{1,0:T(8,128)(2,1)} %bitcast.9, bf16[2,128]{1,0:T(2,128)(2,1)} %skip.1, bf16[4,32,256]{2,1,0:T(8,128)(2,1)} %coarse.5, bf16[8,64,128]{2,1,0:T(8,128)(2,1)} %cot.5), custom_call_target="tpu_custom_call" | custom-call | tf_op jit(solution)/shard_map/pallas_call | solution.py:380
  2.3 15.8 %all-to-all-start = ((bf16[16,8,128]{2,1,0:T(8,128)(2,1)}), bf16[16,8,128]{2,1,0:T(8,128)(2,1)S(1)}, u32[]{:S(2)}, u32[]{:S(2)}) async-start(bf16[16,8,128]{2,1,0:T(8,128)(2,1)} %get-tuple-element.27), calls=%async_computation | async-start | bytes 65536 | tf_op jit(solution)/shard_map/all_to_all | solution.py:410
  18.1 2.9 %collective-permute-start = (bf16[5,64,128]{2,1,0:T(8,128)(2,1)}, bf16[5,64,128]{2,1,0:T(8,128)(2,1)S(1)}, u32[]{:S(2)}, u32[]{:S(2)}) collective-permute-start(bf16[5,64,128]{2,1,0:T(8,128)(2,1)} %get-tuple-element.28), channel_id=1, source_target_pairs={{0,128},{128,0},{256,384},{384,256},{1,129},{129,1},{257,385},{385... | collective-permute-start | bytes 245768 | tf_op jit(solution)/shard_map/ppermute | solution.py:396
  20.9 3.0 %collective-permute-start.1 = (bf16[5,64,128]{2,1,0:T(8,128)(2,1)}, bf16[5,64,128]{2,1,0:T(8,128)(2,1)S(1)}, u32[]{:S(2)}, u32[]{:S(2)}) collective-permute-start(bf16[5,64,128]{2,1,0:T(8,128)(2,1)} %get-tuple-element.29), channel_id=1, source_target_pairs={{128,256},{256,128},{129,257},{257,129},{130,258},{258,130},{131,2... | collective-permute-start | bytes 245768 | tf_op jit(solution)/shard_map/ppermute | solution.py:397
  24.0 5.6 %all-to-all-done.came = bf16[16,8,128]{2,1,0:T(8,128)(2,1)S(1)} async-done(((bf16[16,8,128]{2,1,0:T(8,128)(2,1)}), bf16[16,8,128]{2,1,0:T(8,128)(2,1)S(1)}, u32[]{:S(2)}, u32[]{:S(2)}) %all-to-all-start) | async-done | bytes 32800 | tf_op jit(solution)/shard_map/all_to_all | solution.py:410
  29.5 1.4 %shard_map.111 = bf16[32,128,128]{2,1,0:T(8,128)(2,1)} custom-call(bf16[16,8,128]{2,1,0:T(8,128)(2,1)S(1)} %all-to-all-done.came), custom_call_target="tpu_custom_call" | custom-call | tf_op jit(solution)/shard_map/pallas_call | solution.py:380
  31.0 0.0 copy-start
  31.0 0.0 copy-start.1
  31.0 0.0 collective-permute-done.lat_a
  31.0 0.0 collective-permute-done.1.lat_b
  31.0 9.3 %all-to-all-start.1 = ((bf16[32,128,128]{2,1,0:T(8,128)(2,1)}), bf16[32,128,128]{2,1,0:T(8,128)(2,1)S(1)}, u32[]{:S(2)}, u32[]{:S(2)}) async-start(bf16[32,128,128]{2,1,0:T(8,128)(2,1)} %shard_map.111), calls=%async_computation.1 | async-start | bytes 2097152 | tf_op jit(solution)/shard_map/all_to_all | solution.py:416
  40.3 0.0 copy-done
  40.3 0.0 copy-done.1
  40.3 0.0 copy-start.2
  40.3 0.1 shard_map.112
  40.4 3.4 %collective-permute-start.2 = (bf16[8,16,128]{2,1,0:T(8,128)(2,1)S(1)}, bf16[8,16,128]{2,1,0:T(8,128)(2,1)S(1)}, u32[]{:S(2)}, u32[]{:S(2)}) collective-permute-start(bf16[8,16,128]{2,1,0:T(8,128)(2,1)S(1)} %get-tuple-element.33), channel_id=1, source_target_pairs={{0,1},{1,0},{2,3},{3,2},{4,5},{5,4},{6,7},{7,6},{8,9},{9,8},{10,11... | collective-permute-start | bytes 98312 | tf_op jit(solution)/shard_map/ppermute | solution.py:396
  43.8 6.6 %collective-permute-start.3 = (bf16[8,16,128]{2,1,0:T(8,128)(2,1)S(1)}, bf16[8,16,128]{2,1,0:T(8,128)(2,1)S(1)}, u32[]{:S(2)}, u32[]{:S(2)}) collective-permute-start(bf16[8,16,128]{2,1,0:T(8,128)(2,1)S(1)} %get-tuple-element.34), channel_id=1, source_target_pairs={{1,2},{2,1},{3,4},{4,3},{5,6},{6,5},{7,8},{8,7},{9,10},{10,9},{11,... | collective-permute-start | bytes 98312 | tf_op jit(solution)/shard_map/ppermute | solution.py:397
  50.4 0.0 collective-permute-done.2.lon_a
  50.5 4.0 %collective-permute-done.3.lon_b = bf16[8,16,128]{2,1,0:T(8,128)(2,1)S(1)} collective-permute-done((bf16[8,16,128]{2,1,0:T(8,128)(2,1)S(1)}, bf16[8,16,128]{2,1,0:T(8,128)(2,1)S(1)}, u32[]{:S(2)}, u32[]{:S(2)}) %collective-permute-start.3) | collective-permute-done | bytes 32800 | tf_op jit(solution)/shard_map/ppermute | solution.py:397
  54.5 3.1 %all-to-all-done.1 = bf16[32,128,128]{2,1,0:T(8,128)(2,1)S(1)} async-done(((bf16[32,128,128]{2,1,0:T(8,128)(2,1)}), bf16[32,128,128]{2,1,0:T(8,128)(2,1)S(1)}, u32[]{:S(2)}, u32[]{:S(2)}) %all-to-all-start.1) | async-done | bytes 1048608 | tf_op jit(solution)/shard_map/all_to_all | solution.py:416
  57.5 0.0 copy-done.2
  57.6 4.1 %shard_map.113 = (bf16[8,4,4,32,128]{4,3,2,1,0:T(8,128)(2,1)S(1)}, bf16[10,128,128]{2,1,0:T(8,128)(2,1)S(1)}, bf16[624,256]{1,0:T(8,128)(2,1)S(1)}, bf16[816,128...) custom-call(bf16[8,4,4,32,128]{4,3,2,1,0:T(8,128)(2,1)S(1)} %bitcast.5, ...), custom_call_target="tpu_custom_call" | custom-call | tf_op jit(solution)/shard_map/pallas_call | solution.py:380
  61.7 20.9 %all_to_all.20.came = bf16[32,128,128]{2,1,0:T(8,128)(2,1)S(1)} all-to-all(bf16[32,128,128]{2,1,0:T(8,128)(2,1)S(1)} %bitcast.7), channel_id=1, replica_groups=mesh['xl'=2,'core'=2,'z'=16,'xh'=2,'y'=4] {'xh','y','xl','core'}, dimensions={0} | all-to-all | bytes 2097152 | tf_op jit(solution)/shard_map/all_to_all | solution.py:439
  82.5 0.9 shard_map.114
  83.4 0.0 copy-start.3
  83.4 6.0 %all-to-all-start.3 = ((bf16[32,8,128]{2,1,0:T(8,128)(2,1)}), bf16[32,8,128]{2,1,0:T(8,128)(2,1)S(1)}, u32[]{:S(2)}, u32[]{:S(2)}) async-start(bf16[32,8,128]{2,1,0:T(8,128)(2,1)} %bitcast.3), calls=%async_computation.3 | async-start | bytes 131072 | tf_op jit(solution)/shard_map/all_to_all | solution.py:441
  89.4 0.0 copy-done.3
  89.4 2.9 %shard_map.115 = (bf16[8,64,128]{2,1,0:T(8,128)(2,1)}, bf16[4,32,256]{2,1,0:T(8,128)(2,1)}) custom-call(bf16[8,4,4,32,128]{4,3,2,1,0:T(8,128)(2,1)S(1)} %bitcast.6, bf16[10,128,128]{2,1,0:T(8,128)(2,1)S(1)} %get-tuple-element.36.second, bf16[624,256]{1,0:T(8,128)(2,1)S(1)} %get-tuple-element.37.fine, bf16[816,128]{1,0:T(8,128)(2,1)S(1)} %get-tuple-element.38.cot, ...), custom_call_target="tpu_custom_call" | custom-call | tf_op jit(solution)/shard_map/pallas_call | solution.py:380
  92.3 9.7 %all-to-all-done.3 = bf16[32,8,128]{2,1,0:T(8,128)(2,1)S(1)} async-done(((bf16[32,8,128]{2,1,0:T(8,128)(2,1)}), bf16[32,8,128]{2,1,0:T(8,128)(2,1)S(1)}, u32[]{:S(2)}, u32[]{:S(2)}) %all-to-all-start.3) | async-done | bytes 65568 | tf_op jit(solution)/shard_map/all_to_all | solution.py:441
  102.0 4.0 %collective-permute-start.4 = (f32[2,8,128]{2,1,0:T(8,128)S(1)}, f32[2,8,128]{2,1,0:T(8,128)S(1)}, u32[]{:S(2)}, u32[]{:S(2)}) collective-permute-start(f32[2,8,128]{2,1,0:T(8,128)S(1)} %shard_map.116.mine), channel_id=1, source_target_pairs={{0,128},{128,0},{1,129},{129,1},{2,130},{130,2},{3,131},{131,3},{4... | collective-permute-start | bytes 24584 | tf_op jit(solution)/shard_map/ppermute | solution.py:449
  106.0 0.8 collective-permute-done.4.other
  106.8 0.6 shard_map.117
  (1 shorter events, 0.0 us)
Async XLA Ops:
  2.3 27.2 %all-to-all-start = ((bf16[16,8,128]{2,1,0:T(8,128)(2,1)}), bf16[16,8,128]{2,1,0:T(8,128)(2,1)S(1)}, u32[]{:S(2)}, u32[]{:S(2)}) async-start(bf16[16,8,128]{2,1,0:T(8,128)(2,1)} %get-tuple-element.27), calls=%async_computation | async-start | bytes 65536 | tf_op jit(solution)/shard_map/all_to_all | solution.py:410
  18.1 12.9 %collective-permute-start = (bf16[5,64,128]{2,1,0:T(8,128)(2,1)}, bf16[5,64,128]{2,1,0:T(8,128)(2,1)S(1)}, u32[]{:S(2)}, u32[]{:S(2)}) collective-permute-start(bf16[5,64,128]{2,1,0:T(8,128)(2,1)} %get-tuple-element.28), channel_id=1, source_target_pairs={{0,128},{128,0},{256,384},{384,256},{1,129},{129,1},{257,385},{385... | collective-permute-start | bytes 245768 | tf_op jit(solution)/shard_map/ppermute | solution.py:396
  20.9 10.1 %collective-permute-start.1 = (bf16[5,64,128]{2,1,0:T(8,128)(2,1)}, bf16[5,64,128]{2,1,0:T(8,128)(2,1)S(1)}, u32[]{:S(2)}, u32[]{:S(2)}) collective-permute-start(bf16[5,64,128]{2,1,0:T(8,128)(2,1)} %get-tuple-element.29), channel_id=1, source_target_pairs={{128,256},{256,128},{129,257},{257,129},{130,258},{258,130},{131,2... | collective-permute-start | bytes 245768 | tf_op jit(solution)/shard_map/ppermute | solution.py:397
  31.0 9.3 %copy-start = (bf16[8,64,128]{2,1,0:T(8,128)(2,1)S(1)}, bf16[8,64,128]{2,1,0:T(8,128)(2,1)}, u32[]{:S(2)}) copy-start(bf16[8,64,128]{2,1,0:T(8,128)(2,1)} %cot.5) | copy-start | bytes 393220
  31.0 9.3 %copy-start.1 = (bf16[4,32,256]{2,1,0:T(8,128)(2,1)S(1)}, bf16[4,32,256]{2,1,0:T(8,128)(2,1)}, u32[]{:S(2)}) copy-start(bf16[4,32,256]{2,1,0:T(8,128)(2,1)} %coarse.5) | copy-start | bytes 196612
  31.0 26.6 %all-to-all-start.1 = ((bf16[32,128,128]{2,1,0:T(8,128)(2,1)}), bf16[32,128,128]{2,1,0:T(8,128)(2,1)S(1)}, u32[]{:S(2)}, u32[]{:S(2)}) async-start(bf16[32,128,128]{2,1,0:T(8,128)(2,1)} %shard_map.111), calls=%async_computation.1 | async-start | bytes 2097152 | tf_op jit(solution)/shard_map/all_to_all | solution.py:416
  40.3 17.3 %copy-start.2 = (bf16[2,240,144]{2,1,0:T(8,128)(2,1)S(1)}, bf16[2,240,144]{2,1,0:T(8,128)(2,1)}, u32[]{:S(2)}) copy-start(bf16[2,240,144]{2,1,0:T(8,128)(2,1)} %constant.4.clone.up) | copy-start | bytes 414724
  40.4 10.1 %collective-permute-start.2 = (bf16[8,16,128]{2,1,0:T(8,128)(2,1)S(1)}, bf16[8,16,128]{2,1,0:T(8,128)(2,1)S(1)}, u32[]{:S(2)}, u32[]{:S(2)}) collective-permute-start(bf16[8,16,128]{2,1,0:T(8,128)(2,1)S(1)} %get-tuple-element.33), channel_id=1, source_target_pairs={{0,1},{1,0},{2,3},{3,2},{4,5},{5,4},{6,7},{7,6},{8,9},{9,8},{10,11... | collective-permute-start | bytes 98312 | tf_op jit(solution)/shard_map/ppermute | solution.py:396
  43.8 10.7 %collective-permute-start.3 = (bf16[8,16,128]{2,1,0:T(8,128)(2,1)S(1)}, bf16[8,16,128]{2,1,0:T(8,128)(2,1)S(1)}, u32[]{:S(2)}, u32[]{:S(2)}) collective-permute-start(bf16[8,16,128]{2,1,0:T(8,128)(2,1)S(1)} %get-tuple-element.34), channel_id=1, source_target_pairs={{1,2},{2,1},{3,4},{4,3},{5,6},{6,5},{7,8},{8,7},{9,10},{10,9},{11,... | collective-permute-start | bytes 98312 | tf_op jit(solution)/shard_map/ppermute | solution.py:397
  83.4 6.0 %copy-start.3 = (bf16[32,336]{1,0:T(8,128)(2,1)S(1)}, bf16[32,336]{1,0:T(8,128)(2,1)}, u32[]{:S(2)}) copy-start(bf16[32,336]{1,0:T(8,128)(2,1)} %constant.5.clone.down) | copy-start | bytes 64516
  83.4 18.6 %all-to-all-start.3 = ((bf16[32,8,128]{2,1,0:T(8,128)(2,1)}), bf16[32,8,128]{2,1,0:T(8,128)(2,1)S(1)}, u32[]{:S(2)}, u32[]{:S(2)}) async-start(bf16[32,8,128]{2,1,0:T(8,128)(2,1)} %bitcast.3), calls=%async_computation.3 | async-start | bytes 131072 | tf_op jit(solution)/shard_map/all_to_all | solution.py:441
  102.0 4.8 %collective-permute-start.4 = (f32[2,8,128]{2,1,0:T(8,128)S(1)}, f32[2,8,128]{2,1,0:T(8,128)S(1)}, u32[]{:S(2)}, u32[]{:S(2)}) collective-permute-start(f32[2,8,128]{2,1,0:T(8,128)S(1)} %shard_map.116.mine), channel_id=1, source_target_pairs={{0,128},{128,0},{1,129},{129,1},{2,130},{130,2},{3,131},{131,3},{4... | collective-permute-start | bytes 24584 | tf_op jit(solution)/shard_map/ppermute | solution.py:449
